TPU v7x, 32 devices: a whole 2x2x4 slice. The times are simulated.
32 devices in a mesh: sx: 4 (over y, x), sy: 8 (over z, core).
Axes of the slice: x: 2, y: 2, z: 4, core: 2. Of those that a mesh axis runs over, the one named last changes fastest.
Arguments:
- text_tokens: bfloat16 [8, 32, 4096], P('sy', 'sx'), may hold values from -2.5 to 2.5
- latent: bfloat16 [8, 16, 512], P('sy', 'sx'), may hold values from -6 to 6
- image_offset: int32 [8], P('sy'), may hold values from 0 to 32
- norm_gain: bfloat16 [4096], replicated, may hold values from 0.099609375 to 1.8984375
- w_query: bfloat16 [4096, 4096], P(None, 'sx')
- w_key: bfloat16 [4096, 4096], P(None, 'sx')
- w_value: bfloat16 [4096, 4096], P(None, 'sx'), may hold values from -0.09375 to 0.09375
- w_out: bfloat16 [4096, 4096], P('sx'), may hold values from -0.09375 to 0.09375
- w_down_conv: bfloat16 [288, 128], replicated, may hold values from -0.375 to 0.375
- w_down_proj: bfloat16 [128, 4096], replicated, may hold values from -0.5 to 0.5
- w_up_proj: bfloat16 [4096, 128], replicated, may hold values from -0.09375 to 0.09375
- w_up_out: bfloat16 [128, 32], replicated, may hold values from -0.5 to 0.5
- pred_grad: bfloat16 [8, 16, 512], P('sy', 'sx'), may hold values from -0.8984375 to 0.8984375
- text_grad: bfloat16 [8, 32, 4096], P('sy', 'sx'), may hold values from -0.29882812 to 0.29882812
Outputs:
- prediction: bfloat16 [8, 16, 512], P('sy', 'sx')
- text_out: bfloat16 [8, 32, 4096], P('sy', 'sx')
- grad_down_conv: float32 [288, 128], replicated
- grad_down_proj: float32 [128, 4096], replicated
- grad_up_proj: float32 [4096, 128], replicated
- grad_up_out: float32 [128, 32], replicated
All inputs are finite; a program needn't handle non-finite values.
Results may differ from a plain program's by a relative error of at most 0.028.
Values may be sent and summed in bfloat16 or wider, within the bound.
No kernel may reach another device: no remote copies, remote signals or barrier semaphores. Data moves between devices by JAX's collectives and lax.ppermute only.
A program may use at most 192 MiB of HBM per device.

v0:
```python
import math

import jax
import jax.numpy as jnp
import numpy as np
from jax import lax
from jax.experimental import pallas as pl
from jax.experimental.pallas import tpu as pltpu
from jax.sharding import PartitionSpec as P

HD = 128
EPSILON = 1e-05
NEG_SCORE = -1e30
ROPE_BASE = 500000.0
SCALE = HD ** (-0.5)
LOG2E = math.log2(math.e)
LN2 = math.log(2.0)
F32 = jnp.float32
BF16 = jnp.bfloat16
MIB = 1024 * 1024
VMEM_BYTES = 56 * MIB
SMALL_BYTES = 16 * MIB


def dot(left, right):
    return jnp.dot(left, right, preferred_element_type=F32)


def dot_nt(left, right):
    return lax.dot_general(left, right, (((1,), (1,)), ((), ())), preferred_element_type=F32)


def silu_slope(values):
    sigma = jax.nn.sigmoid(values)
    return sigma * (1.0 + values * (1.0 - sigma))


def silu(values):
    return values * jax.nn.sigmoid(values)


def iota(shape, dim):
    return lax.broadcasted_iota(jnp.int32, shape, dim)


def flip(values):
    return values.astype(F32).T.astype(BF16)


def call(kernel, place, inputs, outs, scratch=(), flops=0, after=(), room=VMEM_BYTES):
    inputs = [(place, pltpu.SMEM)] + list(inputs)
    count = len(inputs)
    skip = count + len(after)
    moved = sum(math.prod(a.shape) * a.dtype.itemsize for a in list(outs) + [a for a, space in inputs if space is None])
    return pl.pallas_call(
        lambda *refs: kernel(*refs[:count], *refs[skip:]),
        out_shape=outs,
        in_specs=[pl.BlockSpec(memory_space=pltpu.VMEM if space is None else space) for _, space in inputs]
        + [pl.BlockSpec(memory_space=pl.ANY) for _ in after],
        out_specs=[pl.BlockSpec(memory_space=pltpu.VMEM) for _ in outs],
        scratch_shapes=list(scratch),
        compiler_params=pltpu.CompilerParams(vmem_limit_bytes=room),
        cost_estimate=pl.CostEstimate(flops=flops, bytes_accessed=moved, transcendentals=0),
    )(*[a for a, _ in inputs], *after)


def fetch(moves, sems):
    moves = [pltpu.make_async_copy(far, near, sems.at[n]) for n, (far, near) in enumerate(moves)]
    for move in moves:
        move.start()
    return moves


def whole_row(gain):
    return jnp.concatenate([gain[r : r + 1, :].astype(F32) for r in range(gain.shape[0])], axis=1)


def weights_kernel(
    place, gain, w_conv, w_down_far, wq_far, wk_far, wv_far, w_up_far, wo_far,
    proj, proj_t, mapped, u, gram, z, conv_t,
    w_down, wq, wk, wv, w_up, wo, sems,
):
    cols = pl.ds(pl.multiple_of(place[0] * HD, HD), HD)
    moves = fetch(
        [(w_down_far, w_down), (wq_far.at[:, cols], wq), (wk_far.at[:, cols], wk), (wv_far.at[:, cols], wv),
         (w_up_far, w_up), (wo_far.at[cols, :], wo)],
        sems,
    )
    conv_t[...] = flip(w_conv[...])
    moves[0].wait()
    down = w_down[...]
    scaled = (down.astype(F32) * whole_row(gain)).astype(BF16)
    gram[...] = dot_nt(down, down).astype(BF16)
    for n, w in enumerate((wq, wk, wv)):
        cols = slice(n * HD, (n + 1) * HD)
        moves[1 + n].wait()
        total = dot(scaled, w[...])
        proj[:, cols] = total.astype(BF16)
        proj_t[cols, :] = total.T.astype(BF16)
        mapped[:, cols] = total.astype(BF16)
        if n < 2:
            mapped[:, (3 + n) * HD : (4 + n) * HD] = pltpu.roll(total, HD // 2, 1).astype(BF16)
    moves[4].wait()
    z[...] = dot(down, w_up[...]).astype(BF16)
    moves[5].wait()
    u[...] = dot(wo[...], w_up[...]).astype(BF16)


def pick(rows, total, spot):
    return (iota((total, rows), 0) == iota((total, rows), 1) + spot).astype(BF16)


def gathered(parts, group):
    rows = parts[0].shape[0]
    total = rows * len(parts)
    return sum(dot(pick(rows, total, (group ^ k) * rows), part[...]) for k, part in enumerate(parts))


def text_kernel(count, repeat, place, *refs):
    gain, wq_far, wk_far, wv_far = refs[:4]
    parts = refs[4 : 4 + count]
    outs = refs[4 + count : -4]
    weights, normed, sums, sems = refs[-4:]
    chunks, _, deep, wide = weights.shape
    cols = pl.ds(pl.multiple_of(place[4] * wide, wide), wide)
    moves = fetch(
        [(far.at[c * deep : (c + 1) * deep, cols], weights.at[c, n])
         for c in range(chunks) for n, far in enumerate((wq_far, wk_far, wv_far))],
        sems,
    )
    rows = normed.shape[0] // 2
    row = whole_row(gain)
    for r in range(2):
        x = gathered([part.at[r] for part in parts], place[2])
        inverse = lax.rsqrt(jnp.mean(x * x, axis=-1, keepdims=True) + EPSILON)
        normed[r * rows : (r + 1) * rows, :] = (x * inverse * row).astype(BF16)
    for c in range(chunks):
        here = normed[:, c * deep : (c + 1) * deep]
        for n in range(3):
            moves[3 * c + n].wait()
            term = dot(here, weights[c, n])
            sums[n] = term if c == 0 else sums[n] + term
    for k, out in enumerate(outs):
        head = pl.ds(pl.multiple_of((place[3] ^ k) // repeat * HD, HD), HD)
        for n in range(3):
            out[:, n * HD : (n + 1) * HD] = sums[n, :, head].astype(BF16)


def text_grad_kernel(count, repeat, place, wo_far, mix, *refs):
    parts = refs[:count]
    outs = refs[count : -3]
    wo, total, sems = refs[-3:]
    groups, deep, _ = wo.shape
    moves = fetch([(wo_far.at[g * deep : (g + 1) * deep, :], wo.at[g]) for g in range(groups)], sems)
    grad_t = gathered([part.at[2] for part in parts], place[2]).T.astype(BF16)
    for g in range(groups):
        moves[g].wait()
        total[g * deep : (g + 1) * deep, :] = dot(wo[g], grad_t)
    for k, out in enumerate(outs):
        peer = place[5] ^ k
        rows = out.shape[0]
        out[:, :HD] = total[pl.ds(pl.multiple_of(peer // repeat * HD, HD), HD), :].T.astype(BF16)
        out[:, HD:] = mix[pl.ds(pl.multiple_of(peer * rows, rows), rows), :]


def text_out_kernel(repeat, peers, place, wo_far, *refs):
    mixes = refs[:peers]
    outs = refs[peers:-3]
    wo, mixed, sems = refs[-3:]
    groups, deep, width = wo.shape
    moves = fetch([(wo_far.at[g * deep : (g + 1) * deep, :], wo.at[g]) for g in range(groups)], sems)
    for k, mix in enumerate(mixes):
        peer = place[5] ^ k

        @pl.when(peer % repeat == 0)
        def _():
            mixed[:, pl.ds(pl.multiple_of(peer // repeat * HD, HD), HD)] = mix[:, HD:]

    total = 0.0
    for g in range(groups):
        moves[g].wait()
        total = total + dot(mixed[:, g * deep : (g + 1) * deep], wo[g])
    whole = total.astype(BF16)
    for k, out in enumerate(outs):
        rows = out.shape[0]
        out[...] = dot(pick(rows, whole.shape[0], (place[2] ^ k) * rows).astype(F32).T.astype(BF16), whole).astype(BF16)


def turned(values, cos, sin):
    return values * cos + pltpu.roll(values, HD // 2, 1) * sin


def rope_tables(positions):
    half = HD // 2
    freq = np.exp(-(2.0 * np.arange(half) / HD) * math.log(ROPE_BASE)).astype(np.float32)
    angle = np.asarray(positions, np.float64)[:, None] * np.concatenate([freq, freq])[None].astype(np.float64)
    sign = np.where(np.arange(HD) < half, -1.0, 1.0)[None]
    return np.stack([np.cos(angle), np.sin(angle) * sign]).astype(np.float32)


def angles(cos_start, sin_start, steps):
    return cos_start * steps[0] - sin_start * steps[1], sin_start * steps[0] + cos_start * steps[1]


def start_row(starts, thr, b, extra):
    row = pl.ds(thr[b] + b * extra, 1)
    return starts[0, row, :], starts[1, row, :]


def image_kernel(high, wide, width, extra, thr, lat_all, cell, conv_t, proj_t, mapped, gram, starts, steps, steps_t, *refs):
    pre_down, act_t, patch_t, q_img, qt, k_img, kt, v_img, vt = refs[-9:]
    images, length, _ = pre_down.shape
    for n in range(images):
        number = pl.program_id(0) * images + n
        lanes = slice(n * length, (n + 1) * length)
        lat = lat_all[:, n * length : (n + 1) * length]
        chan = lat.shape[0]
        row = cell[0:1, :]
        col = cell[1:2, :]
        for r in range(3):
            for c in range(3):
                tap = r * 3 + c
                step = (r - 1) * wide + (c - 1)
                moved = pltpu.roll(lat, -step % lat.shape[1], 1) if step else lat
                keep = (row + (r - 1) >= 0) & (row + (r - 1) < high)
                keep &= (col + (c - 1) >= 0) & (col + (c - 1) < wide)
                patch_t[n, tap * chan : (tap + 1) * chan, :] = jnp.where(keep, moved, 0.0).astype(BF16)
        cos_start, sin_start = start_row(starts, thr, number, extra)
        before_t = dot(conv_t[...], patch_t[n])
        flat_t = silu(before_t).astype(BF16)
        act_t[n] = flat_t
        square = jnp.sum(dot(gram[...], flat_t) * flat_t.astype(F32), axis=0, keepdims=True)
        inv = lax.rsqrt(square * (1.0 / width) + EPSILON)
        heads_t = dot(proj_t[...], flat_t) * inv
        half = HD // 2
        column = lambda values: jnp.broadcast_to(values, (8, HD)).T[half:, :1]
        cos, sin = angles(column(cos_start), column(sin_start), steps_t)
        for at, out, scale in ((0, qt.at[n], SCALE * LOG2E), (HD, kt.at[:, lanes], 1.0)):
            first = heads_t[at : at + half]
            second = heads_t[at + half : at + HD]
            out[:half, :] = ((first * cos - second * sin) * scale).astype(BF16)
            out[half:, :] = ((second * cos + first * sin) * scale).astype(BF16)
        vt[:, lanes] = heads_t[2 * HD :].astype(BF16)
        before = before_t.T
        pre_down[n] = before
        act = silu(before).astype(BF16)
        square = jnp.sum(dot(act, gram[...]) * act.astype(F32), axis=-1, keepdims=True)
        inv = lax.rsqrt(square * (1.0 / width) + EPSILON)
        heads = dot(act, mapped[...])
        cos, sin = angles(cos_start, sin_start, steps)
        cos = cos * inv
        sin = sin * inv
        query = heads[:, :HD] * cos + heads[:, 3 * HD : 4 * HD] * sin
        q_img[n] = (query * (SCALE * LOG2E)).astype(BF16)
        k_img[n] = (heads[:, HD : 2 * HD] * cos + heads[:, 4 * HD :] * sin).astype(BF16)
        v_img[n] = (heads[:, 2 * HD : 3 * HD] * inv).astype(BF16)


def image_rows(sizes, thr, lat_t, cell, conv_t, proj_t, mapped, gram, starts, steps, steps_t, after):
    blocks = thr.shape[0]
    length = steps.shape[1]
    chan = lat_t.shape[0]
    down_chan, taps = conv_t.shape
    whole = lambda a: pl.BlockSpec(a.shape, lambda b: (0,) * len(a.shape))
    outs = [(length, down_chan, F32), (down_chan, length, BF16), (taps, length, BF16), (length, HD, BF16),
            (HD, length, BF16), (length, HD, BF16), None, (length, HD, BF16), None]
    per = 2
    flat = pl.BlockSpec((HD, per * length), lambda b: (0, b))
    return pl.pallas_call(
        lambda *refs: image_kernel(*sizes, *refs),
        out_shape=[jax.ShapeDtypeStruct((blocks, *o[:2]), o[2]) if o else jax.ShapeDtypeStruct((HD, blocks * length), BF16)
                   for o in outs],
        grid=(blocks // per,),
        in_specs=[pl.BlockSpec(memory_space=pltpu.SMEM), pl.BlockSpec((chan, per * length), lambda b: (0, b))]
        + [whole(a) for a in (cell, conv_t, proj_t, mapped, gram, starts, steps, steps_t)]
        + [pl.BlockSpec(memory_space=pl.ANY) for _ in after],
        out_specs=[pl.BlockSpec((per, *o[:2]), lambda b: (b, 0, 0)) if o else flat for o in outs],
        compiler_params=pltpu.CompilerParams(vmem_limit_bytes=VMEM_BYTES),
        cost_estimate=pl.CostEstimate(flops=8_000_000_000, bytes_accessed=8_000_000, transcendentals=0),
    )(thr, lat_t, cell, conv_t, proj_t, mapped, gram, starts, steps, steps_t, *after)


STRIP = 128


def strips(rows):
    return [slice(at, at + STRIP) for at in range(0, rows, STRIP)]


def attend_kernel(
    head, thr, near, far, u, qt_far, k_img_far, vt_far, *refs,
):
    texts = refs[:-18]
    (part, q_txt, qt_txt, k_txt, kt_txt, v_txt, mix_t, mix_txt_t, mix_txt, lse, lse_txt,
     scores, probs, text, qt, keys, vt, sems) = refs[-18:]
    blocks, length, _ = part.shape
    text_total = q_txt.shape[0]
    moves = fetch(
        [(k_img_far, keys.at[text_total:, :]), (qt_far, qt), (vt_far, vt.at[:HD, text_total:])], sems
    )
    row = iota((text_total, 1), 0)
    rows = text_total // blocks
    core = head[5] // len(texts)
    for k, values in enumerate(texts):
        pair = head[5] % len(texts) ^ k
        for r in range(2):
            spot = pl.ds(pl.multiple_of((2 * pair + (core ^ r)) * rows, rows), rows)
            text[spot, :] = values[r * rows : (r + 1) * rows, :]
    shifted = row >= sum(jnp.where(row // rows == b, thr[b], 0) for b in range(blocks))
    cos = jnp.where(shifted, far[0], near[0])
    sin = jnp.where(shifted, far[1], near[1])
    query = turned(text[:, :HD].astype(F32), cos, sin) * (SCALE * LOG2E)
    q_txt[...] = query.astype(BF16)
    qt_txt[...] = query.T.astype(BF16)
    key = turned(text[:, HD : 2 * HD].astype(F32), cos, sin)
    k_txt[...] = key.astype(BF16)
    keys[:text_total, :] = key.astype(BF16)
    kt_txt[...] = key.T.astype(BF16)
    v_txt[...] = text[:, 2 * HD :]
    vt[:HD, :text_total] = flip(text[:, 2 * HD :])
    vt[HD:, :] = jnp.ones((vt.shape[0] - HD, vt.shape[1]), BF16)
    for move in moves:
        move.wait()

    def begin(n):
        turned_query, count, _ = jobs[n]
        scores[n % 2, :count, : turned_query.shape[1]] = dot(keys[:count, :], turned_query)

    def softmax(n):
        turned_query, count, seen = jobs[n]
        wide = turned_query.shape[1]
        here = scores.at[n % 2]
        weights = probs.at[n % 2]
        fold = lambda values: values.reshape(STRIP // 8, 8, wide)
        top = None
        for at in strips(count):
            s = here[at, :wide]
            mask = seen(at)
            if mask is not None:
                s = jnp.where(mask, s, NEG_SCORE)
                here[at, :wide] = s
            peak = jnp.max(fold(s), axis=0)
            top = peak if top is None else jnp.maximum(top, peak)
        top = jnp.max(top, axis=0, keepdims=True)
        for at in strips(count):
            p = jnp.exp2(here[at, :wide] - top)
            mask = seen(at)
            if mask is not None:
                p = jnp.where(mask, p, 0.0)
            weights[at, :wide] = p.astype(BF16)
        mixed = dot(vt[:, :count], weights[:count, :wide])
        whole = mixed[HD : HD + 1, :]
        return mixed[:HD] / whole, top + jnp.log2(whole)

    def image_seen(i):
        return lambda at: iota((STRIP, length), 0) + at.start < thr[i] if at.start < text_total else None

    lane = iota((1, text_total), 1)
    jobs = [(qt[i], text_total + (i + 1) * length, image_seen(i)) for i in range(blocks)]
    jobs.append((
        qt_txt[...], text_total + blocks * length,
        lambda at: iota((STRIP, text_total), 0) + at.start <= lane
        if at.start < text_total else lane >= thr[(at.start - text_total) // length],
    ))
    begin(0)
    for i in range(blocks):
        begin(i + 1)
        mixed, logs = softmax(i)
        lse[i] = logs
        mix_t[i] = mixed.astype(BF16)
        part[i] = dot(mixed.T.astype(BF16), u[...]).astype(part.dtype)
    mixed, logs = softmax(blocks)
    lse_txt[...] = logs
    mix_txt_t[...] = mixed.astype(BF16)
    mix_txt[...] = mixed.T.astype(BF16)


def up_kernel(head, parts, pre_down, z, w_up_out, preds, grad_copies, prediction, grad_out_t):
    act = silu(pre_down[head[1]]).astype(BF16)
    pre_up = dot(act, z[...])
    for p in range(parts.shape[0]):
        pre_up = pre_up + parts[p].astype(F32)
    up_act = silu(pre_up).astype(BF16)
    grad = (dot_nt(preds[...], w_up_out[...]) * silu_slope(pre_up)).astype(BF16)
    for p in range(parts.shape[0]):
        grad_copies[p] = grad
    prediction[...] = dot(up_act, w_up_out[...]).astype(BF16)
    grad_out_t[...] = dot(flip(preds[...]), up_act)


def piece_spot(place, groups, pairs, number):
    group = number // (2 * pairs) ^ place[2]
    pair = number // 2 % pairs ^ place[3]
    return group, pair, number % 2 ^ place[4]


def put_piece(place, pieces, number, rows, values):
    _, groups, pairs, _, _ = pieces.shape
    group, pair, core = piece_spot(place, groups, pairs, number)
    pieces[core, group, pair, rows, :] = values


def add_core_kernel(keep, received, *outs):
    for k, out in enumerate(outs):
        out[...] = (keep[k].astype(F32) + received[k].astype(F32)).astype(BF16)


def add_sx_kernel(count, *refs):
    for m, out in enumerate(refs[count:]):
        out[...] = sum(r[m].astype(F32) for r in refs[:count]).astype(BF16)


def add_kernel(*refs):
    refs[-1][...] = sum(r[...].astype(F32) for r in refs[:-1]).astype(BF16)


def unpack_kernel(groups, pairs, own, place, *refs):
    count = 2 * groups
    grad_conv, grad_down, grad_up, grad_out_t, rest = refs[count:]
    few = refs[0].shape[1] - 2 * own
    per = HD // own
    for n, part in enumerate(refs[:count]):
        for m in range(pairs):
            number = ((place[2] ^ n % groups) * pairs + (place[3] ^ m)) * 2 + (place[4] ^ n // groups)
            grad_up[pl.ds(pl.multiple_of(number * own, own), own), :] = part[m, :own, :].astype(F32)
            cols = pl.ds(pl.multiple_of(number // per * HD, HD), HD)
            rows = pl.ds(pl.multiple_of(number % per * own, own), own)
            grad_down[rows, cols] = part[m, own : 2 * own, :].astype(F32)
            rest[pl.ds(pl.multiple_of(number * few, few), few), :] = part[m, 2 * own :, :].astype(F32)
    taps = grad_conv.shape[0]
    grad_conv[...] = rest[:taps, :]
    grad_out_t[...] = rest[taps : taps + grad_out_t.shape[0], :]


def plain(kernel, inputs, outs, after=()):
    whole = lambda a: pl.BlockSpec(a.shape, lambda: (0,) * len(a.shape))
    moved = sum(math.prod(a.shape) * a.dtype.itemsize for a in list(inputs) + list(outs))
    return pl.pallas_call(
        lambda *refs: kernel(*refs[: len(inputs)], *refs[len(inputs) + len(after) :]),
        out_shape=outs,
        in_specs=[whole(a) for a in inputs] + [pl.BlockSpec(memory_space=pl.ANY) for _ in after],
        out_specs=[whole(a) for a in outs],
        compiler_params=pltpu.CompilerParams(vmem_limit_bytes=SMALL_BYTES),
        cost_estimate=pl.CostEstimate(flops=0, bytes_accessed=moved, transcendentals=0),
    )(*inputs, *after)


def score_products(keys, values, room, first, last, turned_query, turned_grad):
    scores, pulls = room[:2]
    wide = turned_query.shape[1]
    scores[first:last, :wide] = dot(keys[first:last, :], turned_query)
    pulls[first:last, :wide] = dot(values[first:last, :], turned_grad)


def score_grads(room, first, last, logs, delta, seen):
    scores, pulls, probs, slopes = room
    wide = logs.shape[1]
    for at in strips(last)[first // STRIP :]:
        p = jnp.exp2(scores[at, :wide] - logs)
        mask = seen(at)
        if mask is not None:
            p = jnp.where(mask, p, 0.0)
        probs[at, :wide] = p.astype(BF16)
        slopes[at, :wide] = (p * (pulls[at, :wide] - delta)).astype(BF16)


def text_backward_kernel(place, thr, k_img, v_img, q_txt, qt_txt, mix_txt_t, lse_txt, *refs):
    backs = refs[:-7]
    dk, dv, d_txt, *room = refs[-7:]
    text_total = q_txt.shape[0]
    total = k_img.shape[0]
    blocks = thr.shape[0]
    rows = text_total // blocks
    for k, back in enumerate(backs):
        d_txt[pl.ds(pl.multiple_of((place[5] ^ k) * rows, rows), rows), :] = back[:, :HD]
    d_txt_t = d_txt[...].astype(F32).T
    delta = jnp.sum(d_txt_t * mix_txt_t[...].astype(F32), axis=0, keepdims=True)
    lane = iota((1, text_total), 1)
    score_products(k_img, v_img, room, 0, total, qt_txt[...], d_txt_t.astype(BF16))
    score_grads(
        room, 0, total, lse_txt[...], delta,
        lambda at: lane >= thr[at.start // (total // blocks)],
    )
    probs, slopes = room[2:]
    dk[...] = dot(slopes[...], q_txt[...])
    dv[...] = dot(probs[...], d_txt[...])


def backward_kernel(
    share, copies, extra, place, thr, grad_pre, k_txt, kt_txt, v_txt, lse, u, proj, gram, z, gain, starts, steps, grad_out_t, *refs,
):
    blocks, length, _ = grad_pre.shape
    (k_img_far, v_img_far, qt_far, kt_far, q_img_far, mix_t_far, dk_far, dv_far, pre_down_far, act_t_far, patch_t_far,
     wq_far, wk_far, wv_far, wo_far, w_up_far, w_down_far,
     keep, send,
     pieces, dq, dk, dv, cross_sum, small_sum, scores, pulls, probs, slopes,
     keys, values, qt, kt, q_img, mix_t, dk_text, dv_text, pre_down, act_t, patch_t, wq, wk, wv, wo, w_up, w_down,
     sems) = refs
    text_total = k_txt.shape[0]
    width = w_down.shape[1]
    cols = pl.ds(pl.multiple_of(place[0] * HD, HD), HD)
    moves = fetch(
        [(k_img_far, keys.at[text_total:, :]), (v_img_far, values.at[text_total:, :]), (qt_far, qt),
         (kt_far, kt.at[:, text_total:]), (q_img_far, q_img), (mix_t_far, mix_t), (dk_far, dk_text), (dv_far, dv_text),
         (pre_down_far, pre_down), (act_t_far, act_t), (patch_t_far, patch_t),
         (wq_far.at[:, cols], wq), (wk_far.at[:, cols], wk), (wv_far.at[:, cols], wv), (wo_far.at[cols, :], wo),
         (w_up_far, w_up), (w_down_far, w_down)],
        sems,
    )
    cross_sum[...] = jnp.zeros_like(cross_sum)
    small_sum[...] = jnp.zeros_like(small_sum)
    keys[:text_total, :] = k_txt[...]
    values[:text_total, :] = v_txt[...]
    kt[:, :text_total] = kt_txt[...]
    for move in moves[:6]:
        move.wait()

    def begin(i):
        grad = grad_pre[i]
        cross_sum[...] += dot(mix_t[i], grad)
        d_t = dot_nt(u[...], grad).astype(BF16)
        delta = jnp.sum(d_t.astype(F32) * mix_t[i].astype(F32), axis=0, keepdims=True)
        room = [ref.at[i % 2] for ref in (scores, pulls, probs, slopes)]
        score_products(keys, values, room, 0, text_total + (i + 1) * length, qt[i], d_t)
        return room, delta, dot_nt(grad, u[...]).astype(BF16)

    def add(total, before, values):
        if before:
            total[:before, :] += values[:before]
        total[before : before + length, :] = values[before:]

    ahead = begin(0)
    for i in range(blocks):
        room, delta, d_out = ahead
        if i + 1 < blocks:
            ahead = begin(i + 1)
        before = i * length
        end = text_total + before + length
        score_grads(
            room, 0, end, lse[i], delta,
            lambda at: iota((STRIP, length), 0) + at.start < thr[i] if at.start < text_total else None,
        )
        add(dv, before, dot(room[2][text_total:end, :length], d_out))
        add(dk, before, dot(room[3][text_total:end, :length], q_img[i]))
        dq[i] = dot(kt[:, :end], room[3][:end, :length]).T
    for move in moves[6:11]:
        move.wait()
    taps = patch_t.shape[1]

    def block(b, query):
        cos, sin = angles(*start_row(starts, thr, b, extra), steps)
        own_rows = pl.ds(pl.multiple_of(b * length, length), length)

        def back(values):
            return values * cos - pltpu.roll(values, HD // 2, 1) * sin

        before = pre_down[b]
        act = silu(before).astype(BF16)
        act_wide = act.astype(F32)
        image = dot(act, gram[...])
        square = jnp.sum(image * act_wide, axis=-1, keepdims=True)
        inv = lax.rsqrt(square * (1.0 / width) + EPSILON)
        heads = jnp.concatenate(
            [back(query) * (inv * SCALE), back(dk[own_rows, :] + dk_text[own_rows, :]) * (inv * LN2),
             (dv[own_rows, :] + dv_text[own_rows, :]) * inv], axis=1
        ).astype(BF16)
        lift = dot_nt(heads, proj[...])
        crow = inv * inv * (jnp.sum(act_wide * lift, axis=-1, keepdims=True) * (1.0 / width))
        grad = grad_pre[b]
        d_act = (lift - crow * image) * copies + dot_nt(grad, z[...]) * share
        slope = (d_act * silu_slope(before)).astype(BF16)
        flipped = act_t[b]
        return (
            dot(patch_t[b], slope),
            dot(flipped, heads),
            dot(flipped, (act_wide * crow).astype(BF16)),
            dot(flipped, grad),
        )

    def step(n, carry):
        for b in (n, blocks // 2 + n):
            conv, *more = block(b, dq[b])
            small_sum[:taps, :] += conv
            carry = tuple(a + m for a, m in zip(carry, more))
        return carry

    rank = act_t.shape[1]
    spread, pull, inner = lax.fori_loop(
        0, blocks // 2, step,
        (jnp.zeros((rank, 3 * HD), F32), jnp.zeros((rank, rank), F32), jnp.zeros((rank, grad_pre.shape[2]), F32)),
    )
    for move in moves[11:]:
        move.wait()
    spread = (spread * copies).astype(BF16)
    pull = (pull * copies).astype(BF16)
    cross = (cross_sum[...] * copies).T.astype(BF16)
    inner_t = (inner * share).T.astype(BF16)
    inner = (inner * share).astype(BF16)
    small_sum[taps : taps + grad_out_t.shape[0], :] = grad_out_t[...]
    _, groups, pairs, rows, _ = pieces.shape
    own = width // (2 * groups * pairs)
    few = rows - 2 * own
    for at in range(0, width, HD):
        cols = slice(at, at + HD)
        down = dot_nt(spread[:, :HD], wq[cols, :]) + dot_nt(spread[:, HD : 2 * HD], wk[cols, :])
        down = (down + dot_nt(spread[:, 2 * HD :], wv[cols, :])) * gain[at // HD : at // HD + 1, :].astype(F32)
        down = (down - dot(pull, w_down[:, cols]) + dot_nt(inner, w_up[cols, :])).astype(BF16)
        up = (dot(cross, wo[:, cols]) + dot(inner_t, w_down[:, cols])).T.astype(BF16)
        for part in range(0, HD, own):
            put_piece(place, pieces, (at + part) // own, slice(0, own), up[part : part + own])
            put_piece(place, pieces, (at + part) // own, slice(own, 2 * own), down[part : part + own])
    for number in range(2 * groups * pairs):
        put_piece(place, pieces, number, slice(2 * own, rows), small_sum[number * few : (number + 1) * few, :].astype(BF16))
    for move in fetch([(pieces.at[0], keep), (pieces.at[1], send)], sems):
        move.wait()


def shards(
    text_tokens,
    latent,
    image_offset,
    norm_gain,
    w_query,
    w_key,
    w_value,
    w_out,
    w_down_conv,
    w_down_proj,
    w_up_proj,
    w_up_out,
    pred_grad,
    text_grad,
):
    axes = ("sy", "sx")
    text_local = text_tokens[0]
    text_rows, width = text_local.shape
    lat_chan = w_up_out.shape[1]
    up_chan = w_up_proj.shape[1]
    down_chan = w_down_conv.shape[1]
    taps = w_down_conv.shape[0]
    tile_rows = latent.shape[1]
    tile_cols = latent.shape[2] // lat_chan
    row_groups = lax.axis_size("sx")
    blocks = lax.axis_size("sy")
    devices = row_groups * blocks
    high = tile_rows * row_groups
    length = high * tile_cols
    text_block = text_rows * row_groups
    text_total = text_block * blocks
    total = length * blocks
    block_len = length + text_block
    heads_here = w_query.shape[1] // HD
    repeat = blocks // heads_here
    assert heads_here * repeat == blocks and blocks % 2 == 0
    own = lax.axis_index("sy")
    share = 1.0 / devices
    copies = 1.0 / repeat

    device = own * row_groups + lax.axis_index("sx").astype(jnp.int32)
    group = lax.axis_index("sx").astype(jnp.int32)
    own = own.astype(jnp.int32)
    head = jnp.stack([own // repeat, device, group, own // 2, own % 2, own])

    def spread_over(values, axis, count):
        return lax.all_to_all(jnp.broadcast_to(values[None], (count,) + values.shape), axis, 0, 0)

    tag = jnp.broadcast_to(image_offset.astype(BF16)[:, None], (tile_rows, HD))
    packed = jnp.concatenate([latent[0], tag], axis=1)
    hop = lambda values, axis, by: lax.ppermute(
        values, axis, [(i, i ^ by) for i in range(row_groups if axis == "sx" else blocks)]
    )
    trio = jnp.stack([text_local, hop(text_local, "sy", 1), text_grad[0]])
    text_parts = [trio] + [hop(trio, "sx", k) for k in range(1, row_groups)]
    side = spread_over(packed, axes, devices)

    gain = norm_gain.reshape(width // HD, HD)
    small = jax.ShapeDtypeStruct
    square = small((down_chan, down_chan), BF16)
    pairs = blocks // 2
    vmem = pltpu.VMEM
    dma = lambda count: pltpu.SemaphoreType.DMA((count,))
    bf = lambda *shape: small(shape, BF16)
    proj, proj_t, mapped, u, gram, z, conv_t = call(
        weights_kernel, head,
        [(gain, None), (w_down_conv, None)]
        + [(a, pl.ANY) for a in (w_down_proj, w_query, w_key, w_value, w_up_proj, w_out)],
        [bf(down_chan, 3 * HD), bf(3 * HD, down_chan), bf(down_chan, 5 * HD), bf(HD, up_chan),
         bf(down_chan, down_chan), bf(down_chan, up_chan), bf(down_chan, taps)],
        [vmem((down_chan, width), BF16)] + [vmem((width, HD), BF16)] * 3
        + [vmem((width, up_chan), BF16), vmem((HD, width), BF16), dma(6)],
        flops=4_000_000_000,
    )
    both = 2 * text_block
    chunks = 8
    wide = heads_here * HD // 2
    text_here = call(
        lambda *refs: text_kernel(row_groups, repeat, *refs), head,
        [(gain, None)] + [(a, pl.ANY) for a in (w_query, w_key, w_value)] + [(a, None) for a in text_parts],
        [bf(both, 3 * HD)] * pairs,
        [vmem((chunks, 3, width // chunks, wide), BF16), vmem((both, width), BF16), vmem((3, both, wide), F32),
         dma(3 * chunks)],
        flops=6 * both * width * wide,
        after=[proj],
    )
    texts = [
        lax.ppermute(values, "sy", [(2 * z + c, c * pairs + (z ^ k)) for z in range(pairs) for c in range(2)])
        for k, values in enumerate(text_here)
    ]

    side = side.reshape(blocks, row_groups, tile_rows, -1)
    lat_t = side[..., : tile_cols * lat_chan].reshape(total, lat_chan).T.astype(F32)
    offsets = side[:, 0, 0, tile_cols * lat_chan].astype(jnp.int32)
    block_ids = jnp.arange(blocks, dtype=jnp.int32)
    thr = block_ids * text_block + offsets
    ids = np.arange(length, dtype=np.int32)
    cell = np.stack([ids // tile_cols, ids % tile_cols])
    at = np.arange(blocks)[:, None]
    steps = rope_tables(ids)
    steps_t = np.ascontiguousarray(np.swapaxes(steps, 1, 2)[:, HD // 2 :])
    starts = rope_tables((at * block_len + np.arange(text_block + 1)).reshape(-1))
    near = (at * block_len + np.arange(text_block)).reshape(-1)
    near, far = rope_tables(near), rope_tables(near + length)

    chunk = lambda kind, rows=length, cols=HD: small((blocks, rows, cols), kind)
    text_kind = small((text_total, HD), BF16)
    text_flip = small((HD, text_total), BF16)
    side_len = max(length, text_total)
    seq = text_total + total
    pre_down, act_t, patch_t, q_img, qt, k_img, kt, v_img, vt = image_rows(
        (high, tile_cols, width, 1), thr, lat_t, cell, conv_t, proj_t, mapped, gram, starts, steps, steps_t,
        text_here[:1]
    )
    part, q_txt, qt_txt, k_txt, kt_txt, v_txt, mix_t, mix_txt_t, mix_txt, lse, lse_txt = call(
        attend_kernel, head,
        [(thr, pltpu.SMEM), (near, None), (far, None), (u, None), (qt, pl.ANY), (k_img.reshape(total, HD), pl.ANY),
         (vt, pl.ANY)]
        + [(a, None) for a in texts],
        [chunk(BF16, length, up_chan), text_kind, text_flip, text_kind, text_flip, text_kind, chunk(BF16, HD, length),
         text_flip, text_kind, small((blocks, 1, length), F32), small((1, text_total), F32)],
        [vmem((2, seq, side_len), F32), vmem((2, seq, side_len), BF16), vmem((text_total, 3 * HD), BF16),
         vmem(qt.shape, BF16), vmem((seq, HD), BF16), vmem((HD + 16, seq), BF16), dma(3)],
        flops=6_000_000_000,
    )

    own_rows = tile_rows * tile_cols
    part = part if repeat == 1 else part * jnp.asarray(copies, BF16)
    parts = lax.all_to_all(part.reshape(devices, own_rows, up_chan), axes, 0, 0)
    wo_room = [vmem((4, heads_here * HD // 4, width), BF16)]
    text_back = call(
        lambda *refs: text_grad_kernel(row_groups, repeat, *refs), head,
        [(w_out, pl.ANY), (mix_txt, None)] + [(a, None) for a in text_parts],
        [bf(text_block, 2 * HD)] * blocks,
        wo_room + [vmem((heads_here * HD, text_block), F32), dma(4)],
        flops=2 * text_block * width * heads_here * HD,
        after=[part],
    )
    text_back = [text_back[0]] + [hop(text_back[k], "sy", k) for k in range(1, blocks)]
    grad_copies, prediction, grad_out_t = call(
        up_kernel, head,
        [(parts, None), (pre_down.reshape(devices, own_rows, down_chan), None), (z, None), (w_up_out, None),
         (pred_grad[0].reshape(own_rows, lat_chan), None)],
        [small((devices, own_rows, up_chan), BF16), small((own_rows, lat_chan), BF16), small((lat_chan, up_chan), F32)],
        flops=2_000_000_000,
        after=text_back[1:],
        room=SMALL_BYTES,
    )
    grad_pre = lax.all_to_all(grad_copies, axes, 0, 0).reshape(blocks, length, up_chan)

    own_part = width // devices
    few = -(-(taps + lat_chan) // (16 * devices)) * 16
    lump = lambda rows: small((pairs, rows, HD), BF16)
    flat = lambda rows: small((rows, HD), BF16)
    vmem = pltpu.VMEM
    def core_sum(keep, send, rows):
        return plain(add_core_kernel, [keep, hop(send, "sy", 1)], [lump(rows)] * row_groups)

    def sx_sum(sums, rows, after=()):
        sums = [sums[0]] + [hop(sums[k], "sx", k) for k in range(1, row_groups)]
        return plain(lambda *refs: add_sx_kernel(row_groups, *refs), sums, [flat(rows)] * pairs, after)

    def z_sum(sums, rows, after=()):
        sums = [sums[0]] + [hop(sums[m], "sy", 2 * m) for m in range(1, pairs)]
        return plain(add_kernel, sums, [flat(rows)], after)[0]

    def spread_z(mine):
        return jnp.stack([mine] + [hop(mine, "sy", 2 * m) for m in range(1, pairs)])

    def spread_sx(mine):
        near = [mine] + [hop(mine, "sx", k) for k in range(1, row_groups)]
        return near + [hop(values, "sy", 1) for values in near]

    mixed = call(
        lambda *refs: text_out_kernel(repeat, blocks, *refs), head,
        [(w_out, pl.ANY)] + [(a, None) for a in text_back],
        [bf(text_rows, width)] * row_groups,
        wo_room + [vmem((text_block, heads_here * HD), BF16), dma(4)],
        flops=2 * text_block * width * heads_here * HD,
        after=[grad_copies],
    )
    mixed = [mixed[0]] + [hop(mixed[k], "sx", k) for k in range(1, row_groups)]
    text_out = (text_local.astype(F32) + sum(m.astype(F32) for m in mixed)).astype(BF16)
    k_rows, v_rows = k_img.reshape(total, HD), v_img.reshape(total, HD)
    strip_room = lambda *lead: [vmem((*lead, side_len), F32)] * 2 + [vmem((*lead, side_len), BF16)] * 2
    dk, dv = call(
        text_backward_kernel, head,
        [(thr, pltpu.SMEM)] + [(a, None) for a in (k_rows, v_rows, q_txt, qt_txt, mix_txt_t, lse_txt, *text_back)],
        [small((total, HD), F32)] * 2,
        [vmem((text_total, HD), BF16)] + [vmem((total, text_total), kind) for kind in (F32, F32, BF16, BF16)],
        flops=2_000_000_000,
        after=mixed[:1] + [grad_copies],
    )
    rows = 2 * own_part + few
    near_arrays = (k_rows, v_rows, qt, kt, q_img, mix_t, dk, dv, pre_down, act_t, patch_t)
    far_arrays = near_arrays + (w_query, w_key, w_value, w_out, w_up_proj, w_down_proj)
    keep, send = call(
        lambda *refs: backward_kernel(share, copies, 1, *refs), head,
        [(thr, pltpu.SMEM)] + [(a, None) for a in (
            grad_pre, k_txt, kt_txt, v_txt, lse, u, proj, gram, z, gain, starts, steps, grad_out_t)]
        + [(a, pl.ANY) for a in far_arrays],
        [small((row_groups, pairs, rows, HD), BF16)] * 2,
        [vmem((2, row_groups, pairs, rows, HD), BF16), vmem((blocks, length, HD), F32), vmem((total, HD), F32),
         vmem((total, HD), F32), vmem((HD, up_chan), F32), vmem((devices * few, HD), F32)]
        + strip_room(2, seq)
        + [vmem((seq, HD), BF16)] * 2 + [vmem(qt.shape, BF16), vmem((HD, seq), BF16)]
        + [vmem(a.shape, a.dtype) for a in (q_img, mix_t, dk, dv, pre_down, act_t, patch_t)]
        + [vmem((width, HD), BF16)] * 3
        + [vmem((HD, width), BF16), vmem(w_up_proj.shape, BF16), vmem(w_down_proj.shape, BF16),
           pltpu.SemaphoreType.DMA((len(far_arrays),))],
        flops=30_000_000_000,
        after=mixed[1:],
    )
    mine = spread_z(z_sum(sx_sum(core_sum(keep, send, rows), rows), rows))
    grad_conv, grad_down, grad_up, grad_out_t = call(
        lambda *refs: unpack_kernel(row_groups, pairs, own_part, *refs), head,
        [(a, None) for a in spread_sx(mine)],
        [small((taps, down_chan), F32), small((down_chan, width), F32), small((width, up_chan), F32),
         small((lat_chan, up_chan), F32)],
        [vmem((devices * few, HD), F32)],
        room=2 * SMALL_BYTES,
    )
    return (
        prediction.reshape(1, tile_rows, tile_cols * lat_chan),
        text_out[None],
        grad_conv,
        grad_down,
        grad_up,
        grad_out_t.T,
    )


def solution(mesh):
    placed = (
        P("sy", "sx", None),
        P("sy", "sx", None),
        P("sy"),
        P(),
        P(None, "sx"),
        P(None, "sx"),
        P(None, "sx"),
        P("sx", None),
        P(),
        P(),
        P(),
        P(),
        P("sy", "sx", None),
        P("sy", "sx", None),
    )
    return jax.shard_map(
        shards,
        mesh=mesh,
        in_specs=placed,
        out_specs=(P("sy", "sx", None), P("sy", "sx", None), P(), P(), P(), P()),
        check_vma=False,
    )
```

profile of v0, /device:TPU:0, one launch (start us, length us, event | category | flops | bytes accessed | tf_op | source)
XLA Modules:
  0.0 183.3 jit_solution(14054753099083818553)
XLA Ops:
  0.6 0.5 collective-permute-start
  1.8 0.7 concatenate.3
  2.5 0.7 broadcast_in_dim.7
  3.2 7.0 %all-to-all-start = ((bf16[32,4,640]{2,1,0:T(4,128)(2,1)}), bf16[32,4,640]{2,1,0:T(4,128)(2,1)S(1)}, u32[]{:S(2)}, u32[]{:S(2)}) async-start(bf16[32,4,640]{2,1,0:T(4,128)(2,1)} %broadcast_in_dim.7), calls=%async_computation | async-start | bytes 327680 | tf_op jit(solution)/shard_map/all_to_all | solution.py:665
  10.2 0.6 stack.45.refs_0_
  10.8 0.9 pad_maximum_fusion.1.refs_5_.refs_3_
  11.7 2.7 %collective-permute-start.3 = (bf16[3,8,4096]{2,1,0:T(8,128)(2,1)S(1)}, bf16[3,8,4096]{2,1,0:T(8,128)(2,1)S(1)}, u32[]{:S(2)}, u32[]{:S(2)}) collective-permute-start(bf16[3,8,4096]{2,1,0:T(8,128)(2,1)S(1)} %pad_maximum_fusion.1.refs_5_.refs_3_), channel_id=1, source_target_pairs={{0,24},{8,16},{16,8},{24,0},{1,25},{9,17},{17,9},{25,1},{2,26},{10... | collective-permute-start | bytes 589832 | tf_op jit(solution)/shard_map/ppermute | solution.py:669
  14.5 0.6 collective-permute-start.2
  15.3 6.1 %shard_map.235 = (bf16[128,384]{1,0:T(8,128)(2,1)}, bf16[384,128]{1,0:T(8,128)(2,1)}, bf16[128,640]{1,0:T(8,128)(2,1)}, bf16[128,128]{1,0:T(8,128)(2,1)}, bf16[1...) custom-call(s32[6]{0:T(128)} %stack.45.refs_0_, bf16[32,128]{1,0:T(8,128)(2,1)} %bitcast.37, ...), custom_call_target="tpu_custom_call" | custom-call | flops 4000000000 | bytes 614400 | tf_op jit(solution)/shard_map/pallas_call | solution.py:55
  21.5 3.5 %collective-permute-done.2.refs_7_.refs_5_ = bf16[3,8,4096]{2,1,0:T(8,128)(2,1)S(1)} collective-permute-done((bf16[3,8,4096]{2,1,0:T(8,128)(2,1)S(1)}, bf16[3,8,4096]{2,1,0:T(8,128)(2,1)S(1)}, u32[]{:S(2)}, u32[]{:S(2)}) %collective-permute-start.2) | collective-permute-done | bytes 196640 | tf_op jit(solution)/shard_map/ppermute | solution.py:669
  25.0 0.7 copy-done.15
  25.7 7.3 %shard_map.236 = (bf16[64,384]{1,0:T(8,128)(2,1)}, bf16[64,384]{1,0:T(8,128)(2,1)}, bf16[64,384]{1,0:T(8,128)(2,1)}, bf16[64,384]{1,0:T(8,128)(2,1)}) custom-call(s32[6]{0:T(128)} %stack.45.refs_0_, bf16[32,128]{1,0:T(8,128)(2,1)} %bitcast.38, bf16[4096,1024]{1,0:T(8,128)(2,1)} %refs_26_.1, bf16[4096,1024]{1,0:T(8,128)(2,1)} %refs_27_.1, ...), custom_call_target="tpu_custom_call" | custom-call | flops 805306368 | bytes 991232 | tf_op jit(solution)/shard_map/pallas_call | solution.py:55
  33.1 2.0 %collective-permute-start.6 = (bf16[64,384]{1,0:T(8,128)(2,1)}, bf16[64,384]{1,0:T(8,128)(2,1)S(1)}, u32[]{:S(2)}, u32[]{:S(2)}) collective-permute-start(bf16[64,384]{1,0:T(8,128)(2,1)} %get-tuple-element.79), channel_id=1, source_target_pairs={{0,2},{1,6},{2,3},{3,7},{4,0},{5,4},{6,1},{7,5},{8,10},{9,14},{10,... | collective-permute-start | bytes 147464 | tf_op jit(solution)/shard_map/ppermute | solution.py:706
  35.1 3.2 %collective-permute-start.7 = (bf16[64,384]{1,0:T(8,128)(2,1)}, bf16[64,384]{1,0:T(8,128)(2,1)S(1)}, u32[]{:S(2)}, u32[]{:S(2)}) collective-permute-start(bf16[64,384]{1,0:T(8,128)(2,1)} %get-tuple-element.80), channel_id=1, source_target_pairs={{0,3},{1,7},{2,2},{3,6},{4,1},{5,5},{6,0},{7,4},{8,11},{9,15},{10,... | collective-permute-start | bytes 147464 | tf_op jit(solution)/shard_map/ppermute | solution.py:706
  38.3 1.5 collective-permute-start.4
  40.1 0.6 multiply_add_fusion.refs_0_.refs_1_
  41.0 1.0 copy.29
  42.0 7.3 %shard_map.237 = (f32[8,256,128]{2,1,0:T(8,128)}, bf16[8,128,256]{2,1,0:T(8,128)(2,1)}, bf16[8,288,256]{2,1,0:T(8,128)(2,1)}, bf16[8,256,128]{2,1,0:T(8,128)(2,1...) custom-call(s32[8]{0:T(128)} %multiply_add_fusion.refs_0_.refs_1_, ...), custom_call_target="tpu_custom_call" | custom-call | flops 8000000000 | bytes 8000000 | tf_op jit(solution)/shard_map/pallas_call | solution.py:269
  49.4 0.5 copy-done.28
  50.0 9.3 %shard_map.238 = (bf16[8,256,128]{2,1,0:T(8,128)(2,1)}, bf16[256,128]{1,0:T(8,128)(2,1)}, bf16[128,256]{1,0:T(8,128)(2,1)}, bf16[256,128]{1,0:T(8,128)(2,1)}, bf...) custom-call(s32[6]{0:T(128)} %stack.45.refs_0_, ...), custom_call_target="tpu_custom_call" | custom-call | flops 6000000000 | bytes 2270208 | tf_op jit(solution)/shard_map/pallas_call | solution.py:55
  59.4 6.5 %all-to-all-start.1 = ((bf16[32,64,128]{2,1,0:T(8,128)(2,1)}), bf16[32,64,128]{2,1,0:T(8,128)(2,1)S(1)}, u32[]{:S(2)}, u32[]{:S(2)}) async-start(bf16[32,64,128]{2,1,0:T(8,128)(2,1)} %bitcast.27), calls=%async_computation.1 | async-start | bytes 1048576 | tf_op jit(solution)/shard_map/all_to_all | solution.py:747
  65.9 6.5 %shard_map.239 = (bf16[32,256]{1,0:T(8,128)(2,1)}, bf16[32,256]{1,0:T(8,128)(2,1)}, bf16[32,256]{1,0:T(8,128)(2,1)}, bf16[32,256]{1,0:T(8,128)(2,1)}, bf16[32,25...) custom-call(s32[6]{0:T(128)} %stack.45.refs_0_, ...), custom_call_target="tpu_custom_call" | custom-call | flops 268435456 | bytes 983040 | tf_op jit(solution)/shard_map/pallas_call | solution.py:55
  72.7 1.7 collective-permute-start.9
  74.4 2.6 %collective-permute-start.11 = (bf16[32,256]{1,0:T(8,128)(2,1)}, bf16[32,256]{1,0:T(8,128)(2,1)S(1)}, u32[]{:S(2)}, u32[]{:S(2)}) collective-permute-start(bf16[32,256]{1,0:T(8,128)(2,1)} %get-tuple-element.88), channel_id=1, source_target_pairs={{0,4},{1,5},{2,6},{3,7},{4,0},{5,1},{6,2},{7,3},{8,12},{9,13},{10,... | collective-permute-start | bytes 49160 | tf_op jit(solution)/shard_map/ppermute | solution.py:669
  77.1 3.5 %collective-permute-start.13 = (bf16[32,256]{1,0:T(8,128)(2,1)}, bf16[32,256]{1,0:T(8,128)(2,1)S(1)}, u32[]{:S(2)}, u32[]{:S(2)}) collective-permute-start(bf16[32,256]{1,0:T(8,128)(2,1)} %get-tuple-element.90), channel_id=1, source_target_pairs={{0,6},{1,7},{2,4},{3,5},{4,2},{5,3},{6,0},{7,1},{8,14},{9,15},{10,... | collective-permute-start | bytes 49160 | tf_op jit(solution)/shard_map/ppermute | solution.py:669
  80.9 1.0 collective-permute-done.11.refs_9_.refs_6_.refs_12_
  81.9 1.0 collective-permute-done.13.refs_11_.refs_8_.refs_14_
  82.9 2.9 %collective-permute-done.14.refs_12_.refs_9_.refs_15_ = bf16[32,256]{1,0:T(8,128)(2,1)S(1)} collective-permute-done((bf16[32,256]{1,0:T(8,128)(2,1)}, bf16[32,256]{1,0:T(8,128)(2,1)S(1)}, u32[]{:S(2)}, u32[]{:S(2)}) %collective-permute-start.14) | collective-permute-done | bytes 16416 | tf_op jit(solution)/shard_map/ppermute | solution.py:669
  85.8 1.6 shard_map.240
  87.5 3.1 %all-to-all-start.2 = ((bf16[32,64,128]{2,1,0:T(8,128)(2,1)}), bf16[32,64,128]{2,1,0:T(8,128)(2,1)S(1)}, u32[]{:S(2)}, u32[]{:S(2)}) async-start(bf16[32,64,128]{2,1,0:T(8,128)(2,1)} %get-tuple-element.94.refs_10_.refs_17_), calls=%async_computation.2 | async-start | bytes 1048576 | tf_op jit(solution)/shard_map/all_to_all | solution.py:767
  90.6 5.7 %shard_map.241 = (bf16[8,4096]{1,0:T(8,128)(2,1)}, bf16[8,4096]{1,0:T(8,128)(2,1)}, bf16[8,4096]{1,0:T(8,128)(2,1)}, bf16[8,4096]{1,0:T(8,128)(2,1)}) custom-call(s32[6]{0:T(128)} %stack.45.refs_0_, bf16[1024,4096]{1,0:T(8,128)(2,1)} %refs_29_.1, bf16[32,256]{1,0:T(8,128)(2,1)} %get-tuple-element.93.refs_2_.refs_8_, bf16[32,256]{1,0:T(8,128)(2,1)} %copy-done.3, ...), custom_call_target="tpu_custom_call" | custom-call | flops 268435456 | bytes 393216 | tf_op jit(solution)/shard_map/pallas_call | solution.py:55
  96.3 1.6 collective-permute-start.15
  98.0 1.5 collective-permute-start.16
  99.4 0.5 collective-permute-start.17
  99.9 3.9 %shard_map.242 = (f32[2048,128]{1,0:T(8,128)}, f32[2048,128]{1,0:T(8,128)}) custom-call(s32[6]{0:T(128)} %stack.45.refs_0_, s32[8]{0:T(128)} %multiply_add_fusion.refs_0_.refs_1_, bf16[2048,128]{1,0:T(8,128)(2,1)} %bitcast.43, bf16[2048,128]{1,0:T(8,128)(2,1)} %bitcast.45, bf16[256,128]{1,0:T(8,128)(2,1)} %get-tuple-element.108.refs_4_, ...), custom_call_target="tpu_custom_call" | custom-call | flops 2000000000 | bytes 3474432 | tf_op jit(solution)/shard_map/pallas_call | solution.py:55
  103.9 1.2 collective-permute-done.17.refs_34_
  105.1 1.5 all-to-all-done.2
  106.7 0.8 copy-done.17
  107.5 22.8 %shard_map.243 = (bf16[4,4,272,128]{3,2,1,0:T(8,128)(2,1)}, bf16[4,4,272,128]{3,2,1,0:T(8,128)(2,1)}) custom-call(s32[6]{0:T(128)} %stack.45.refs_0_, s32[8]{0:T(128)} %multiply_add_fusion.refs_0_.refs_1_, bf16[8,256,128]{2,1,0:T(8,128)(2,1)} %bitcast.30, bf16[256,128]{1,0:T(8,128)(2,1)} %get-tuple-element.99.refs_3_, ...), custom_call_target="tpu_custom_call" | custom-call | flops 30000001024 | bytes 3710976 | tf_op jit(solution)/shard_map/pallas_call | solution.py:55
  130.4 3.0 %collective-permute-done.18.refs_1_ = bf16[4,4,272,128]{3,2,1,0:T(8,128)(2,1)S(1)} collective-permute-done((bf16[4,4,272,128]{3,2,1,0:T(8,128)(2,1)}, bf16[4,4,272,128]{3,2,1,0:T(8,128)(2,1)S(1)}, u32[]{:S(2)}, u32[]{:S(2)}) %collective-permute-start.18) | collective-permute-done | bytes 1114144 | tf_op jit(solution)/shard_map/ppermute | solution.py:669
  133.3 1.2 copy-done
  135.1 1.5 collective-permute-start.20
  136.6 1.8 collective-permute-start.21
  138.4 6.0 %collective-permute-done.19.refs_1_ = bf16[4,272,128]{2,1,0:T(8,128)(2,1)S(1)} collective-permute-done((bf16[4,272,128]{2,1,0:T(8,128)(2,1)S(1)}, bf16[4,272,128]{2,1,0:T(8,128)(2,1)S(1)}, u32[]{:S(2)}, u32[]{:S(2)}) %collective-permute-start.19) | collective-permute-done | bytes 278560 | tf_op jit(solution)/shard_map/ppermute | solution.py:669
  144.4 5.2 %collective-permute-done.21.refs_3_ = bf16[4,272,128]{2,1,0:T(8,128)(2,1)S(1)} collective-permute-done((bf16[4,272,128]{2,1,0:T(8,128)(2,1)S(1)}, bf16[4,272,128]{2,1,0:T(8,128)(2,1)S(1)}, u32[]{:S(2)}, u32[]{:S(2)}) %collective-permute-start.21) | collective-permute-done | bytes 278560 | tf_op jit(solution)/shard_map/ppermute | solution.py:669
  149.8 1.0 collective-permute-start.22
  150.9 1.7 collective-permute-start.23
  152.6 1.7 collective-permute-start.24
  154.5 3.3 %collective-permute-done.23.refs_2_ = bf16[272,128]{1,0:T(8,128)(2,1)S(1)} collective-permute-done((bf16[272,128]{1,0:T(8,128)(2,1)S(1)}, bf16[272,128]{1,0:T(8,128)(2,1)S(1)}, u32[]{:S(2)}, u32[]{:S(2)}) %collective-permute-start.23) | collective-permute-done | bytes 69664 | tf_op jit(solution)/shard_map/ppermute | solution.py:669
  157.8 1.0 collective-permute-done.24.refs_3_
  158.8 1.8 collective-permute-start.27
  160.6 1.2 collective-permute-start.26
  161.8 1.5 collective-permute-start.25
  163.3 1.8 collective-permute-done.27
  165.1 1.5 collective-permute-done.26
  166.7 1.7 collective-permute-start.30
  168.4 1.1 collective-permute-start.29
  169.5 0.8 collective-permute-start.28
  170.3 0.7 reshape.49
  170.9 5.6 %collective-permute-done.30.refs_4_ = bf16[4,272,128]{2,1,0:T(8,128)(2,1)S(1)} collective-permute-done((bf16[4,272,128]{2,1,0:T(8,128)(2,1)S(1)}, bf16[4,272,128]{2,1,0:T(8,128)(2,1)S(1)}, u32[]{:S(2)}, u32[]{:S(2)}) %collective-permute-start.30) | collective-permute-done | bytes 278560 | tf_op jit(solution)/shard_map/ppermute | solution.py:669
  176.5 2.0 %collective-permute-done.29.refs_3_ = bf16[4,272,128]{2,1,0:T(8,128)(2,1)S(1)} collective-permute-done((bf16[4,272,128]{2,1,0:T(8,128)(2,1)S(1)}, bf16[4,272,128]{2,1,0:T(8,128)(2,1)S(1)}, u32[]{:S(2)}, u32[]{:S(2)}) %collective-permute-start.29) | collective-permute-done | bytes 278560 | tf_op jit(solution)/shard_map/ppermute | solution.py:669
  178.5 0.5 collective-permute-start.32
  179.0 0.7 fusion
  180.5 2.8 %shard_map.247 = (f32[288,128]{1,0:T(8,128)}, f32[128,4096]{1,0:T(8,128)}, f32[4096,128]{1,0:T(8,128)}, f32[32,128]{1,0:T(8,128)}) custom-call(s32[6]{0:T(128)S(1)} %copy-done.2, bf16[4,272,128]{2,1,0:T(8,128)(2,1)S(1)} %pad_maximum_fusion.refs_1_, bf16[4,272,128]{2,1,0:T(8,128)(2,1)S(1)} %collective-permute-done.28.refs_2_, ...), custom_call_target="tpu_custom_call" | custom-call | bytes 6586368 | tf_op jit(solution)/shard_map/pallas_call | solution.py:55
  (103 shorter events, 3.7 us)
Async XLA Ops:
  0.6 10.2 %collective-permute-start = (bf16[8,4096]{1,0:T(8,128)(2,1)}, bf16[8,4096]{1,0:T(8,128)(2,1)S(1)}, u32[]{:S(2)}, u32[]{:S(2)}) collective-permute-start(bf16[8,4096]{1,0:T(8,128)(2,1)} %bitcast.32), channel_id=1, source_target_pairs={{0,1},{1,0},{2,3},{3,2},{4,5},{5,4},{6,7},{7,6},{8,9},{9,8},{10,11... | collective-permute-start | bytes 196616 | tf_op jit(solution)/shard_map/ppermute | solution.py:669
  3.2 36.6 %all-to-all-start = ((bf16[32,4,640]{2,1,0:T(4,128)(2,1)}), bf16[32,4,640]{2,1,0:T(4,128)(2,1)S(1)}, u32[]{:S(2)}, u32[]{:S(2)}) async-start(bf16[32,4,640]{2,1,0:T(4,128)(2,1)} %broadcast_in_dim.7), calls=%async_computation | async-start | bytes 327680 | tf_op jit(solution)/shard_map/all_to_all | solution.py:665
  11.7 9.7 %copy-start.13 = (bf16[3,8,4096]{2,1,0:T(8,128)(2,1)}, bf16[3,8,4096]{2,1,0:T(8,128)(2,1)S(1)}, u32[]{:S(2)}) copy-start(bf16[3,8,4096]{2,1,0:T(8,128)(2,1)S(1)} %pad_maximum_fusion.1.refs_5_.refs_3_) | copy-start | bytes 589828
  11.7 9.7 %collective-permute-start.3 = (bf16[3,8,4096]{2,1,0:T(8,128)(2,1)S(1)}, bf16[3,8,4096]{2,1,0:T(8,128)(2,1)S(1)}, u32[]{:S(2)}, u32[]{:S(2)}) collective-permute-start(bf16[3,8,4096]{2,1,0:T(8,128)(2,1)S(1)} %pad_maximum_fusion.1.refs_5_.refs_3_), channel_id=1, source_target_pairs={{0,24},{8,16},{16,8},{24,0},{1,25},{9,17},{17,9},{25,1},{2,26},{10... | collective-permute-start | bytes 589832 | tf_op jit(solution)/shard_map/ppermute | solution.py:669
  14.5 10.5 %collective-permute-start.2 = (bf16[3,8,4096]{2,1,0:T(8,128)(2,1)S(1)}, bf16[3,8,4096]{2,1,0:T(8,128)(2,1)S(1)}, u32[]{:S(2)}, u32[]{:S(2)}) collective-permute-start(bf16[3,8,4096]{2,1,0:T(8,128)(2,1)S(1)} %pad_maximum_fusion.1.refs_5_.refs_3_), channel_id=1, source_target_pairs={{0,16},{8,24},{16,0},{24,8},{1,17},{9,25},{17,1},{25,9},{2,18},{10... | collective-permute-start | bytes 589832 | tf_op jit(solution)/shard_map/ppermute | solution.py:669
  15.0 9.9 %collective-permute-start.1 = (bf16[3,8,4096]{2,1,0:T(8,128)(2,1)S(1)}, bf16[3,8,4096]{2,1,0:T(8,128)(2,1)S(1)}, u32[]{:S(2)}, u32[]{:S(2)}) collective-permute-start(bf16[3,8,4096]{2,1,0:T(8,128)(2,1)S(1)} %pad_maximum_fusion.1.refs_5_.refs_3_), channel_id=1, source_target_pairs={{0,8},{8,0},{16,24},{24,16},{1,9},{9,1},{17,25},{25,17},{2,10},{10... | collective-permute-start | bytes 589832 | tf_op jit(solution)/shard_map/ppermute | solution.py:669
  21.4 3.5 %copy-start.14 = (bf16[3,8,4096]{2,1,0:T(8,128)(2,1)}, bf16[3,8,4096]{2,1,0:T(8,128)(2,1)S(1)}, u32[]{:S(2)}) copy-start(bf16[3,8,4096]{2,1,0:T(8,128)(2,1)S(1)} %collective-permute-done.3.refs_8_.refs_6_) | copy-start | bytes 589828
  33.0 16.3 %collective-permute-start.5 = (bf16[64,384]{1,0:T(8,128)(2,1)}, bf16[64,384]{1,0:T(8,128)(2,1)S(1)}, u32[]{:S(2)}, u32[]{:S(2)}) collective-permute-start(bf16[64,384]{1,0:T(8,128)(2,1)} %get-tuple-element.78), channel_id=1, source_target_pairs={{0,1},{1,5},{2,0},{3,4},{4,3},{5,7},{6,2},{7,6},{8,9},{9,13},{10,8... | collective-permute-start | bytes 147464 | tf_op jit(solution)/shard_map/ppermute | solution.py:706
  33.1 16.2 %collective-permute-start.6 = (bf16[64,384]{1,0:T(8,128)(2,1)}, bf16[64,384]{1,0:T(8,128)(2,1)S(1)}, u32[]{:S(2)}, u32[]{:S(2)}) collective-permute-start(bf16[64,384]{1,0:T(8,128)(2,1)} %get-tuple-element.79), channel_id=1, source_target_pairs={{0,2},{1,6},{2,3},{3,7},{4,0},{5,4},{6,1},{7,5},{8,10},{9,14},{10,... | collective-permute-start | bytes 147464 | tf_op jit(solution)/shard_map/ppermute | solution.py:706
  35.1 14.3 %collective-permute-start.7 = (bf16[64,384]{1,0:T(8,128)(2,1)}, bf16[64,384]{1,0:T(8,128)(2,1)S(1)}, u32[]{:S(2)}, u32[]{:S(2)}) collective-permute-start(bf16[64,384]{1,0:T(8,128)(2,1)} %get-tuple-element.80), channel_id=1, source_target_pairs={{0,3},{1,7},{2,2},{3,6},{4,1},{5,5},{6,0},{7,4},{8,11},{9,15},{10,... | collective-permute-start | bytes 147464 | tf_op jit(solution)/shard_map/ppermute | solution.py:706
  38.3 11.0 %collective-permute-start.4 = (bf16[64,384]{1,0:T(8,128)(2,1)}, bf16[64,384]{1,0:T(8,128)(2,1)S(1)}, u32[]{:S(2)}, u32[]{:S(2)}) collective-permute-start(bf16[64,384]{1,0:T(8,128)(2,1)} %get-tuple-element.74.refs_10_), channel_id=1, source_target_pairs={{0,0},{1,4},{2,1},{3,5},{4,2},{5,6},{6,3},{7,7},{8,8},{9,12},{10,9... | collective-permute-start | bytes 147464 | tf_op jit(solution)/shard_map/ppermute | solution.py:706
  59.4 26.4 %all-to-all-start.1 = ((bf16[32,64,128]{2,1,0:T(8,128)(2,1)}), bf16[32,64,128]{2,1,0:T(8,128)(2,1)S(1)}, u32[]{:S(2)}, u32[]{:S(2)}) async-start(bf16[32,64,128]{2,1,0:T(8,128)(2,1)} %bitcast.27), calls=%async_computation.1 | async-start | bytes 1048576 | tf_op jit(solution)/shard_map/all_to_all | solution.py:747
  65.8 14.8 %copy-start.27 = (bf16[1,4,512]{2,1,0:T(4,128)(2,1)S(1)}, bf16[1,4,512]{2,1,0:T(4,128)(2,1)}, u32[]{:S(2)}) copy-start(bf16[1,4,512]{2,1,0:T(4,128)(2,1)} %param.32) | copy-start | bytes 12292
  65.9 14.9 %copy-start.26 = (bf16[128,32]{0,1:T(8,128)(2,1)S(1)}, bf16[128,32]{0,1:T(8,128)(2,1)}, u32[]{:S(2)}) copy-start(bf16[128,32]{0,1:T(8,128)(2,1)} %param.31) | copy-start | bytes 24580
  65.9 19.9 %copy-start.1 = (s32[6]{0:T(128)S(1)}, s32[6]{0:T(128)}, u32[]{:S(2)}) copy-start(s32[6]{0:T(128)} %stack.45.refs_0_) | copy-start | bytes 76
  65.9 19.9 %copy-start.10 = (bf16[128,128]{1,0:T(8,128)(2,1)S(1)}, bf16[128,128]{1,0:T(8,128)(2,1)}, u32[]{:S(2)}) copy-start(bf16[128,128]{1,0:T(8,128)(2,1)} %get-tuple-element.83.refs_3_.refs_10_) | copy-start | bytes 98308
  65.9 19.9 %copy-start.11 = (f32[8,256,128]{2,1,0:T(8,128)S(1)}, f32[8,256,128]{2,1,0:T(8,128)}, u32[]{:S(2)}) copy-start(f32[8,256,128]{2,1,0:T(8,128)} %get-tuple-element.82.refs_23_) | copy-start | bytes 3145732
  72.4 4.7 %collective-permute-start.8 = (bf16[32,256]{1,0:T(8,128)(2,1)}, bf16[32,256]{1,0:T(8,128)(2,1)S(1)}, u32[]{:S(2)}, u32[]{:S(2)}) collective-permute-start(bf16[32,256]{1,0:T(8,128)(2,1)} %get-tuple-element.85), channel_id=1, source_target_pairs={{0,1},{1,0},{2,3},{3,2},{4,5},{5,4},{6,7},{7,6},{8,9},{9,8},{10,11... | collective-permute-start | bytes 49160 | tf_op jit(solution)/shard_map/ppermute | solution.py:669
  72.7 7.9 %collective-permute-start.9 = (bf16[32,256]{1,0:T(8,128)(2,1)}, bf16[32,256]{1,0:T(8,128)(2,1)S(1)}, u32[]{:S(2)}, u32[]{:S(2)}) collective-permute-start(bf16[32,256]{1,0:T(8,128)(2,1)} %get-tuple-element.86), channel_id=1, source_target_pairs={{0,2},{1,3},{2,0},{3,1},{4,6},{5,7},{6,4},{7,5},{8,10},{9,11},{10,... | collective-permute-start | bytes 49160 | tf_op jit(solution)/shard_map/ppermute | solution.py:669
  74.4 6.5 %collective-permute-start.10 = (bf16[32,256]{1,0:T(8,128)(2,1)}, bf16[32,256]{1,0:T(8,128)(2,1)S(1)}, u32[]{:S(2)}, u32[]{:S(2)}) collective-permute-start(bf16[32,256]{1,0:T(8,128)(2,1)} %get-tuple-element.87), channel_id=1, source_target_pairs={{0,3},{1,2},{2,1},{3,0},{4,7},{5,6},{6,5},{7,4},{8,11},{9,10},{10,... | collective-permute-start | bytes 49160 | tf_op jit(solution)/shard_map/ppermute | solution.py:669
  74.4 7.5 %collective-permute-start.11 = (bf16[32,256]{1,0:T(8,128)(2,1)}, bf16[32,256]{1,0:T(8,128)(2,1)S(1)}, u32[]{:S(2)}, u32[]{:S(2)}) collective-permute-start(bf16[32,256]{1,0:T(8,128)(2,1)} %get-tuple-element.88), channel_id=1, source_target_pairs={{0,4},{1,5},{2,6},{3,7},{4,0},{5,1},{6,2},{7,3},{8,12},{9,13},{10,... | collective-permute-start | bytes 49160 | tf_op jit(solution)/shard_map/ppermute | solution.py:669
  77.0 4.9 %collective-permute-start.12 = (bf16[32,256]{1,0:T(8,128)(2,1)}, bf16[32,256]{1,0:T(8,128)(2,1)S(1)}, u32[]{:S(2)}, u32[]{:S(2)}) collective-permute-start(bf16[32,256]{1,0:T(8,128)(2,1)} %get-tuple-element.89), channel_id=1, source_target_pairs={{0,5},{1,4},{2,7},{3,6},{4,1},{5,0},{6,3},{7,2},{8,13},{9,12},{10,... | collective-permute-start | bytes 49160 | tf_op jit(solution)/shard_map/ppermute | solution.py:669
  77.1 10.4 %copy-start.3 = (bf16[32,256]{1,0:T(8,128)(2,1)}, bf16[32,256]{1,0:T(8,128)(2,1)S(1)}, u32[]{:S(2)}) copy-start(bf16[32,256]{1,0:T(8,128)(2,1)S(1)} %collective-permute-done.8.refs_6_.refs_3_.refs_9_) | copy-start | bytes 49156
  77.1 5.8 %collective-permute-start.13 = (bf16[32,256]{1,0:T(8,128)(2,1)}, bf16[32,256]{1,0:T(8,128)(2,1)S(1)}, u32[]{:S(2)}, u32[]{:S(2)}) collective-permute-start(bf16[32,256]{1,0:T(8,128)(2,1)} %get-tuple-element.90), channel_id=1, source_target_pairs={{0,6},{1,7},{2,4},{3,5},{4,2},{5,3},{6,0},{7,1},{8,14},{9,15},{10,... | collective-permute-start | bytes 49160 | tf_op jit(solution)/shard_map/ppermute | solution.py:669
  80.6 6.8 %copy-start.4 = (bf16[32,256]{1,0:T(8,128)(2,1)}, bf16[32,256]{1,0:T(8,128)(2,1)S(1)}, u32[]{:S(2)}) copy-start(bf16[32,256]{1,0:T(8,128)(2,1)S(1)} %collective-permute-done.9.refs_7_.refs_4_.refs_10_) | copy-start | bytes 49156
  80.6 5.2 %collective-permute-start.14 = (bf16[32,256]{1,0:T(8,128)(2,1)}, bf16[32,256]{1,0:T(8,128)(2,1)S(1)}, u32[]{:S(2)}, u32[]{:S(2)}) collective-permute-start(bf16[32,256]{1,0:T(8,128)(2,1)} %get-tuple-element.91), channel_id=1, source_target_pairs={{0,7},{1,6},{2,5},{3,4},{4,3},{5,2},{6,1},{7,0},{8,15},{9,14},{10,... | collective-permute-start | bytes 49160 | tf_op jit(solution)/shard_map/ppermute | solution.py:669
  80.9 6.6 %copy-start.5 = (bf16[32,256]{1,0:T(8,128)(2,1)}, bf16[32,256]{1,0:T(8,128)(2,1)S(1)}, u32[]{:S(2)}) copy-start(bf16[32,256]{1,0:T(8,128)(2,1)S(1)} %collective-permute-done.10.refs_8_.refs_5_.refs_11_) | copy-start | bytes 49156
  81.9 5.6 %copy-start.6 = (bf16[32,256]{1,0:T(8,128)(2,1)}, bf16[32,256]{1,0:T(8,128)(2,1)S(1)}, u32[]{:S(2)}) copy-start(bf16[32,256]{1,0:T(8,128)(2,1)S(1)} %collective-permute-done.11.refs_9_.refs_6_.refs_12_) | copy-start | bytes 49156
  81.9 5.6 %copy-start.7 = (bf16[32,256]{1,0:T(8,128)(2,1)}, bf16[32,256]{1,0:T(8,128)(2,1)S(1)}, u32[]{:S(2)}) copy-start(bf16[32,256]{1,0:T(8,128)(2,1)S(1)} %collective-permute-done.12.refs_10_.refs_7_.refs_13_) | copy-start | bytes 49156
  82.9 4.6 %copy-start.8 = (bf16[32,256]{1,0:T(8,128)(2,1)}, bf16[32,256]{1,0:T(8,128)(2,1)S(1)}, u32[]{:S(2)}) copy-start(bf16[32,256]{1,0:T(8,128)(2,1)S(1)} %collective-permute-done.13.refs_11_.refs_8_.refs_14_) | copy-start | bytes 49156
  85.8 1.7 copy-start.9
  87.5 8.8 %copy-start.12 = (f32[32,128]{1,0:T(8,128)}, f32[32,128]{1,0:T(8,128)S(1)}, u32[]{:S(2)}) copy-start(f32[32,128]{1,0:T(8,128)S(1)} %get-tuple-element.103.refs_14_) | copy-start | bytes 49156
  87.5 19.1 %all-to-all-start.2 = ((bf16[32,64,128]{2,1,0:T(8,128)(2,1)}), bf16[32,64,128]{2,1,0:T(8,128)(2,1)S(1)}, u32[]{:S(2)}, u32[]{:S(2)}) async-start(bf16[32,64,128]{2,1,0:T(8,128)(2,1)} %get-tuple-element.94.refs_10_.refs_17_), calls=%async_computation.2 | async-start | bytes 1048576 | tf_op jit(solution)/shard_map/all_to_all | solution.py:767
  96.3 7.5 %collective-permute-start.15 = (bf16[8,4096]{1,0:T(8,128)(2,1)}, bf16[8,4096]{1,0:T(8,128)(2,1)S(1)}, u32[]{:S(2)}, u32[]{:S(2)}) collective-permute-start(bf16[8,4096]{1,0:T(8,128)(2,1)} %get-tuple-element.96), channel_id=1, source_target_pairs={{0,8},{8,0},{16,24},{24,16},{1,9},{9,1},{17,25},{25,17},{2,10},{10... | collective-permute-start | bytes 196616 | tf_op jit(solution)/shard_map/ppermute | solution.py:669
  98.0 5.9 %collective-permute-start.16 = (bf16[8,4096]{1,0:T(8,128)(2,1)}, bf16[8,4096]{1,0:T(8,128)(2,1)S(1)}, u32[]{:S(2)}, u32[]{:S(2)}) collective-permute-start(bf16[8,4096]{1,0:T(8,128)(2,1)} %get-tuple-element.97), channel_id=1, source_target_pairs={{0,16},{8,24},{16,0},{24,8},{1,17},{9,25},{17,1},{25,9},{2,18},{10... | collective-permute-start | bytes 196616 | tf_op jit(solution)/shard_map/ppermute | solution.py:669
  99.4 5.7 %collective-permute-start.17 = (bf16[8,4096]{1,0:T(8,128)(2,1)}, bf16[8,4096]{1,0:T(8,128)(2,1)S(1)}, u32[]{:S(2)}, u32[]{:S(2)}) collective-permute-start(bf16[8,4096]{1,0:T(8,128)(2,1)} %get-tuple-element.98), channel_id=1, source_target_pairs={{0,24},{8,16},{16,8},{24,0},{1,25},{9,17},{17,9},{25,1},{2,26},{10... | collective-permute-start | bytes 196616 | tf_op jit(solution)/shard_map/ppermute | solution.py:669
  103.8 2.8 %copy-start.20 = (bf16[8,4096]{1,0:T(8,128)(2,1)}, bf16[8,4096]{1,0:T(8,128)(2,1)S(1)}, u32[]{:S(2)}) copy-start(bf16[8,4096]{1,0:T(8,128)(2,1)S(1)} %collective-permute-done.15.refs_32_) | copy-start | bytes 196612
  103.9 2.8 %copy-start.22 = (bf16[8,4096]{1,0:T(8,128)(2,1)}, bf16[8,4096]{1,0:T(8,128)(2,1)S(1)}, u32[]{:S(2)}) copy-start(bf16[8,4096]{1,0:T(8,128)(2,1)S(1)} %collective-permute-done.16.refs_33_) | copy-start | bytes 196612
  105.1 1.5 copy-start.24
  106.6 0.8 copy-start.17
  130.3 3.0 %collective-permute-start.18 = (bf16[4,4,272,128]{3,2,1,0:T(8,128)(2,1)}, bf16[4,4,272,128]{3,2,1,0:T(8,128)(2,1)S(1)}, u32[]{:S(2)}, u32[]{:S(2)}) collective-permute-start(bf16[4,4,272,128]{3,2,1,0:T(8,128)(2,1)} %get-tuple-element.117), channel_id=1, source_target_pairs={{0,1},{1,0},{2,3},{3,2},{4,5},{5,4},{6,7},{7,6},{8,9},{9,8},{10,11... | collective-permute-start | bytes 3342344 | tf_op jit(solution)/shard_map/ppermute | solution.py:669
  133.3 1.2 copy-start
  134.6 44.5 %copy-start.18 = (bf16[1,8,4096]{2,1,0:T(8,128)(2,1)S(1)}, bf16[1,8,4096]{2,1,0:T(8,128)(2,1)}, u32[]{:S(2)}) copy-start(bf16[1,8,4096]{2,1,0:T(8,128)(2,1)} %param.20) | copy-start | bytes 196612
  134.6 44.5 %copy-start.19 = (bf16[8,4096]{1,0:T(8,128)(2,1)S(1)}, bf16[8,4096]{1,0:T(8,128)(2,1)}, u32[]{:S(2)}) copy-start(bf16[8,4096]{1,0:T(8,128)(2,1)} %get-tuple-element.95.refs_16_) | copy-start | bytes 196612
  134.6 44.5 %copy-start.21 = (bf16[8,4096]{1,0:T(8,128)(2,1)S(1)}, bf16[8,4096]{1,0:T(8,128)(2,1)}, u32[]{:S(2)}) copy-start(bf16[8,4096]{1,0:T(8,128)(2,1)} %copy-done.20) | copy-start | bytes 196612
  134.6 44.5 %copy-start.23 = (bf16[8,4096]{1,0:T(8,128)(2,1)S(1)}, bf16[8,4096]{1,0:T(8,128)(2,1)}, u32[]{:S(2)}) copy-start(bf16[8,4096]{1,0:T(8,128)(2,1)} %copy-done.22) | copy-start | bytes 196612
  134.6 44.5 %copy-start.25 = (bf16[8,4096]{1,0:T(8,128)(2,1)S(1)}, bf16[8,4096]{1,0:T(8,128)(2,1)}, u32[]{:S(2)}) copy-start(bf16[8,4096]{1,0:T(8,128)(2,1)} %copy-done.24) | copy-start | bytes 196612
  134.6 45.9 %copy-start.2 = (s32[6]{0:T(128)S(1)}, s32[6]{0:T(128)}, u32[]{:S(2)}) copy-start(s32[6]{0:T(128)} %stack.45.refs_0_) | copy-start | bytes 76
  134.9 9.6 %collective-permute-start.19 = (bf16[4,272,128]{2,1,0:T(8,128)(2,1)S(1)}, bf16[4,272,128]{2,1,0:T(8,128)(2,1)S(1)}, u32[]{:S(2)}, u32[]{:S(2)}) collective-permute-start(bf16[4,272,128]{2,1,0:T(8,128)(2,1)S(1)} %get-tuple-element.119), channel_id=1, source_target_pairs={{0,8},{8,0},{16,24},{24,16},{1,9},{9,1},{17,25},{25,17},{2,10},{10... | collective-permute-start | bytes 835592 | tf_op jit(solution)/shard_map/ppermute | solution.py:669
  135.1 9.3 %collective-permute-start.20 = (bf16[4,272,128]{2,1,0:T(8,128)(2,1)S(1)}, bf16[4,272,128]{2,1,0:T(8,128)(2,1)S(1)}, u32[]{:S(2)}, u32[]{:S(2)}) collective-permute-start(bf16[4,272,128]{2,1,0:T(8,128)(2,1)S(1)} %get-tuple-element.120), channel_id=1, source_target_pairs={{0,16},{8,24},{16,0},{24,8},{1,17},{9,25},{17,1},{25,9},{2,18},{10... | collective-permute-start | bytes 835592 | tf_op jit(solution)/shard_map/ppermute | solution.py:669
  136.6 13.0 %collective-permute-start.21 = (bf16[4,272,128]{2,1,0:T(8,128)(2,1)S(1)}, bf16[4,272,128]{2,1,0:T(8,128)(2,1)S(1)}, u32[]{:S(2)}, u32[]{:S(2)}) collective-permute-start(bf16[4,272,128]{2,1,0:T(8,128)(2,1)S(1)} %get-tuple-element.121), channel_id=1, source_target_pairs={{0,24},{8,16},{16,8},{24,0},{1,25},{9,17},{17,9},{25,1},{2,26},{10... | collective-permute-start | bytes 835592 | tf_op jit(solution)/shard_map/ppermute | solution.py:669
  149.8 4.7 %collective-permute-start.22 = (bf16[272,128]{1,0:T(8,128)(2,1)S(1)}, bf16[272,128]{1,0:T(8,128)(2,1)S(1)}, u32[]{:S(2)}, u32[]{:S(2)}) collective-permute-start(bf16[272,128]{1,0:T(8,128)(2,1)S(1)} %get-tuple-element.123), channel_id=1, source_target_pairs={{0,2},{1,3},{2,0},{3,1},{4,6},{5,7},{6,4},{7,5},{8,10},{9,11},{10,... | collective-permute-start | bytes 208904 | tf_op jit(solution)/shard_map/ppermute | solution.py:669
  150.9 6.9 %collective-permute-start.23 = (bf16[272,128]{1,0:T(8,128)(2,1)S(1)}, bf16[272,128]{1,0:T(8,128)(2,1)S(1)}, u32[]{:S(2)}, u32[]{:S(2)}) collective-permute-start(bf16[272,128]{1,0:T(8,128)(2,1)S(1)} %get-tuple-element.124), channel_id=1, source_target_pairs={{0,4},{1,5},{2,6},{3,7},{4,0},{5,1},{6,2},{7,3},{8,12},{9,13},{10,... | collective-permute-start | bytes 208904 | tf_op jit(solution)/shard_map/ppermute | solution.py:669
  152.6 6.2 %collective-permute-start.24 = (bf16[272,128]{1,0:T(8,128)(2,1)S(1)}, bf16[272,128]{1,0:T(8,128)(2,1)S(1)}, u32[]{:S(2)}, u32[]{:S(2)}) collective-permute-start(bf16[272,128]{1,0:T(8,128)(2,1)S(1)} %get-tuple-element.125), channel_id=1, source_target_pairs={{0,6},{1,7},{2,4},{3,5},{4,2},{5,3},{6,0},{7,1},{8,14},{9,15},{10,... | collective-permute-start | bytes 208904 | tf_op jit(solution)/shard_map/ppermute | solution.py:669
  158.8 6.3 %collective-permute-start.27 = (bf16[272,128]{1,0:T(8,128)(2,1)S(1)}, bf16[272,128]{1,0:T(8,128)(2,1)S(1)}, u32[]{:S(2)}, u32[]{:S(2)}) collective-permute-start(bf16[272,128]{1,0:T(8,128)(2,1)S(1)} %shard_map.246), channel_id=1, source_target_pairs={{0,6},{1,7},{2,4},{3,5},{4,2},{5,3},{6,0},{7,1},{8,14},{9,15},{10,... | collective-permute-start | bytes 208904 | tf_op jit(solution)/shard_map/ppermute | solution.py:669
  160.6 6.1 %collective-permute-start.26 = (bf16[272,128]{1,0:T(8,128)(2,1)S(1)}, bf16[272,128]{1,0:T(8,128)(2,1)S(1)}, u32[]{:S(2)}, u32[]{:S(2)}) collective-permute-start(bf16[272,128]{1,0:T(8,128)(2,1)S(1)} %shard_map.246), channel_id=1, source_target_pairs={{0,4},{1,5},{2,6},{3,7},{4,0},{5,1},{6,2},{7,3},{8,12},{9,13},{10,... | collective-permute-start | bytes 208904 | tf_op jit(solution)/shard_map/ppermute | solution.py:669
  161.8 4.9 %collective-permute-start.25 = (bf16[272,128]{1,0:T(8,128)(2,1)S(1)}, bf16[272,128]{1,0:T(8,128)(2,1)S(1)}, u32[]{:S(2)}, u32[]{:S(2)}) collective-permute-start(bf16[272,128]{1,0:T(8,128)(2,1)S(1)} %shard_map.246), channel_id=1, source_target_pairs={{0,2},{1,3},{2,0},{3,1},{4,6},{5,7},{6,4},{7,5},{8,10},{9,11},{10,... | collective-permute-start | bytes 208904 | tf_op jit(solution)/shard_map/ppermute | solution.py:669
  166.7 9.8 %collective-permute-start.30 = (bf16[4,272,128]{2,1,0:T(8,128)(2,1)S(1)}, bf16[4,272,128]{2,1,0:T(8,128)(2,1)S(1)}, u32[]{:S(2)}, u32[]{:S(2)}) collective-permute-start(bf16[4,272,128]{2,1,0:T(8,128)(2,1)S(1)} %pad_maximum_fusion.refs_1_), channel_id=1, source_target_pairs={{0,24},{8,16},{16,8},{24,0},{1,25},{9,17},{17,9},{25,1},{2,26},{10... | collective-permute-start | bytes 835592 | tf_op jit(solution)/shard_map/ppermute | solution.py:669
  168.4 10.1 %collective-permute-start.29 = (bf16[4,272,128]{2,1,0:T(8,128)(2,1)S(1)}, bf16[4,272,128]{2,1,0:T(8,128)(2,1)S(1)}, u32[]{:S(2)}, u32[]{:S(2)}) collective-permute-start(bf16[4,272,128]{2,1,0:T(8,128)(2,1)S(1)} %pad_maximum_fusion.refs_1_), channel_id=1, source_target_pairs={{0,16},{8,24},{16,0},{24,8},{1,17},{9,25},{17,1},{25,9},{2,18},{10... | collective-permute-start | bytes 835592 | tf_op jit(solution)/shard_map/ppermute | solution.py:669
  169.5 9.1 %collective-permute-start.28 = (bf16[4,272,128]{2,1,0:T(8,128)(2,1)S(1)}, bf16[4,272,128]{2,1,0:T(8,128)(2,1)S(1)}, u32[]{:S(2)}, u32[]{:S(2)}) collective-permute-start(bf16[4,272,128]{2,1,0:T(8,128)(2,1)S(1)} %pad_maximum_fusion.refs_1_), channel_id=1, source_target_pairs={{0,8},{8,0},{16,24},{24,16},{1,9},{9,1},{17,25},{25,17},{2,10},{10... | collective-permute-start | bytes 835592 | tf_op jit(solution)/shard_map/ppermute | solution.py:669
  170.9 8.8 %collective-permute-start.31 = (bf16[4,272,128]{2,1,0:T(8,128)(2,1)S(1)}, bf16[4,272,128]{2,1,0:T(8,128)(2,1)S(1)}, u32[]{:S(2)}, u32[]{:S(2)}) collective-permute-start(bf16[4,272,128]{2,1,0:T(8,128)(2,1)S(1)} %pad_maximum_fusion.refs_1_), channel_id=1, source_target_pairs={{0,1},{1,0},{2,3},{3,2},{4,5},{5,4},{6,7},{7,6},{8,9},{9,8},{10,11... | collective-permute-start | bytes 835592 | tf_op jit(solution)/shard_map/ppermute | solution.py:669
  176.5 3.2 %collective-permute-start.34 = (bf16[4,272,128]{2,1,0:T(8,128)(2,1)S(1)}, bf16[4,272,128]{2,1,0:T(8,128)(2,1)S(1)}, u32[]{:S(2)}, u32[]{:S(2)}) collective-permute-start(bf16[4,272,128]{2,1,0:T(8,128)(2,1)S(1)} %collective-permute-done.30.refs_4_), channel_id=1, source_target_pairs={{0,1},{1,0},{2,3},{3,2},{4,5},{5,4},{6,7},{7,6},{8,9},{9,8},{10,11... | collective-permute-start | bytes 835592 | tf_op jit(solution)/shard_map/ppermute | solution.py:669
  178.5 1.6 collective-permute-start.33
  178.5 2.0 %collective-permute-start.32 = (bf16[4,272,128]{2,1,0:T(8,128)(2,1)S(1)}, bf16[4,272,128]{2,1,0:T(8,128)(2,1)S(1)}, u32[]{:S(2)}, u32[]{:S(2)}) collective-permute-start(bf16[4,272,128]{2,1,0:T(8,128)(2,1)S(1)} %collective-permute-done.28.refs_2_), channel_id=1, source_target_pairs={{0,1},{1,0},{2,3},{3,2},{4,5},{5,4},{6,7},{7,6},{8,9},{9,8},{10,11... | collective-permute-start | bytes 835592 | tf_op jit(solution)/shard_map/ppermute | solution.py:669
  (6 other events, 3.9 us)
where the time goes:
time: 184 us; the launch traced here: 183 us
  Pallas kernels  73.8 us (40%)
  starting transfers between devices  55.8 us (30%)
  waiting for transfers between devices  41.6 us (23%)
  local copies, waits for them, and re-layouts  7.78 us (4%)
  other arithmetic  2.47 us (1%)
    pallas_call x9, Pallas kernels, call(): pl.pallas_call(lambda *refs: kernel(*refs[:count], *refs[skip:]), out_sha...  66.1 us
    ppermute x31, waiting for transfers between devices, shards(): lax.ppermute(values, axis, [(i, i ^ by) for i in range(row_groups if axis...  40.1 us
    ppermute x31, starting transfers between devices, shards(): lax.ppermute(values, axis, [(i, i ^ by) for i in range(row_groups if axis...  32.5 us
    pallas_call x1, Pallas kernels, image_rows(): pl.pallas_call(lambda *refs: image_kernel(*sizes, *refs), out_shape=[jax....  7.31 us
    all_to_all x1, starting transfers between devices, spread_over(): lax.all_to_all(jnp.broadcast_to(values[None], (count,) + values.shape), a...  6.96 us
    ppermute x4, starting transfers between devices, shards(): lax.ppermute(values, 'sy', [(2 * z + c, c * pairs + (z ^ k)) for z in ran...  6.76 us
    all_to_all x1, starting transfers between devices, shards(): parts = lax.all_to_all(part.reshape(devices, own_rows, up_chan), axes, 0, 0)  6.46 us
  transfers between devices with their start and end apart: 38, of which 18 were waited for; matrix products, arithmetic and copies ran while one was open for 4% of the time, Pallas kernels for 20%

commit v1 on v0

--- a/solution.py
+++ b/solution.py
@@ -75,21 +75,41 @@
     return jnp.concatenate([gain[r : r + 1, :].astype(F32) for r in range(gain.shape[0])], axis=1)
 
 
-def weights_kernel(
-    place, gain, w_conv, w_down_far, wq_far, wk_far, wv_far, w_up_far, wo_far,
-    proj, proj_t, mapped, u, gram, z, conv_t,
-    w_down, wq, wk, wv, w_up, wo, sems,
-):
+def pick(rows, total, spot):
+    return (iota((total, rows), 0) == iota((total, rows), 1) + spot).astype(BF16)
+
+
+def gathered(parts, group):
+    rows = parts[0].shape[0]
+    total = rows * len(parts)
+    return sum(dot(pick(rows, total, (group ^ k) * rows), part[...]) for k, part in enumerate(parts))
+
+
+def front_kernel(count, repeat, place, gain, w_conv, w_down_far, wq_far, wk_far, wv_far, w_up_far, wo_far, *refs):
+    parts = refs[:count]
+    proj, proj_t, mapped, u, gram, z, conv_t = refs[count : count + 7]
+    outs = refs[count + 7 : -10]
+    w_down, wq, wk, wv, w_up, wo, weights, normed, sums, sems = refs[-10:]
+    chunks, _, deep, wide = weights.shape
     cols = pl.ds(pl.multiple_of(place[0] * HD, HD), HD)
+    half = pl.ds(pl.multiple_of(place[4] * wide, wide), wide)
     moves = fetch(
         [(w_down_far, w_down), (wq_far.at[:, cols], wq), (wk_far.at[:, cols], wk), (wv_far.at[:, cols], wv),
-         (w_up_far, w_up), (wo_far.at[cols, :], wo)],
+         (w_up_far, w_up), (wo_far.at[cols, :], wo)]
+        + [(far.at[c * deep : (c + 1) * deep, half], weights.at[c, n])
+           for c in range(chunks) for n, far in enumerate((wq_far, wk_far, wv_far))],
         sems,
     )
     conv_t[...] = flip(w_conv[...])
+    rows = normed.shape[0] // 2
+    row = whole_row(gain)
+    for r in range(2):
+        x = gathered([part.at[r] for part in parts], place[2])
+        inverse = lax.rsqrt(jnp.mean(x * x, axis=-1, keepdims=True) + EPSILON)
+        normed[r * rows : (r + 1) * rows, :] = (x * inverse * row).astype(BF16)
     moves[0].wait()
     down = w_down[...]
-    scaled = (down.astype(F32) * whole_row(gain)).astype(BF16)
+    scaled = (down.astype(F32) * row).astype(BF16)
     gram[...] = dot_nt(down, down).astype(BF16)
     for n, w in enumerate((wq, wk, wv)):
         cols = slice(n * HD, (n + 1) * HD)
@@ -104,40 +124,10 @@
     z[...] = dot(down, w_up[...]).astype(BF16)
     moves[5].wait()
     u[...] = dot(wo[...], w_up[...]).astype(BF16)
-
-
-def pick(rows, total, spot):
-    return (iota((total, rows), 0) == iota((total, rows), 1) + spot).astype(BF16)
-
-
-def gathered(parts, group):
-    rows = parts[0].shape[0]
-    total = rows * len(parts)
-    return sum(dot(pick(rows, total, (group ^ k) * rows), part[...]) for k, part in enumerate(parts))
-
-
-def text_kernel(count, repeat, place, *refs):
-    gain, wq_far, wk_far, wv_far = refs[:4]
-    parts = refs[4 : 4 + count]
-    outs = refs[4 + count : -4]
-    weights, normed, sums, sems = refs[-4:]
-    chunks, _, deep, wide = weights.shape
-    cols = pl.ds(pl.multiple_of(place[4] * wide, wide), wide)
-    moves = fetch(
-        [(far.at[c * deep : (c + 1) * deep, cols], weights.at[c, n])
-         for c in range(chunks) for n, far in enumerate((wq_far, wk_far, wv_far))],
-        sems,
-    )
-    rows = normed.shape[0] // 2
-    row = whole_row(gain)
-    for r in range(2):
-        x = gathered([part.at[r] for part in parts], place[2])
-        inverse = lax.rsqrt(jnp.mean(x * x, axis=-1, keepdims=True) + EPSILON)
-        normed[r * rows : (r + 1) * rows, :] = (x * inverse * row).astype(BF16)
     for c in range(chunks):
         here = normed[:, c * deep : (c + 1) * deep]
         for n in range(3):
-            moves[3 * c + n].wait()
+            moves[6 + 3 * c + n].wait()
             term = dot(here, weights[c, n])
             sums[n] = term if c == 0 else sums[n] + term
     for k, out in enumerate(outs):
@@ -152,14 +142,14 @@
     wo, total, sems = refs[-3:]
     groups, deep, _ = wo.shape
     moves = fetch([(wo_far.at[g * deep : (g + 1) * deep, :], wo.at[g]) for g in range(groups)], sems)
-    grad_t = gathered([part.at[2] for part in parts], place[2]).T.astype(BF16)
+    grad = gathered([part.at[2] for part in parts], place[2]).astype(BF16)
     for g in range(groups):
         moves[g].wait()
-        total[g * deep : (g + 1) * deep, :] = dot(wo[g], grad_t)
+        total[:, g * deep : (g + 1) * deep] = dot_nt(grad, wo[g])
     for k, out in enumerate(outs):
         peer = place[5] ^ k
         rows = out.shape[0]
-        out[:, :HD] = total[pl.ds(pl.multiple_of(peer // repeat * HD, HD), HD), :].T.astype(BF16)
+        out[:, :HD] = total[:, pl.ds(pl.multiple_of(peer // repeat * HD, HD), HD)].astype(BF16)
         out[:, HD:] = mix[pl.ds(pl.multiple_of(peer * rows, rows), rows), :]
 
 
@@ -494,17 +484,18 @@
      wq_far, wk_far, wv_far, wo_far, w_up_far, w_down_far,
      keep, send,
      pieces, dq, dk, dv, cross_sum, small_sum, scores, pulls, probs, slopes,
-     keys, values, qt, kt, q_img, mix_t, dk_text, dv_text, pre_down, act_t, patch_t, wq, wk, wv, wo, w_up, w_down,
+     keys, values, qt, kt, q_img, mix_t, dk_text, dv_text, pre_down, act_t, patch_t, w_cols, w_rows, w_up,
      sems) = refs
     text_total = k_txt.shape[0]
-    width = w_down.shape[1]
+    width = w_up.shape[0]
     cols = pl.ds(pl.multiple_of(place[0] * HD, HD), HD)
     moves = fetch(
         [(k_img_far, keys.at[text_total:, :]), (v_img_far, values.at[text_total:, :]), (qt_far, qt),
          (kt_far, kt.at[:, text_total:]), (q_img_far, q_img), (mix_t_far, mix_t), (dk_far, dk_text), (dv_far, dv_text),
          (pre_down_far, pre_down), (act_t_far, act_t), (patch_t_far, patch_t),
-         (wq_far.at[:, cols], wq), (wk_far.at[:, cols], wk), (wv_far.at[:, cols], wv), (wo_far.at[cols, :], wo),
-         (w_up_far, w_up), (w_down_far, w_down)],
+         (wq_far.at[:, cols], w_cols.at[:, :HD]), (wk_far.at[:, cols], w_cols.at[:, HD : 2 * HD]),
+         (wv_far.at[:, cols], w_cols.at[:, 2 * HD :]), (wo_far.at[cols, :], w_rows.at[:HD, :]),
+         (w_up_far, w_up), (w_down_far, w_rows.at[HD:, :])],
         sems,
     )
     cross_sum[...] = jnp.zeros_like(cross_sum)
@@ -600,15 +591,18 @@
     _, groups, pairs, rows, _ = pieces.shape
     own = width // (2 * groups * pairs)
     few = rows - 2 * own
-    for at in range(0, width, HD):
-        cols = slice(at, at + HD)
-        down = dot_nt(spread[:, :HD], wq[cols, :]) + dot_nt(spread[:, HD : 2 * HD], wk[cols, :])
-        down = (down + dot_nt(spread[:, 2 * HD :], wv[cols, :])) * gain[at // HD : at // HD + 1, :].astype(F32)
-        down = (down - dot(pull, w_down[:, cols]) + dot_nt(inner, w_up[cols, :])).astype(BF16)
-        up = (dot(cross, wo[:, cols]) + dot(inner_t, w_down[:, cols])).T.astype(BF16)
-        for part in range(0, HD, own):
-            put_piece(place, pieces, (at + part) // own, slice(0, own), up[part : part + own])
-            put_piece(place, pieces, (at + part) // own, slice(own, 2 * own), down[part : part + own])
+    both_t = jnp.concatenate([cross, inner_t], axis=1)
+    for at in range(0, width, 2 * HD):
+        cols = slice(at, at + 2 * HD)
+        scale = whole_row(gain[at // HD : at // HD + 2, :])
+        down = dot_nt(spread, w_cols[cols, :]) * scale
+        down = (down - dot(pull, w_rows[HD:, cols]) + dot_nt(inner, w_up[cols, :])).astype(BF16)
+        up = dot(both_t, w_rows[:, cols]).T.astype(BF16)
+        for part in range(0, 2 * HD, own):
+            number = (at + part) // own
+            tile = part // HD * HD
+            put_piece(place, pieces, number, slice(0, own), up[part : part + own])
+            put_piece(place, pieces, number, slice(own, 2 * own), down[part - tile : part - tile + own, tile : tile + HD])
     for number in range(2 * groups * pairs):
         put_piece(place, pieces, number, slice(2 * own, rows), small_sum[number * few : (number + 1) * few, :].astype(BF16))
     for move in fetch([(pieces.at[0], keep), (pieces.at[1], send)], sems):
@@ -670,6 +664,7 @@
         values, axis, [(i, i ^ by) for i in range(row_groups if axis == "sx" else blocks)]
     )
     trio = jnp.stack([text_local, hop(text_local, "sy", 1), text_grad[0]])
+    packed, trio = lax.optimization_barrier((packed, trio))
     text_parts = [trio] + [hop(trio, "sx", k) for k in range(1, row_groups)]
     side = spread_over(packed, axes, devices)
 
@@ -680,27 +675,21 @@
     vmem = pltpu.VMEM
     dma = lambda count: pltpu.SemaphoreType.DMA((count,))
     bf = lambda *shape: small(shape, BF16)
-    proj, proj_t, mapped, u, gram, z, conv_t = call(
-        weights_kernel, head,
-        [(gain, None), (w_down_conv, None)]
-        + [(a, pl.ANY) for a in (w_down_proj, w_query, w_key, w_value, w_up_proj, w_out)],
-        [bf(down_chan, 3 * HD), bf(3 * HD, down_chan), bf(down_chan, 5 * HD), bf(HD, up_chan),
-         bf(down_chan, down_chan), bf(down_chan, up_chan), bf(down_chan, taps)],
-        [vmem((down_chan, width), BF16)] + [vmem((width, HD), BF16)] * 3
-        + [vmem((width, up_chan), BF16), vmem((HD, width), BF16), dma(6)],
-        flops=4_000_000_000,
-    )
     both = 2 * text_block
     chunks = 8
     wide = heads_here * HD // 2
-    text_here = call(
-        lambda *refs: text_kernel(row_groups, repeat, *refs), head,
-        [(gain, None)] + [(a, pl.ANY) for a in (w_query, w_key, w_value)] + [(a, None) for a in text_parts],
-        [bf(both, 3 * HD)] * pairs,
-        [vmem((chunks, 3, width // chunks, wide), BF16), vmem((both, width), BF16), vmem((3, both, wide), F32),
-         dma(3 * chunks)],
-        flops=6 * both * width * wide,
-        after=[proj],
+    proj, proj_t, mapped, u, gram, z, conv_t, *text_here = call(
+        lambda *refs: front_kernel(row_groups, repeat, *refs), head,
+        [(gain, None), (w_down_conv, None)]
+        + [(a, pl.ANY) for a in (w_down_proj, w_query, w_key, w_value, w_up_proj, w_out)]
+        + [(a, None) for a in text_parts],
+        [bf(down_chan, 3 * HD), bf(3 * HD, down_chan), bf(down_chan, 5 * HD), bf(HD, up_chan),
+         bf(down_chan, down_chan), bf(down_chan, up_chan), bf(down_chan, taps)] + [bf(both, 3 * HD)] * pairs,
+        [vmem((down_chan, width), BF16)] + [vmem((width, HD), BF16)] * 3
+        + [vmem((width, up_chan), BF16), vmem((HD, width), BF16),
+           vmem((chunks, 3, width // chunks, wide), BF16), vmem((both, width), BF16), vmem((3, both, wide), F32),
+           dma(6 + 3 * chunks)],
+        flops=4_000_000_000 + 6 * both * width * wide,
     )
     texts = [
         lax.ppermute(values, "sy", [(2 * z + c, c * pairs + (z ^ k)) for z in range(pairs) for c in range(2)])
@@ -750,7 +739,7 @@
         lambda *refs: text_grad_kernel(row_groups, repeat, *refs), head,
         [(w_out, pl.ANY), (mix_txt, None)] + [(a, None) for a in text_parts],
         [bf(text_block, 2 * HD)] * blocks,
-        wo_room + [vmem((heads_here * HD, text_block), F32), dma(4)],
+        wo_room + [vmem((text_block, heads_here * HD), F32), dma(4)],
         flops=2 * text_block * width * heads_here * HD,
         after=[part],
     )
@@ -823,8 +812,7 @@
         + strip_room(2, seq)
         + [vmem((seq, HD), BF16)] * 2 + [vmem(qt.shape, BF16), vmem((HD, seq), BF16)]
         + [vmem(a.shape, a.dtype) for a in (q_img, mix_t, dk, dv, pre_down, act_t, patch_t)]
-        + [vmem((width, HD), BF16)] * 3
-        + [vmem((HD, width), BF16), vmem(w_up_proj.shape, BF16), vmem(w_down_proj.shape, BF16),
+        + [vmem((width, 3 * HD), BF16), vmem((HD + down_chan, width), BF16), vmem(w_up_proj.shape, BF16),
            pltpu.SemaphoreType.DMA((len(far_arrays),))],
         flops=30_000_000_000,
         after=mixed[1:],

time: 184 us -> 179 us (0.973)
  Pallas kernels: 73.8 us -> 70.2 us
    pallas_call x9 -> x8, Pallas kernels: 66.1 us -> 62.5 us  [call(): pl.pallas_call(lambda *refs: kernel(*refs[:count], *refs[skip:]), out_sha...]
  transfers between devices with their start and end apart: 38 -> 38, of which waited for: 18 -> 19; matrix products, arithmetic and copies ran while one was open for 4% -> 3% of each run, Pallas kernels for 20% -> 20%
where the time goes in v1:
time: 179 us; the launch traced here: 178 us
  Pallas kernels  70.2 us (39%)
  starting transfers between devices  56.3 us (31%)
  waiting for transfers between devices  39.9 us (22%)
  local copies, waits for them, and re-layouts  7.66 us (4%)
  other arithmetic  2.41 us (1%)
    pallas_call x8, Pallas kernels, call(): pl.pallas_call(lambda *refs: kernel(*refs[:count], *refs[skip:]), out_sha...  62.5 us
    ppermute x31, waiting for transfers between devices, shards(): lax.ppermute(values, axis, [(i, i ^ by) for i in range(row_groups if axis...  38.4 us
    ppermute x31, starting transfers between devices, shards(): lax.ppermute(values, axis, [(i, i ^ by) for i in range(row_groups if axis...  33.2 us
    ppermute x4, starting transfers between devices, shards(): lax.ppermute(values, 'sy', [(2 * z + c, c * pairs + (z ^ k)) for z in ran...  7.4 us
    pallas_call x1, Pallas kernels, image_rows(): pl.pallas_call(lambda *refs: image_kernel(*sizes, *refs), out_shape=[jax....  7.31 us
    all_to_all x1, starting transfers between devices, shards(): parts = lax.all_to_all(part.reshape(devices, own_rows, up_chan), axes, 0, 0)  6.37 us
    all_to_all x1, starting transfers between devices, spread_over(): lax.all_to_all(jnp.broadcast_to(values[None], (count,) + values.shape), a...  6.25 us
  transfers between devices with their start and end apart: 38, of which 19 were waited for; matrix products, arithmetic and copies ran while one was open for 3% of the time, Pallas kernels for 20%

profile of v1, /device:TPU:0, one launch (start us, length us, event | category | flops | bytes accessed | tf_op | source)
XLA Modules:
  0.0 178.3 jit_solution(6570740375516134244)
XLA Ops:
  0.6 0.5 collective-permute-start
  1.8 0.7 concatenate.3
  2.5 0.9 pad_maximum_fusion.1.refs_9_.refs_3_
  3.4 3.6 %collective-permute-start.3 = (bf16[3,8,4096]{2,1,0:T(8,128)(2,1)S(1)}, bf16[3,8,4096]{2,1,0:T(8,128)(2,1)S(1)}, u32[]{:S(2)}, u32[]{:S(2)}) collective-permute-start(bf16[3,8,4096]{2,1,0:T(8,128)(2,1)S(1)} %pad_maximum_fusion.1.refs_9_.refs_3_), channel_id=1, source_target_pairs={{0,24},{8,16},{16,8},{24,0},{1,25},{9,17},{17,9},{25,1},{2,26},{10... | collective-permute-start | bytes 589832 | tf_op jit(solution)/shard_map/ppermute | solution.py:663
  7.0 0.5 collective-permute-start.2
  7.7 0.6 stack.45.refs_0_
  8.2 0.7 broadcast_in_dim.7
  9.0 6.2 %all-to-all-start = ((bf16[32,4,640]{2,1,0:T(4,128)(2,1)}), bf16[32,4,640]{2,1,0:T(4,128)(2,1)S(1)}, u32[]{:S(2)}, u32[]{:S(2)}) async-start(bf16[32,4,640]{2,1,0:T(4,128)(2,1)} %broadcast_in_dim.7), calls=%async_computation | async-start | bytes 327680 | tf_op jit(solution)/shard_map/all_to_all | solution.py:659
  15.2 1.5 collective-permute-done.2.refs_11_.refs_5_
  17.0 0.3 copy-done.15
  17.4 0.3 copy-done.16
  17.7 9.6 %shard_map.235 = (bf16[128,384]{1,0:T(8,128)(2,1)}, bf16[384,128]{1,0:T(8,128)(2,1)}, bf16[128,640]{1,0:T(8,128)(2,1)}, bf16[128,128]{1,0:T(8,128)(2,1)}, bf16[1...) custom-call(s32[6]{0:T(128)} %stack.45.refs_0_, ...), custom_call_target="tpu_custom_call" | custom-call | flops 4805306368 | bytes 1597440 | tf_op jit(solution)/shard_map/pallas_call | solution.py:55
  27.4 2.0 %collective-permute-start.6 = (bf16[64,384]{1,0:T(8,128)(2,1)}, bf16[64,384]{1,0:T(8,128)(2,1)S(1)}, u32[]{:S(2)}, u32[]{:S(2)}) collective-permute-start(bf16[64,384]{1,0:T(8,128)(2,1)} %get-tuple-element.82), channel_id=1, source_target_pairs={{0,2},{1,6},{2,3},{3,7},{4,0},{5,4},{6,1},{7,5},{8,10},{9,14},{10,... | collective-permute-start | bytes 147464 | tf_op jit(solution)/shard_map/ppermute | solution.py:695
  29.4 3.9 %collective-permute-start.7 = (bf16[64,384]{1,0:T(8,128)(2,1)}, bf16[64,384]{1,0:T(8,128)(2,1)S(1)}, u32[]{:S(2)}, u32[]{:S(2)}) collective-permute-start(bf16[64,384]{1,0:T(8,128)(2,1)} %get-tuple-element.83), channel_id=1, source_target_pairs={{0,3},{1,7},{2,2},{3,6},{4,1},{5,5},{6,0},{7,4},{8,11},{9,15},{10,... | collective-permute-start | bytes 147464 | tf_op jit(solution)/shard_map/ppermute | solution.py:695
  33.3 1.5 collective-permute-start.4
  35.0 0.5 multiply_add_fusion.refs_0_.refs_1_
  35.9 1.0 copy.29
  36.9 7.3 %shard_map.236 = (f32[8,256,128]{2,1,0:T(8,128)}, bf16[8,128,256]{2,1,0:T(8,128)(2,1)}, bf16[8,288,256]{2,1,0:T(8,128)(2,1)}, bf16[8,256,128]{2,1,0:T(8,128)(2,1...) custom-call(s32[8]{0:T(128)} %multiply_add_fusion.refs_0_.refs_1_, ...), custom_call_target="tpu_custom_call" | custom-call | flops 8000000000 | bytes 8000000 | tf_op jit(solution)/shard_map/pallas_call | solution.py:259
  44.3 0.6 copy-done.28
  44.9 9.3 %shard_map.237 = (bf16[8,256,128]{2,1,0:T(8,128)(2,1)}, bf16[256,128]{1,0:T(8,128)(2,1)}, bf16[128,256]{1,0:T(8,128)(2,1)}, bf16[256,128]{1,0:T(8,128)(2,1)}, bf...) custom-call(s32[6]{0:T(128)} %stack.45.refs_0_, ...), custom_call_target="tpu_custom_call" | custom-call | flops 6000000000 | bytes 2270208 | tf_op jit(solution)/shard_map/pallas_call | solution.py:55
  54.2 6.4 %all-to-all-start.1 = ((bf16[32,64,128]{2,1,0:T(8,128)(2,1)}), bf16[32,64,128]{2,1,0:T(8,128)(2,1)S(1)}, u32[]{:S(2)}, u32[]{:S(2)}) async-start(bf16[32,64,128]{2,1,0:T(8,128)(2,1)} %bitcast.27), calls=%async_computation.1 | async-start | bytes 1048576 | tf_op jit(solution)/shard_map/all_to_all | solution.py:736
  60.7 8.4 %shard_map.238 = (bf16[32,256]{1,0:T(8,128)(2,1)}, bf16[32,256]{1,0:T(8,128)(2,1)}, bf16[32,256]{1,0:T(8,128)(2,1)}, bf16[32,256]{1,0:T(8,128)(2,1)}, bf16[32,25...) custom-call(s32[6]{0:T(128)} %stack.45.refs_0_, ...), custom_call_target="tpu_custom_call" | custom-call | flops 268435456 | bytes 983040 | tf_op jit(solution)/shard_map/pallas_call | solution.py:55
  69.4 1.7 collective-permute-start.9
  71.1 2.6 %collective-permute-start.11 = (bf16[32,256]{1,0:T(8,128)(2,1)}, bf16[32,256]{1,0:T(8,128)(2,1)S(1)}, u32[]{:S(2)}, u32[]{:S(2)}) collective-permute-start(bf16[32,256]{1,0:T(8,128)(2,1)} %get-tuple-element.91), channel_id=1, source_target_pairs={{0,4},{1,5},{2,6},{3,7},{4,0},{5,1},{6,2},{7,3},{8,12},{9,13},{10,... | collective-permute-start | bytes 49160 | tf_op jit(solution)/shard_map/ppermute | solution.py:663
  73.8 3.5 %collective-permute-start.13 = (bf16[32,256]{1,0:T(8,128)(2,1)}, bf16[32,256]{1,0:T(8,128)(2,1)S(1)}, u32[]{:S(2)}, u32[]{:S(2)}) collective-permute-start(bf16[32,256]{1,0:T(8,128)(2,1)} %get-tuple-element.93), channel_id=1, source_target_pairs={{0,6},{1,7},{2,4},{3,5},{4,2},{5,3},{6,0},{7,1},{8,14},{9,15},{10,... | collective-permute-start | bytes 49160 | tf_op jit(solution)/shard_map/ppermute | solution.py:663
  78.0 1.6 collective-permute-done.13.refs_11_.refs_8_.refs_14_
  79.6 2.9 %collective-permute-done.14.refs_12_.refs_9_.refs_15_ = bf16[32,256]{1,0:T(8,128)(2,1)S(1)} collective-permute-done((bf16[32,256]{1,0:T(8,128)(2,1)}, bf16[32,256]{1,0:T(8,128)(2,1)S(1)}, u32[]{:S(2)}, u32[]{:S(2)}) %collective-permute-start.14) | collective-permute-done | bytes 16416 | tf_op jit(solution)/shard_map/ppermute | solution.py:663
  82.6 1.6 shard_map.239
  84.2 3.1 %all-to-all-start.2 = ((bf16[32,64,128]{2,1,0:T(8,128)(2,1)}), bf16[32,64,128]{2,1,0:T(8,128)(2,1)S(1)}, u32[]{:S(2)}, u32[]{:S(2)}) async-start(bf16[32,64,128]{2,1,0:T(8,128)(2,1)} %get-tuple-element.97.refs_10_.refs_17_), calls=%async_computation.2 | async-start | bytes 1048576 | tf_op jit(solution)/shard_map/all_to_all | solution.py:756
  87.3 5.7 %shard_map.240 = (bf16[8,4096]{1,0:T(8,128)(2,1)}, bf16[8,4096]{1,0:T(8,128)(2,1)}, bf16[8,4096]{1,0:T(8,128)(2,1)}, bf16[8,4096]{1,0:T(8,128)(2,1)}) custom-call(s32[6]{0:T(128)} %stack.45.refs_0_, bf16[1024,4096]{1,0:T(8,128)(2,1)} %refs_29_.1, bf16[32,256]{1,0:T(8,128)(2,1)} %get-tuple-element.96.refs_2_.refs_8_, bf16[32,256]{1,0:T(8,128)(2,1)} %copy-done.1, ...), custom_call_target="tpu_custom_call" | custom-call | flops 268435456 | bytes 393216 | tf_op jit(solution)/shard_map/pallas_call | solution.py:55
  93.1 1.6 collective-permute-start.15
  94.7 1.5 collective-permute-start.16
  96.1 0.5 collective-permute-start.17
  96.6 3.9 %shard_map.241 = (f32[2048,128]{1,0:T(8,128)}, f32[2048,128]{1,0:T(8,128)}) custom-call(s32[6]{0:T(128)} %stack.45.refs_0_, s32[8]{0:T(128)} %multiply_add_fusion.refs_0_.refs_1_, bf16[2048,128]{1,0:T(8,128)(2,1)} %bitcast.42, bf16[2048,128]{1,0:T(8,128)(2,1)} %bitcast.44, bf16[256,128]{1,0:T(8,128)(2,1)} %get-tuple-element.112.refs_4_, ...), custom_call_target="tpu_custom_call" | custom-call | flops 2000000000 | bytes 3474432 | tf_op jit(solution)/shard_map/pallas_call | solution.py:55
  100.6 1.2 collective-permute-done.17.refs_34_
  101.8 1.5 all-to-all-done.2
  103.4 0.8 copy-done.17
  104.2 21.1 %shard_map.242 = (bf16[4,4,272,128]{3,2,1,0:T(8,128)(2,1)}, bf16[4,4,272,128]{3,2,1,0:T(8,128)(2,1)}) custom-call(s32[6]{0:T(128)} %stack.45.refs_0_, s32[8]{0:T(128)} %multiply_add_fusion.refs_0_.refs_1_, bf16[8,256,128]{2,1,0:T(8,128)(2,1)} %bitcast.30, bf16[256,128]{1,0:T(8,128)(2,1)} %get-tuple-element.102.refs_3_, ...), custom_call_target="tpu_custom_call" | custom-call | flops 30000001024 | bytes 3710976 | tf_op jit(solution)/shard_map/pallas_call | solution.py:55
  125.4 3.0 %collective-permute-done.18.refs_1_ = bf16[4,4,272,128]{3,2,1,0:T(8,128)(2,1)S(1)} collective-permute-done((bf16[4,4,272,128]{3,2,1,0:T(8,128)(2,1)}, bf16[4,4,272,128]{3,2,1,0:T(8,128)(2,1)S(1)}, u32[]{:S(2)}, u32[]{:S(2)}) %collective-permute-start.18) | collective-permute-done | bytes 1114144 | tf_op jit(solution)/shard_map/ppermute | solution.py:663
  128.3 1.2 copy-done
  130.1 1.5 collective-permute-start.20
  131.6 1.8 collective-permute-start.21
  133.4 6.0 %collective-permute-done.19.refs_1_ = bf16[4,272,128]{2,1,0:T(8,128)(2,1)S(1)} collective-permute-done((bf16[4,272,128]{2,1,0:T(8,128)(2,1)S(1)}, bf16[4,272,128]{2,1,0:T(8,128)(2,1)S(1)}, u32[]{:S(2)}, u32[]{:S(2)}) %collective-permute-start.19) | collective-permute-done | bytes 278560 | tf_op jit(solution)/shard_map/ppermute | solution.py:663
  139.4 5.2 %collective-permute-done.21.refs_3_ = bf16[4,272,128]{2,1,0:T(8,128)(2,1)S(1)} collective-permute-done((bf16[4,272,128]{2,1,0:T(8,128)(2,1)S(1)}, bf16[4,272,128]{2,1,0:T(8,128)(2,1)S(1)}, u32[]{:S(2)}, u32[]{:S(2)}) %collective-permute-start.21) | collective-permute-done | bytes 278560 | tf_op jit(solution)/shard_map/ppermute | solution.py:663
  144.8 1.0 collective-permute-start.22
  145.9 1.7 collective-permute-start.23
  147.6 1.7 collective-permute-start.24
  149.5 3.3 %collective-permute-done.23.refs_2_ = bf16[272,128]{1,0:T(8,128)(2,1)S(1)} collective-permute-done((bf16[272,128]{1,0:T(8,128)(2,1)S(1)}, bf16[272,128]{1,0:T(8,128)(2,1)S(1)}, u32[]{:S(2)}, u32[]{:S(2)}) %collective-permute-start.23) | collective-permute-done | bytes 69664 | tf_op jit(solution)/shard_map/ppermute | solution.py:663
  152.7 1.0 collective-permute-done.24.refs_3_
  153.8 1.8 collective-permute-start.27
  155.6 1.2 collective-permute-start.26
  156.8 1.5 collective-permute-start.25
  158.3 1.8 %collective-permute-done.27 = bf16[272,128]{1,0:T(8,128)(2,1)S(1)} collective-permute-done((bf16[272,128]{1,0:T(8,128)(2,1)S(1)}, bf16[272,128]{1,0:T(8,128)(2,1)S(1)}, u32[]{:S(2)}, u32[]{:S(2)}) %collective-permute-start.27) | collective-permute-done | bytes 69664 | tf_op jit(solution)/shard_map/ppermute | solution.py:663
  160.1 1.5 collective-permute-done.26
  161.7 1.7 collective-permute-start.30
  163.4 1.1 collective-permute-start.29
  164.5 0.8 collective-permute-start.28
  165.2 0.7 reshape.49
  165.9 5.6 %collective-permute-done.30.refs_4_ = bf16[4,272,128]{2,1,0:T(8,128)(2,1)S(1)} collective-permute-done((bf16[4,272,128]{2,1,0:T(8,128)(2,1)S(1)}, bf16[4,272,128]{2,1,0:T(8,128)(2,1)S(1)}, u32[]{:S(2)}, u32[]{:S(2)}) %collective-permute-start.30) | collective-permute-done | bytes 278560 | tf_op jit(solution)/shard_map/ppermute | solution.py:663
  171.5 2.0 %collective-permute-done.29.refs_3_ = bf16[4,272,128]{2,1,0:T(8,128)(2,1)S(1)} collective-permute-done((bf16[4,272,128]{2,1,0:T(8,128)(2,1)S(1)}, bf16[4,272,128]{2,1,0:T(8,128)(2,1)S(1)}, u32[]{:S(2)}, u32[]{:S(2)}) %collective-permute-start.29) | collective-permute-done | bytes 278560 | tf_op jit(solution)/shard_map/ppermute | solution.py:663
  173.5 0.5 collective-permute-start.32
  174.1 0.7 fusion
  175.1 0.4 collective-permute-done.32.refs_6_
  175.5 2.8 %shard_map.246 = (f32[288,128]{1,0:T(8,128)}, f32[128,4096]{1,0:T(8,128)}, f32[4096,128]{1,0:T(8,128)}, f32[32,128]{1,0:T(8,128)}) custom-call(s32[6]{0:T(128)S(1)} %copy-done.9, bf16[4,272,128]{2,1,0:T(8,128)(2,1)S(1)} %pad_maximum_fusion.refs_1_, bf16[4,272,128]{2,1,0:T(8,128)(2,1)S(1)} %collective-permute-done.28.refs_2_, ...), custom_call_target="tpu_custom_call" | custom-call | bytes 6586368 | tf_op jit(solution)/shard_map/pallas_call | solution.py:55
  (102 shorter events, 3.7 us)
Async XLA Ops:
  0.6 1.9 %collective-permute-start = (bf16[8,4096]{1,0:T(8,128)(2,1)}, bf16[8,4096]{1,0:T(8,128)(2,1)S(1)}, u32[]{:S(2)}, u32[]{:S(2)}) collective-permute-start(bf16[8,4096]{1,0:T(8,128)(2,1)} %bitcast.32), channel_id=1, source_target_pairs={{0,1},{1,0},{2,3},{3,2},{4,5},{5,4},{6,7},{7,6},{8,9},{9,8},{10,11... | collective-permute-start | bytes 196616 | tf_op jit(solution)/shard_map/ppermute | solution.py:663
  3.4 13.6 %copy-start.13 = (bf16[3,8,4096]{2,1,0:T(8,128)(2,1)}, bf16[3,8,4096]{2,1,0:T(8,128)(2,1)S(1)}, u32[]{:S(2)}) copy-start(bf16[3,8,4096]{2,1,0:T(8,128)(2,1)S(1)} %pad_maximum_fusion.1.refs_9_.refs_3_) | copy-start | bytes 589828
  3.4 11.8 %collective-permute-start.3 = (bf16[3,8,4096]{2,1,0:T(8,128)(2,1)S(1)}, bf16[3,8,4096]{2,1,0:T(8,128)(2,1)S(1)}, u32[]{:S(2)}, u32[]{:S(2)}) collective-permute-start(bf16[3,8,4096]{2,1,0:T(8,128)(2,1)S(1)} %pad_maximum_fusion.1.refs_9_.refs_3_), channel_id=1, source_target_pairs={{0,24},{8,16},{16,8},{24,0},{1,25},{9,17},{17,9},{25,1},{2,26},{10... | collective-permute-start | bytes 589832 | tf_op jit(solution)/shard_map/ppermute | solution.py:663
  7.0 9.7 %collective-permute-start.2 = (bf16[3,8,4096]{2,1,0:T(8,128)(2,1)S(1)}, bf16[3,8,4096]{2,1,0:T(8,128)(2,1)S(1)}, u32[]{:S(2)}, u32[]{:S(2)}) collective-permute-start(bf16[3,8,4096]{2,1,0:T(8,128)(2,1)S(1)} %pad_maximum_fusion.1.refs_9_.refs_3_), channel_id=1, source_target_pairs={{0,16},{8,24},{16,0},{24,8},{1,17},{9,25},{17,1},{25,9},{2,18},{10... | collective-permute-start | bytes 589832 | tf_op jit(solution)/shard_map/ppermute | solution.py:663
  7.5 9.5 %collective-permute-start.1 = (bf16[3,8,4096]{2,1,0:T(8,128)(2,1)S(1)}, bf16[3,8,4096]{2,1,0:T(8,128)(2,1)S(1)}, u32[]{:S(2)}, u32[]{:S(2)}) collective-permute-start(bf16[3,8,4096]{2,1,0:T(8,128)(2,1)S(1)} %pad_maximum_fusion.1.refs_9_.refs_3_), channel_id=1, source_target_pairs={{0,8},{8,0},{16,24},{24,16},{1,9},{9,1},{17,25},{25,17},{2,10},{10... | collective-permute-start | bytes 589832 | tf_op jit(solution)/shard_map/ppermute | solution.py:663
  9.0 25.8 %all-to-all-start = ((bf16[32,4,640]{2,1,0:T(4,128)(2,1)}), bf16[32,4,640]{2,1,0:T(4,128)(2,1)S(1)}, u32[]{:S(2)}, u32[]{:S(2)}) async-start(bf16[32,4,640]{2,1,0:T(4,128)(2,1)} %broadcast_in_dim.7), calls=%async_computation | async-start | bytes 327680 | tf_op jit(solution)/shard_map/all_to_all | solution.py:659
  15.2 1.8 %copy-start.14 = (bf16[3,8,4096]{2,1,0:T(8,128)(2,1)}, bf16[3,8,4096]{2,1,0:T(8,128)(2,1)S(1)}, u32[]{:S(2)}) copy-start(bf16[3,8,4096]{2,1,0:T(8,128)(2,1)S(1)} %collective-permute-done.3.refs_12_.refs_6_) | copy-start | bytes 589828
  27.3 16.9 %collective-permute-start.5 = (bf16[64,384]{1,0:T(8,128)(2,1)}, bf16[64,384]{1,0:T(8,128)(2,1)S(1)}, u32[]{:S(2)}, u32[]{:S(2)}) collective-permute-start(bf16[64,384]{1,0:T(8,128)(2,1)} %get-tuple-element.81), channel_id=1, source_target_pairs={{0,1},{1,5},{2,0},{3,4},{4,3},{5,7},{6,2},{7,6},{8,9},{9,13},{10,8... | collective-permute-start | bytes 147464 | tf_op jit(solution)/shard_map/ppermute | solution.py:695
  27.4 16.8 %collective-permute-start.6 = (bf16[64,384]{1,0:T(8,128)(2,1)}, bf16[64,384]{1,0:T(8,128)(2,1)S(1)}, u32[]{:S(2)}, u32[]{:S(2)}) collective-permute-start(bf16[64,384]{1,0:T(8,128)(2,1)} %get-tuple-element.82), channel_id=1, source_target_pairs={{0,2},{1,6},{2,3},{3,7},{4,0},{5,4},{6,1},{7,5},{8,10},{9,14},{10,... | collective-permute-start | bytes 147464 | tf_op jit(solution)/shard_map/ppermute | solution.py:695
  29.4 14.8 %collective-permute-start.7 = (bf16[64,384]{1,0:T(8,128)(2,1)}, bf16[64,384]{1,0:T(8,128)(2,1)S(1)}, u32[]{:S(2)}, u32[]{:S(2)}) collective-permute-start(bf16[64,384]{1,0:T(8,128)(2,1)} %get-tuple-element.83), channel_id=1, source_target_pairs={{0,3},{1,7},{2,2},{3,6},{4,1},{5,5},{6,0},{7,4},{8,11},{9,15},{10,... | collective-permute-start | bytes 147464 | tf_op jit(solution)/shard_map/ppermute | solution.py:695
  33.3 11.0 %collective-permute-start.4 = (bf16[64,384]{1,0:T(8,128)(2,1)}, bf16[64,384]{1,0:T(8,128)(2,1)S(1)}, u32[]{:S(2)}, u32[]{:S(2)}) collective-permute-start(bf16[64,384]{1,0:T(8,128)(2,1)} %get-tuple-element.77.refs_10_), channel_id=1, source_target_pairs={{0,0},{1,4},{2,1},{3,5},{4,2},{5,6},{6,3},{7,7},{8,8},{9,12},{10,9... | collective-permute-start | bytes 147464 | tf_op jit(solution)/shard_map/ppermute | solution.py:695
  54.2 28.3 %all-to-all-start.1 = ((bf16[32,64,128]{2,1,0:T(8,128)(2,1)}), bf16[32,64,128]{2,1,0:T(8,128)(2,1)S(1)}, u32[]{:S(2)}, u32[]{:S(2)}) async-start(bf16[32,64,128]{2,1,0:T(8,128)(2,1)} %bitcast.27), calls=%async_computation.1 | async-start | bytes 1048576 | tf_op jit(solution)/shard_map/all_to_all | solution.py:736
  60.6 16.8 %copy-start.27 = (bf16[1,4,512]{2,1,0:T(4,128)(2,1)S(1)}, bf16[1,4,512]{2,1,0:T(4,128)(2,1)}, u32[]{:S(2)}) copy-start(bf16[1,4,512]{2,1,0:T(4,128)(2,1)} %param.32) | copy-start | bytes 12292
  60.6 16.9 %copy-start.26 = (bf16[128,32]{0,1:T(8,128)(2,1)S(1)}, bf16[128,32]{0,1:T(8,128)(2,1)}, u32[]{:S(2)}) copy-start(bf16[128,32]{0,1:T(8,128)(2,1)} %param.31) | copy-start | bytes 24580
  60.6 21.9 %copy-start.8 = (s32[6]{0:T(128)S(1)}, s32[6]{0:T(128)}, u32[]{:S(2)}) copy-start(s32[6]{0:T(128)} %stack.45.refs_0_) | copy-start | bytes 76
  60.7 21.9 %copy-start.10 = (bf16[128,128]{1,0:T(8,128)(2,1)S(1)}, bf16[128,128]{1,0:T(8,128)(2,1)}, u32[]{:S(2)}) copy-start(bf16[128,128]{1,0:T(8,128)(2,1)} %get-tuple-element.86.refs_3_.refs_10_) | copy-start | bytes 98308
  60.7 21.9 %copy-start.11 = (f32[8,256,128]{2,1,0:T(8,128)S(1)}, f32[8,256,128]{2,1,0:T(8,128)}, u32[]{:S(2)}) copy-start(f32[8,256,128]{2,1,0:T(8,128)} %get-tuple-element.85.refs_23_) | copy-start | bytes 3145732
  69.1 4.7 %collective-permute-start.8 = (bf16[32,256]{1,0:T(8,128)(2,1)}, bf16[32,256]{1,0:T(8,128)(2,1)S(1)}, u32[]{:S(2)}, u32[]{:S(2)}) collective-permute-start(bf16[32,256]{1,0:T(8,128)(2,1)} %get-tuple-element.88), channel_id=1, source_target_pairs={{0,1},{1,0},{2,3},{3,2},{4,5},{5,4},{6,7},{7,6},{8,9},{9,8},{10,11... | collective-permute-start | bytes 49160 | tf_op jit(solution)/shard_map/ppermute | solution.py:663
  69.4 7.9 %collective-permute-start.9 = (bf16[32,256]{1,0:T(8,128)(2,1)}, bf16[32,256]{1,0:T(8,128)(2,1)S(1)}, u32[]{:S(2)}, u32[]{:S(2)}) collective-permute-start(bf16[32,256]{1,0:T(8,128)(2,1)} %get-tuple-element.89), channel_id=1, source_target_pairs={{0,2},{1,3},{2,0},{3,1},{4,6},{5,7},{6,4},{7,5},{8,10},{9,11},{10,... | collective-permute-start | bytes 49160 | tf_op jit(solution)/shard_map/ppermute | solution.py:663
  71.1 6.5 %collective-permute-start.10 = (bf16[32,256]{1,0:T(8,128)(2,1)}, bf16[32,256]{1,0:T(8,128)(2,1)S(1)}, u32[]{:S(2)}, u32[]{:S(2)}) collective-permute-start(bf16[32,256]{1,0:T(8,128)(2,1)} %get-tuple-element.90), channel_id=1, source_target_pairs={{0,3},{1,2},{2,1},{3,0},{4,7},{5,6},{6,5},{7,4},{8,11},{9,10},{10,... | collective-permute-start | bytes 49160 | tf_op jit(solution)/shard_map/ppermute | solution.py:663
  71.1 6.5 %collective-permute-start.11 = (bf16[32,256]{1,0:T(8,128)(2,1)}, bf16[32,256]{1,0:T(8,128)(2,1)S(1)}, u32[]{:S(2)}, u32[]{:S(2)}) collective-permute-start(bf16[32,256]{1,0:T(8,128)(2,1)} %get-tuple-element.91), channel_id=1, source_target_pairs={{0,4},{1,5},{2,6},{3,7},{4,0},{5,1},{6,2},{7,3},{8,12},{9,13},{10,... | collective-permute-start | bytes 49160 | tf_op jit(solution)/shard_map/ppermute | solution.py:663
  73.7 4.3 %collective-permute-start.12 = (bf16[32,256]{1,0:T(8,128)(2,1)}, bf16[32,256]{1,0:T(8,128)(2,1)S(1)}, u32[]{:S(2)}, u32[]{:S(2)}) collective-permute-start(bf16[32,256]{1,0:T(8,128)(2,1)} %get-tuple-element.92), channel_id=1, source_target_pairs={{0,5},{1,4},{2,7},{3,6},{4,1},{5,0},{6,3},{7,2},{8,13},{9,12},{10,... | collective-permute-start | bytes 49160 | tf_op jit(solution)/shard_map/ppermute | solution.py:663
  73.8 10.4 %copy-start.1 = (bf16[32,256]{1,0:T(8,128)(2,1)}, bf16[32,256]{1,0:T(8,128)(2,1)S(1)}, u32[]{:S(2)}) copy-start(bf16[32,256]{1,0:T(8,128)(2,1)S(1)} %collective-permute-done.8.refs_6_.refs_3_.refs_9_) | copy-start | bytes 49156
  73.8 5.8 %collective-permute-start.13 = (bf16[32,256]{1,0:T(8,128)(2,1)}, bf16[32,256]{1,0:T(8,128)(2,1)S(1)}, u32[]{:S(2)}, u32[]{:S(2)}) collective-permute-start(bf16[32,256]{1,0:T(8,128)(2,1)} %get-tuple-element.93), channel_id=1, source_target_pairs={{0,6},{1,7},{2,4},{3,5},{4,2},{5,3},{6,0},{7,1},{8,14},{9,15},{10,... | collective-permute-start | bytes 49160 | tf_op jit(solution)/shard_map/ppermute | solution.py:663
  77.4 6.8 %copy-start.2 = (bf16[32,256]{1,0:T(8,128)(2,1)}, bf16[32,256]{1,0:T(8,128)(2,1)S(1)}, u32[]{:S(2)}) copy-start(bf16[32,256]{1,0:T(8,128)(2,1)S(1)} %collective-permute-done.9.refs_7_.refs_4_.refs_10_) | copy-start | bytes 49156
  77.4 5.2 %collective-permute-start.14 = (bf16[32,256]{1,0:T(8,128)(2,1)}, bf16[32,256]{1,0:T(8,128)(2,1)S(1)}, u32[]{:S(2)}, u32[]{:S(2)}) collective-permute-start(bf16[32,256]{1,0:T(8,128)(2,1)} %get-tuple-element.94), channel_id=1, source_target_pairs={{0,7},{1,6},{2,5},{3,4},{4,3},{5,2},{6,1},{7,0},{8,15},{9,14},{10,... | collective-permute-start | bytes 49160 | tf_op jit(solution)/shard_map/ppermute | solution.py:663
  77.6 6.6 %copy-start.3 = (bf16[32,256]{1,0:T(8,128)(2,1)}, bf16[32,256]{1,0:T(8,128)(2,1)S(1)}, u32[]{:S(2)}) copy-start(bf16[32,256]{1,0:T(8,128)(2,1)S(1)} %collective-permute-done.10.refs_8_.refs_5_.refs_11_) | copy-start | bytes 49156
  77.6 6.5 %copy-start.4 = (bf16[32,256]{1,0:T(8,128)(2,1)}, bf16[32,256]{1,0:T(8,128)(2,1)S(1)}, u32[]{:S(2)}) copy-start(bf16[32,256]{1,0:T(8,128)(2,1)S(1)} %collective-permute-done.11.refs_9_.refs_6_.refs_12_) | copy-start | bytes 49156
  78.0 6.2 %copy-start.5 = (bf16[32,256]{1,0:T(8,128)(2,1)}, bf16[32,256]{1,0:T(8,128)(2,1)S(1)}, u32[]{:S(2)}) copy-start(bf16[32,256]{1,0:T(8,128)(2,1)S(1)} %collective-permute-done.12.refs_10_.refs_7_.refs_13_) | copy-start | bytes 49156
  79.6 4.6 %copy-start.6 = (bf16[32,256]{1,0:T(8,128)(2,1)}, bf16[32,256]{1,0:T(8,128)(2,1)S(1)}, u32[]{:S(2)}) copy-start(bf16[32,256]{1,0:T(8,128)(2,1)S(1)} %collective-permute-done.13.refs_11_.refs_8_.refs_14_) | copy-start | bytes 49156
  82.5 1.7 copy-start.7
  84.2 8.8 %copy-start.12 = (f32[32,128]{1,0:T(8,128)}, f32[32,128]{1,0:T(8,128)S(1)}, u32[]{:S(2)}) copy-start(f32[32,128]{1,0:T(8,128)S(1)} %get-tuple-element.107.refs_14_) | copy-start | bytes 49156
  84.2 19.1 %all-to-all-start.2 = ((bf16[32,64,128]{2,1,0:T(8,128)(2,1)}), bf16[32,64,128]{2,1,0:T(8,128)(2,1)S(1)}, u32[]{:S(2)}, u32[]{:S(2)}) async-start(bf16[32,64,128]{2,1,0:T(8,128)(2,1)} %get-tuple-element.97.refs_10_.refs_17_), calls=%async_computation.2 | async-start | bytes 1048576 | tf_op jit(solution)/shard_map/all_to_all | solution.py:756
  93.1 7.5 %collective-permute-start.15 = (bf16[8,4096]{1,0:T(8,128)(2,1)}, bf16[8,4096]{1,0:T(8,128)(2,1)S(1)}, u32[]{:S(2)}, u32[]{:S(2)}) collective-permute-start(bf16[8,4096]{1,0:T(8,128)(2,1)} %get-tuple-element.99), channel_id=1, source_target_pairs={{0,8},{8,0},{16,24},{24,16},{1,9},{9,1},{17,25},{25,17},{2,10},{10... | collective-permute-start | bytes 196616 | tf_op jit(solution)/shard_map/ppermute | solution.py:663
  94.7 5.9 %collective-permute-start.16 = (bf16[8,4096]{1,0:T(8,128)(2,1)}, bf16[8,4096]{1,0:T(8,128)(2,1)S(1)}, u32[]{:S(2)}, u32[]{:S(2)}) collective-permute-start(bf16[8,4096]{1,0:T(8,128)(2,1)} %get-tuple-element.100), channel_id=1, source_target_pairs={{0,16},{8,24},{16,0},{24,8},{1,17},{9,25},{17,1},{25,9},{2,18},{10... | collective-permute-start | bytes 196616 | tf_op jit(solution)/shard_map/ppermute | solution.py:663
  96.1 5.7 %collective-permute-start.17 = (bf16[8,4096]{1,0:T(8,128)(2,1)}, bf16[8,4096]{1,0:T(8,128)(2,1)S(1)}, u32[]{:S(2)}, u32[]{:S(2)}) collective-permute-start(bf16[8,4096]{1,0:T(8,128)(2,1)} %get-tuple-element.101), channel_id=1, source_target_pairs={{0,24},{8,16},{16,8},{24,0},{1,25},{9,17},{17,9},{25,1},{2,26},{10... | collective-permute-start | bytes 196616 | tf_op jit(solution)/shard_map/ppermute | solution.py:663
  100.5 2.8 %copy-start.20 = (bf16[8,4096]{1,0:T(8,128)(2,1)}, bf16[8,4096]{1,0:T(8,128)(2,1)S(1)}, u32[]{:S(2)}) copy-start(bf16[8,4096]{1,0:T(8,128)(2,1)S(1)} %collective-permute-done.15.refs_32_) | copy-start | bytes 196612
  100.6 2.8 %copy-start.22 = (bf16[8,4096]{1,0:T(8,128)(2,1)}, bf16[8,4096]{1,0:T(8,128)(2,1)S(1)}, u32[]{:S(2)}) copy-start(bf16[8,4096]{1,0:T(8,128)(2,1)S(1)} %collective-permute-done.16.refs_33_) | copy-start | bytes 196612
  101.8 1.5 copy-start.24
  103.4 0.8 copy-start.17
  125.3 3.0 %collective-permute-start.18 = (bf16[4,4,272,128]{3,2,1,0:T(8,128)(2,1)}, bf16[4,4,272,128]{3,2,1,0:T(8,128)(2,1)S(1)}, u32[]{:S(2)}, u32[]{:S(2)}) collective-permute-start(bf16[4,4,272,128]{3,2,1,0:T(8,128)(2,1)} %get-tuple-element.121), channel_id=1, source_target_pairs={{0,1},{1,0},{2,3},{3,2},{4,5},{5,4},{6,7},{7,6},{8,9},{9,8},{10,11... | collective-permute-start | bytes 3342344 | tf_op jit(solution)/shard_map/ppermute | solution.py:663
  128.3 1.2 copy-start
  129.6 44.5 %copy-start.18 = (bf16[1,8,4096]{2,1,0:T(8,128)(2,1)S(1)}, bf16[1,8,4096]{2,1,0:T(8,128)(2,1)}, u32[]{:S(2)}) copy-start(bf16[1,8,4096]{2,1,0:T(8,128)(2,1)} %param.20) | copy-start | bytes 196612
  129.6 44.5 %copy-start.19 = (bf16[8,4096]{1,0:T(8,128)(2,1)S(1)}, bf16[8,4096]{1,0:T(8,128)(2,1)}, u32[]{:S(2)}) copy-start(bf16[8,4096]{1,0:T(8,128)(2,1)} %get-tuple-element.98.refs_16_) | copy-start | bytes 196612
  129.6 44.5 %copy-start.21 = (bf16[8,4096]{1,0:T(8,128)(2,1)S(1)}, bf16[8,4096]{1,0:T(8,128)(2,1)}, u32[]{:S(2)}) copy-start(bf16[8,4096]{1,0:T(8,128)(2,1)} %copy-done.20) | copy-start | bytes 196612
  129.6 44.5 %copy-start.23 = (bf16[8,4096]{1,0:T(8,128)(2,1)S(1)}, bf16[8,4096]{1,0:T(8,128)(2,1)}, u32[]{:S(2)}) copy-start(bf16[8,4096]{1,0:T(8,128)(2,1)} %copy-done.22) | copy-start | bytes 196612
  129.6 44.5 %copy-start.25 = (bf16[8,4096]{1,0:T(8,128)(2,1)S(1)}, bf16[8,4096]{1,0:T(8,128)(2,1)}, u32[]{:S(2)}) copy-start(bf16[8,4096]{1,0:T(8,128)(2,1)} %copy-done.24) | copy-start | bytes 196612
  129.6 45.9 %copy-start.9 = (s32[6]{0:T(128)S(1)}, s32[6]{0:T(128)}, u32[]{:S(2)}) copy-start(s32[6]{0:T(128)} %stack.45.refs_0_) | copy-start | bytes 76
  129.9 9.6 %collective-permute-start.19 = (bf16[4,272,128]{2,1,0:T(8,128)(2,1)S(1)}, bf16[4,272,128]{2,1,0:T(8,128)(2,1)S(1)}, u32[]{:S(2)}, u32[]{:S(2)}) collective-permute-start(bf16[4,272,128]{2,1,0:T(8,128)(2,1)S(1)} %get-tuple-element.123), channel_id=1, source_target_pairs={{0,8},{8,0},{16,24},{24,16},{1,9},{9,1},{17,25},{25,17},{2,10},{10... | collective-permute-start | bytes 835592 | tf_op jit(solution)/shard_map/ppermute | solution.py:663
  130.1 9.3 %collective-permute-start.20 = (bf16[4,272,128]{2,1,0:T(8,128)(2,1)S(1)}, bf16[4,272,128]{2,1,0:T(8,128)(2,1)S(1)}, u32[]{:S(2)}, u32[]{:S(2)}) collective-permute-start(bf16[4,272,128]{2,1,0:T(8,128)(2,1)S(1)} %get-tuple-element.124), channel_id=1, source_target_pairs={{0,16},{8,24},{16,0},{24,8},{1,17},{9,25},{17,1},{25,9},{2,18},{10... | collective-permute-start | bytes 835592 | tf_op jit(solution)/shard_map/ppermute | solution.py:663
  131.6 13.0 %collective-permute-start.21 = (bf16[4,272,128]{2,1,0:T(8,128)(2,1)S(1)}, bf16[4,272,128]{2,1,0:T(8,128)(2,1)S(1)}, u32[]{:S(2)}, u32[]{:S(2)}) collective-permute-start(bf16[4,272,128]{2,1,0:T(8,128)(2,1)S(1)} %get-tuple-element.125), channel_id=1, source_target_pairs={{0,24},{8,16},{16,8},{24,0},{1,25},{9,17},{17,9},{25,1},{2,26},{10... | collective-permute-start | bytes 835592 | tf_op jit(solution)/shard_map/ppermute | solution.py:663
  144.8 4.7 %collective-permute-start.22 = (bf16[272,128]{1,0:T(8,128)(2,1)S(1)}, bf16[272,128]{1,0:T(8,128)(2,1)S(1)}, u32[]{:S(2)}, u32[]{:S(2)}) collective-permute-start(bf16[272,128]{1,0:T(8,128)(2,1)S(1)} %get-tuple-element.127), channel_id=1, source_target_pairs={{0,2},{1,3},{2,0},{3,1},{4,6},{5,7},{6,4},{7,5},{8,10},{9,11},{10,... | collective-permute-start | bytes 208904 | tf_op jit(solution)/shard_map/ppermute | solution.py:663
  145.9 6.9 %collective-permute-start.23 = (bf16[272,128]{1,0:T(8,128)(2,1)S(1)}, bf16[272,128]{1,0:T(8,128)(2,1)S(1)}, u32[]{:S(2)}, u32[]{:S(2)}) collective-permute-start(bf16[272,128]{1,0:T(8,128)(2,1)S(1)} %get-tuple-element.128), channel_id=1, source_target_pairs={{0,4},{1,5},{2,6},{3,7},{4,0},{5,1},{6,2},{7,3},{8,12},{9,13},{10,... | collective-permute-start | bytes 208904 | tf_op jit(solution)/shard_map/ppermute | solution.py:663
  147.6 6.2 %collective-permute-start.24 = (bf16[272,128]{1,0:T(8,128)(2,1)S(1)}, bf16[272,128]{1,0:T(8,128)(2,1)S(1)}, u32[]{:S(2)}, u32[]{:S(2)}) collective-permute-start(bf16[272,128]{1,0:T(8,128)(2,1)S(1)} %get-tuple-element.129), channel_id=1, source_target_pairs={{0,6},{1,7},{2,4},{3,5},{4,2},{5,3},{6,0},{7,1},{8,14},{9,15},{10,... | collective-permute-start | bytes 208904 | tf_op jit(solution)/shard_map/ppermute | solution.py:663
  153.8 6.3 %collective-permute-start.27 = (bf16[272,128]{1,0:T(8,128)(2,1)S(1)}, bf16[272,128]{1,0:T(8,128)(2,1)S(1)}, u32[]{:S(2)}, u32[]{:S(2)}) collective-permute-start(bf16[272,128]{1,0:T(8,128)(2,1)S(1)} %shard_map.245), channel_id=1, source_target_pairs={{0,6},{1,7},{2,4},{3,5},{4,2},{5,3},{6,0},{7,1},{8,14},{9,15},{10,... | collective-permute-start | bytes 208904 | tf_op jit(solution)/shard_map/ppermute | solution.py:663
  155.6 6.1 %collective-permute-start.26 = (bf16[272,128]{1,0:T(8,128)(2,1)S(1)}, bf16[272,128]{1,0:T(8,128)(2,1)S(1)}, u32[]{:S(2)}, u32[]{:S(2)}) collective-permute-start(bf16[272,128]{1,0:T(8,128)(2,1)S(1)} %shard_map.245), channel_id=1, source_target_pairs={{0,4},{1,5},{2,6},{3,7},{4,0},{5,1},{6,2},{7,3},{8,12},{9,13},{10,... | collective-permute-start | bytes 208904 | tf_op jit(solution)/shard_map/ppermute | solution.py:663
  156.8 4.9 %collective-permute-start.25 = (bf16[272,128]{1,0:T(8,128)(2,1)S(1)}, bf16[272,128]{1,0:T(8,128)(2,1)S(1)}, u32[]{:S(2)}, u32[]{:S(2)}) collective-permute-start(bf16[272,128]{1,0:T(8,128)(2,1)S(1)} %shard_map.245), channel_id=1, source_target_pairs={{0,2},{1,3},{2,0},{3,1},{4,6},{5,7},{6,4},{7,5},{8,10},{9,11},{10,... | collective-permute-start | bytes 208904 | tf_op jit(solution)/shard_map/ppermute | solution.py:663
  161.7 9.8 %collective-permute-start.30 = (bf16[4,272,128]{2,1,0:T(8,128)(2,1)S(1)}, bf16[4,272,128]{2,1,0:T(8,128)(2,1)S(1)}, u32[]{:S(2)}, u32[]{:S(2)}) collective-permute-start(bf16[4,272,128]{2,1,0:T(8,128)(2,1)S(1)} %pad_maximum_fusion.refs_1_), channel_id=1, source_target_pairs={{0,24},{8,16},{16,8},{24,0},{1,25},{9,17},{17,9},{25,1},{2,26},{10... | collective-permute-start | bytes 835592 | tf_op jit(solution)/shard_map/ppermute | solution.py:663
  163.4 10.2 %collective-permute-start.29 = (bf16[4,272,128]{2,1,0:T(8,128)(2,1)S(1)}, bf16[4,272,128]{2,1,0:T(8,128)(2,1)S(1)}, u32[]{:S(2)}, u32[]{:S(2)}) collective-permute-start(bf16[4,272,128]{2,1,0:T(8,128)(2,1)S(1)} %pad_maximum_fusion.refs_1_), channel_id=1, source_target_pairs={{0,16},{8,24},{16,0},{24,8},{1,17},{9,25},{17,1},{25,9},{2,18},{10... | collective-permute-start | bytes 835592 | tf_op jit(solution)/shard_map/ppermute | solution.py:663
  164.5 9.1 %collective-permute-start.28 = (bf16[4,272,128]{2,1,0:T(8,128)(2,1)S(1)}, bf16[4,272,128]{2,1,0:T(8,128)(2,1)S(1)}, u32[]{:S(2)}, u32[]{:S(2)}) collective-permute-start(bf16[4,272,128]{2,1,0:T(8,128)(2,1)S(1)} %pad_maximum_fusion.refs_1_), channel_id=1, source_target_pairs={{0,8},{8,0},{16,24},{24,16},{1,9},{9,1},{17,25},{25,17},{2,10},{10... | collective-permute-start | bytes 835592 | tf_op jit(solution)/shard_map/ppermute | solution.py:663
  165.9 8.8 %collective-permute-start.31 = (bf16[4,272,128]{2,1,0:T(8,128)(2,1)S(1)}, bf16[4,272,128]{2,1,0:T(8,128)(2,1)S(1)}, u32[]{:S(2)}, u32[]{:S(2)}) collective-permute-start(bf16[4,272,128]{2,1,0:T(8,128)(2,1)S(1)} %pad_maximum_fusion.refs_1_), channel_id=1, source_target_pairs={{0,1},{1,0},{2,3},{3,2},{4,5},{5,4},{6,7},{7,6},{8,9},{9,8},{10,11... | collective-permute-start | bytes 835592 | tf_op jit(solution)/shard_map/ppermute | solution.py:663
  171.5 3.2 %collective-permute-start.34 = (bf16[4,272,128]{2,1,0:T(8,128)(2,1)S(1)}, bf16[4,272,128]{2,1,0:T(8,128)(2,1)S(1)}, u32[]{:S(2)}, u32[]{:S(2)}) collective-permute-start(bf16[4,272,128]{2,1,0:T(8,128)(2,1)S(1)} %collective-permute-done.30.refs_4_), channel_id=1, source_target_pairs={{0,1},{1,0},{2,3},{3,2},{4,5},{5,4},{6,7},{7,6},{8,9},{9,8},{10,11... | collective-permute-start | bytes 835592 | tf_op jit(solution)/shard_map/ppermute | solution.py:663
  173.5 1.6 collective-permute-start.33
  173.5 2.0 %collective-permute-start.32 = (bf16[4,272,128]{2,1,0:T(8,128)(2,1)S(1)}, bf16[4,272,128]{2,1,0:T(8,128)(2,1)S(1)}, u32[]{:S(2)}, u32[]{:S(2)}) collective-permute-start(bf16[4,272,128]{2,1,0:T(8,128)(2,1)S(1)} %collective-permute-done.28.refs_2_), channel_id=1, source_target_pairs={{0,1},{1,0},{2,3},{3,2},{4,5},{5,4},{6,7},{7,6},{8,9},{9,8},{10,11... | collective-permute-start | bytes 835592 | tf_op jit(solution)/shard_map/ppermute | solution.py:663
  (6 other events, 3.8 us)

commit v2 on v1

--- a/solution.py
+++ b/solution.py
@@ -138,25 +138,36 @@
 
 def text_grad_kernel(count, repeat, place, wo_far, mix, *refs):
     parts = refs[:count]
-    outs = refs[count : -3]
-    wo, total, sems = refs[-3:]
+    keep, send, wo, total, sems = refs[count:]
     groups, deep, _ = wo.shape
     moves = fetch([(wo_far.at[g * deep : (g + 1) * deep, :], wo.at[g]) for g in range(groups)], sems)
-    grad = gathered([part.at[2] for part in parts], place[2]).astype(BF16)
+    grad_t = gathered([part.at[2] for part in parts], place[2]).T.astype(BF16)
     for g in range(groups):
         moves[g].wait()
-        total[:, g * deep : (g + 1) * deep] = dot_nt(grad, wo[g])
-    for k, out in enumerate(outs):
-        peer = place[5] ^ k
-        rows = out.shape[0]
-        out[:, :HD] = total[:, pl.ds(pl.multiple_of(peer // repeat * HD, HD), HD)].astype(BF16)
-        out[:, HD:] = mix[pl.ds(pl.multiple_of(peer * rows, rows), rows), :]
+        total[g * deep : (g + 1) * deep, :] = dot(wo[g], grad_t)
+    pairs, rows, _ = keep.shape
+    for flip_core, out in enumerate((keep, send)):
+        for m in range(pairs):
+            peer = (place[3] ^ m) * 2 + (place[4] ^ flip_core)
+            out[m, :, :HD] = total[pl.ds(pl.multiple_of(peer // repeat * HD, HD), HD), :].T.astype(BF16)
+            out[m, :, HD:] = mix[pl.ds(pl.multiple_of(peer * rows, rows), rows), :]
+
+
+def merge_kernel(keep, received, *outs):
+    rows = keep.shape[1]
+    for m, out in enumerate(outs):
+        out[:rows, :] = keep[m]
+        out[rows:, :] = received[m]
+
+
+def by_peer(backs, rows):
+    return [backs[k // 2].at[k % 2 * rows : (k % 2 + 1) * rows, :] for k in range(2 * len(backs))]
 
 
 def text_out_kernel(repeat, peers, place, wo_far, *refs):
-    mixes = refs[:peers]
-    outs = refs[peers:-3]
+    outs = refs[peers // 2 : -3]
     wo, mixed, sems = refs[-3:]
+    mixes = by_peer(refs[: peers // 2], mixed.shape[0])
     groups, deep, width = wo.shape
     moves = fetch([(wo_far.at[g * deep : (g + 1) * deep, :], wo.at[g]) for g in range(groups)], sems)
     for k, mix in enumerate(mixes):
@@ -254,7 +265,7 @@
     whole = lambda a: pl.BlockSpec(a.shape, lambda b: (0,) * len(a.shape))
     outs = [(length, down_chan, F32), (down_chan, length, BF16), (taps, length, BF16), (length, HD, BF16),
             (HD, length, BF16), (length, HD, BF16), None, (length, HD, BF16), None]
-    per = 2
+    per = math.gcd(blocks, 4)
     flat = pl.BlockSpec((HD, per * length), lambda b: (0, b))
     return pl.pallas_call(
         lambda *refs: image_kernel(*sizes, *refs),
@@ -455,13 +466,12 @@
 
 
 def text_backward_kernel(place, thr, k_img, v_img, q_txt, qt_txt, mix_txt_t, lse_txt, *refs):
-    backs = refs[:-7]
     dk, dv, d_txt, *room = refs[-7:]
     text_total = q_txt.shape[0]
     total = k_img.shape[0]
     blocks = thr.shape[0]
     rows = text_total // blocks
-    for k, back in enumerate(backs):
+    for k, back in enumerate(by_peer(refs[:-7], rows)):
         d_txt[pl.ds(pl.multiple_of((place[5] ^ k) * rows, rows), rows), :] = back[:, :HD]
     d_txt_t = d_txt[...].astype(F32).T
     delta = jnp.sum(d_txt_t * mix_txt_t[...].astype(F32), axis=0, keepdims=True)
@@ -569,7 +579,7 @@
         )
 
     def step(n, carry):
-        for b in (n, blocks // 2 + n):
+        for b in (n, blocks // 4 + n, blocks // 2 + n, 3 * (blocks // 4) + n):
             conv, *more = block(b, dq[b])
             small_sum[:taps, :] += conv
             carry = tuple(a + m for a, m in zip(carry, more))
@@ -577,7 +587,7 @@
 
     rank = act_t.shape[1]
     spread, pull, inner = lax.fori_loop(
-        0, blocks // 2, step,
+        0, blocks // 4, step,
         (jnp.zeros((rank, 3 * HD), F32), jnp.zeros((rank, rank), F32), jnp.zeros((rank, grad_pre.shape[2]), F32)),
     )
     for move in moves[11:]:
@@ -738,12 +748,14 @@
     text_back = call(
         lambda *refs: text_grad_kernel(row_groups, repeat, *refs), head,
         [(w_out, pl.ANY), (mix_txt, None)] + [(a, None) for a in text_parts],
-        [bf(text_block, 2 * HD)] * blocks,
-        wo_room + [vmem((text_block, heads_here * HD), F32), dma(4)],
+        [bf(pairs, text_block, 2 * HD)] * 2,
+        wo_room + [vmem((heads_here * HD, text_block), F32), dma(4)],
         flops=2 * text_block * width * heads_here * HD,
         after=[part],
     )
-    text_back = [text_back[0]] + [hop(text_back[k], "sy", k) for k in range(1, blocks)]
+    keep, send = text_back
+    text_back = plain(merge_kernel, [keep, hop(send, "sy", 1)], [bf(2 * text_block, 2 * HD)] * pairs)
+    text_back = [text_back[0]] + [hop(text_back[m], "sy", 2 * m) for m in range(1, pairs)]
     grad_copies, prediction, grad_out_t = call(
         up_kernel, head,
         [(parts, None), (pre_down.reshape(devices, own_rows, down_chan), None), (z, None), (w_up_out, None),

time: 179 us -> 175 us (0.978)
  starting transfers between devices: 56.3 us -> 52.7 us
  Pallas kernels: 70.2 us -> 67 us
    ppermute x31 -> x28, starting transfers between devices: 33.2 us -> 29.6 us  [shards(): lax.ppermute(values, axis, [(i, i ^ by) for i in range(row_groups if axis...]
    pallas_call x8, Pallas kernels: 62.5 us -> 59.6 us  [call(): pl.pallas_call(lambda *refs: kernel(*refs[:count], *refs[skip:]), out_sha...]
    ppermute x31 -> x28, waiting for transfers between devices: 38.4 us -> 40 us  [shards(): lax.ppermute(values, axis, [(i, i ^ by) for i in range(row_groups if axis...]
    unnamed x65 -> x61, local copies, waits for them, and re-layouts: 3.58 us -> 4.97 us
  transfers between devices with their start and end apart: 38 -> 35, of which waited for: 19 -> 20; matrix products, arithmetic and copies ran while one was open for 3% -> 3% of each run, Pallas kernels for 20% -> 19%
where the time goes in v2:
time: 175 us; the launch traced here: 174 us
  Pallas kernels  67 us (38%)
  starting transfers between devices  52.7 us (30%)
  waiting for transfers between devices  41.5 us (24%)
  local copies, waits for them, and re-layouts  9.1 us (5%)
  other arithmetic  2.4 us (1%)
    pallas_call x8, Pallas kernels, call(): pl.pallas_call(lambda *refs: kernel(*refs[:count], *refs[skip:]), out_sha...  59.6 us
    ppermute x28, waiting for transfers between devices, shards(): lax.ppermute(values, axis, [(i, i ^ by) for i in range(row_groups if axis...  40 us
    ppermute x28, starting transfers between devices, shards(): lax.ppermute(values, axis, [(i, i ^ by) for i in range(row_groups if axis...  29.6 us
    ppermute x4, starting transfers between devices, shards(): lax.ppermute(values, 'sy', [(2 * z + c, c * pairs + (z ^ k)) for z in ran...  7.41 us
    pallas_call x1, Pallas kernels, image_rows(): pl.pallas_call(lambda *refs: image_kernel(*sizes, *refs), out_shape=[jax....  7 us
    all_to_all x1, starting transfers between devices, shards(): parts = lax.all_to_all(part.reshape(devices, own_rows, up_chan), axes, 0, 0)  6.38 us
    all_to_all x1, starting transfers between devices, spread_over(): lax.all_to_all(jnp.broadcast_to(values[None], (count,) + values.shape), a...  6.25 us
    unnamed x61, local copies, waits for them, and re-layouts  4.97 us
  transfers between devices with their start and end apart: 35, of which 20 were waited for; matrix products, arithmetic and copies ran while one was open for 3% of the time, Pallas kernels for 19%

profile of v2, /device:TPU:0, one launch (start us, length us, event | category | flops | bytes accessed | tf_op | source)
XLA Modules:
  0.0 174.4 jit_solution(3172583502310427607)
XLA Ops:
  0.6 0.5 collective-permute-start
  1.8 0.7 concatenate.3
  2.5 0.9 pad_maximum_fusion.1.refs_9_.refs_3_
  3.4 3.6 %collective-permute-start.3 = (bf16[3,8,4096]{2,1,0:T(8,128)(2,1)S(1)}, bf16[3,8,4096]{2,1,0:T(8,128)(2,1)S(1)}, u32[]{:S(2)}, u32[]{:S(2)}) collective-permute-start(bf16[3,8,4096]{2,1,0:T(8,128)(2,1)S(1)} %pad_maximum_fusion.1.refs_9_.refs_3_), channel_id=1, source_target_pairs={{0,24},{8,16},{16,8},{24,0},{1,25},{9,17},{17,9},{25,1},{2,26},{10... | collective-permute-start | bytes 589832 | tf_op jit(solution)/shard_map/ppermute | solution.py:673
  7.0 0.5 collective-permute-start.2
  7.7 0.6 stack.45.refs_0_
  8.3 0.7 broadcast_in_dim.7
  9.0 6.2 %all-to-all-start = ((bf16[32,4,640]{2,1,0:T(4,128)(2,1)}), bf16[32,4,640]{2,1,0:T(4,128)(2,1)S(1)}, u32[]{:S(2)}, u32[]{:S(2)}) async-start(bf16[32,4,640]{2,1,0:T(4,128)(2,1)} %broadcast_in_dim.7), calls=%async_computation | async-start | bytes 327680 | tf_op jit(solution)/shard_map/all_to_all | solution.py:669
  15.3 1.4 collective-permute-done.2.refs_11_.refs_5_
  17.7 9.6 %shard_map.235 = (bf16[128,384]{1,0:T(8,128)(2,1)}, bf16[384,128]{1,0:T(8,128)(2,1)}, bf16[128,640]{1,0:T(8,128)(2,1)}, bf16[128,128]{1,0:T(8,128)(2,1)}, bf16[1...) custom-call(s32[6]{0:T(128)} %stack.45.refs_0_, ...), custom_call_target="tpu_custom_call" | custom-call | flops 4805306368 | bytes 1597440 | tf_op jit(solution)/shard_map/pallas_call | solution.py:55
  27.4 2.0 %collective-permute-start.6 = (bf16[64,384]{1,0:T(8,128)(2,1)}, bf16[64,384]{1,0:T(8,128)(2,1)S(1)}, u32[]{:S(2)}, u32[]{:S(2)}) collective-permute-start(bf16[64,384]{1,0:T(8,128)(2,1)} %get-tuple-element.80), channel_id=1, source_target_pairs={{0,2},{1,6},{2,3},{3,7},{4,0},{5,4},{6,1},{7,5},{8,10},{9,14},{10,... | collective-permute-start | bytes 147464 | tf_op jit(solution)/shard_map/ppermute | solution.py:705
  29.4 3.9 %collective-permute-start.7 = (bf16[64,384]{1,0:T(8,128)(2,1)}, bf16[64,384]{1,0:T(8,128)(2,1)S(1)}, u32[]{:S(2)}, u32[]{:S(2)}) collective-permute-start(bf16[64,384]{1,0:T(8,128)(2,1)} %get-tuple-element.81), channel_id=1, source_target_pairs={{0,3},{1,7},{2,2},{3,6},{4,1},{5,5},{6,0},{7,4},{8,11},{9,15},{10,... | collective-permute-start | bytes 147464 | tf_op jit(solution)/shard_map/ppermute | solution.py:705
  33.3 1.5 collective-permute-start.4
  35.0 0.5 multiply_add_fusion.refs_0_.refs_1_
  35.8 1.0 copy.29
  36.9 7.0 %shard_map.236 = (f32[8,256,128]{2,1,0:T(8,128)}, bf16[8,128,256]{2,1,0:T(8,128)(2,1)}, bf16[8,288,256]{2,1,0:T(8,128)(2,1)}, bf16[8,256,128]{2,1,0:T(8,128)(2,1...) custom-call(s32[8]{0:T(128)} %multiply_add_fusion.refs_0_.refs_1_, ...), custom_call_target="tpu_custom_call" | custom-call | flops 8000000000 | bytes 8000000 | tf_op jit(solution)/shard_map/pallas_call | solution.py:270
  43.9 0.5 copy-done.26
  44.6 9.3 %shard_map.237 = (bf16[8,256,128]{2,1,0:T(8,128)(2,1)}, bf16[256,128]{1,0:T(8,128)(2,1)}, bf16[128,256]{1,0:T(8,128)(2,1)}, bf16[256,128]{1,0:T(8,128)(2,1)}, bf...) custom-call(s32[6]{0:T(128)} %stack.45.refs_0_, ...), custom_call_target="tpu_custom_call" | custom-call | flops 6000000000 | bytes 2270208 | tf_op jit(solution)/shard_map/pallas_call | solution.py:55
  53.9 6.4 %all-to-all-start.1 = ((bf16[32,64,128]{2,1,0:T(8,128)(2,1)}), bf16[32,64,128]{2,1,0:T(8,128)(2,1)S(1)}, u32[]{:S(2)}, u32[]{:S(2)}) async-start(bf16[32,64,128]{2,1,0:T(8,128)(2,1)} %bitcast.27), calls=%async_computation.1 | async-start | bytes 1048576 | tf_op jit(solution)/shard_map/all_to_all | solution.py:746
  60.3 6.5 %shard_map.238 = (bf16[4,32,256]{2,1,0:T(8,128)(2,1)}, bf16[4,32,256]{2,1,0:T(8,128)(2,1)}) custom-call(s32[6]{0:T(128)} %stack.45.refs_0_, bf16[1024,4096]{1,0:T(8,128)(2,1)} %refs_29_.1, bf16[256,128]{1,0:T(8,128)(2,1)} %get-tuple-element.85.refs_2_, bf16[3,8,4096]{2,1,0:T(8,128)(2,1)} %copy-done.11, bf16[3,8,4096]{2,1,0:T(8,128)(2,1)} %copy-done.14, ...), custom_call_target="tpu_custom_call" | custom-call | flops 268435456 | bytes 983040 | tf_op jit(solution)/shard_map/pallas_call | solution.py:55
  67.1 1.2 collective-permute-done.8.refs_1_
  68.3 0.8 copy-done.1
  69.2 0.6 copy-done.2
  69.8 1.8 %collective-permute-start.9 = (bf16[64,256]{1,0:T(8,128)(2,1)S(1)}, bf16[64,256]{1,0:T(8,128)(2,1)S(1)}, u32[]{:S(2)}, u32[]{:S(2)}) collective-permute-start(bf16[64,256]{1,0:T(8,128)(2,1)S(1)} %get-tuple-element.88), channel_id=1, source_target_pairs={{0,2},{1,3},{2,0},{3,1},{4,6},{5,7},{6,4},{7,5},{8,10},{9,11},{10,... | collective-permute-start | bytes 98312 | tf_op jit(solution)/shard_map/ppermute | solution.py:673
  71.6 2.4 %collective-permute-start.10 = (bf16[64,256]{1,0:T(8,128)(2,1)S(1)}, bf16[64,256]{1,0:T(8,128)(2,1)S(1)}, u32[]{:S(2)}, u32[]{:S(2)}) collective-permute-start(bf16[64,256]{1,0:T(8,128)(2,1)S(1)} %get-tuple-element.89), channel_id=1, source_target_pairs={{0,4},{1,5},{2,6},{3,7},{4,0},{5,1},{6,2},{7,3},{8,12},{9,13},{10,... | collective-permute-start | bytes 98312 | tf_op jit(solution)/shard_map/ppermute | solution.py:673
  74.4 2.5 %collective-permute-done.10.refs_7_.refs_4_.refs_10_ = bf16[64,256]{1,0:T(8,128)(2,1)S(1)} collective-permute-done((bf16[64,256]{1,0:T(8,128)(2,1)S(1)}, bf16[64,256]{1,0:T(8,128)(2,1)S(1)}, u32[]{:S(2)}, u32[]{:S(2)}) %collective-permute-start.10) | collective-permute-done | bytes 32800 | tf_op jit(solution)/shard_map/ppermute | solution.py:673
  77.0 2.7 %collective-permute-done.11.refs_8_.refs_5_.refs_11_ = bf16[64,256]{1,0:T(8,128)(2,1)S(1)} collective-permute-done((bf16[64,256]{1,0:T(8,128)(2,1)S(1)}, bf16[64,256]{1,0:T(8,128)(2,1)S(1)}, u32[]{:S(2)}, u32[]{:S(2)}) %collective-permute-start.11) | collective-permute-done | bytes 32800 | tf_op jit(solution)/shard_map/ppermute | solution.py:673
  79.7 1.6 shard_map.240
  81.4 3.0 %all-to-all-start.2 = ((bf16[32,64,128]{2,1,0:T(8,128)(2,1)}), bf16[32,64,128]{2,1,0:T(8,128)(2,1)S(1)}, u32[]{:S(2)}, u32[]{:S(2)}) async-start(bf16[32,64,128]{2,1,0:T(8,128)(2,1)} %get-tuple-element.93.refs_6_.refs_13_), calls=%async_computation.2 | async-start | bytes 1048576 | tf_op jit(solution)/shard_map/all_to_all | solution.py:768
  84.4 5.7 %shard_map.241 = (bf16[8,4096]{1,0:T(8,128)(2,1)}, bf16[8,4096]{1,0:T(8,128)(2,1)}, bf16[8,4096]{1,0:T(8,128)(2,1)}, bf16[8,4096]{1,0:T(8,128)(2,1)}) custom-call(s32[6]{0:T(128)} %stack.45.refs_0_, bf16[1024,4096]{1,0:T(8,128)(2,1)} %refs_29_.1, bf16[64,256]{1,0:T(8,128)(2,1)} %copy-done.2, bf16[64,256]{1,0:T(8,128)(2,1)} %copy-done.3, ...), custom_call_target="tpu_custom_call" | custom-call | flops 268435456 | bytes 393216 | tf_op jit(solution)/shard_map/pallas_call | solution.py:55
  90.1 1.6 collective-permute-start.12
  91.7 1.5 collective-permute-start.13
  93.2 0.5 collective-permute-start.14
  93.6 3.9 %shard_map.242 = (f32[2048,128]{1,0:T(8,128)}, f32[2048,128]{1,0:T(8,128)}) custom-call(s32[6]{0:T(128)} %stack.45.refs_0_, s32[8]{0:T(128)} %multiply_add_fusion.refs_0_.refs_1_, bf16[2048,128]{1,0:T(8,128)(2,1)} %bitcast.42, bf16[2048,128]{1,0:T(8,128)(2,1)} %bitcast.44, bf16[256,128]{1,0:T(8,128)(2,1)} %get-tuple-element.108.refs_4_, ...), custom_call_target="tpu_custom_call" | custom-call | flops 2000000000 | bytes 3474432 | tf_op jit(solution)/shard_map/pallas_call | solution.py:55
  97.6 1.3 collective-permute-done.14.refs_34_
  98.8 1.5 all-to-all-done.2
  100.4 0.8 copy-done.15
  101.2 20.2 %shard_map.243 = (bf16[4,4,272,128]{3,2,1,0:T(8,128)(2,1)}, bf16[4,4,272,128]{3,2,1,0:T(8,128)(2,1)}) custom-call(s32[6]{0:T(128)} %stack.45.refs_0_, s32[8]{0:T(128)} %multiply_add_fusion.refs_0_.refs_1_, bf16[8,256,128]{2,1,0:T(8,128)(2,1)} %bitcast.30, bf16[256,128]{1,0:T(8,128)(2,1)} %get-tuple-element.98.refs_3_, ...), custom_call_target="tpu_custom_call" | custom-call | flops 30000001024 | bytes 3710976 | tf_op jit(solution)/shard_map/pallas_call | solution.py:55
  121.5 3.0 %collective-permute-done.15.refs_1_ = bf16[4,4,272,128]{3,2,1,0:T(8,128)(2,1)S(1)} collective-permute-done((bf16[4,4,272,128]{3,2,1,0:T(8,128)(2,1)}, bf16[4,4,272,128]{3,2,1,0:T(8,128)(2,1)S(1)}, u32[]{:S(2)}, u32[]{:S(2)}) %collective-permute-start.15) | collective-permute-done | bytes 1114144 | tf_op jit(solution)/shard_map/ppermute | solution.py:673
  124.5 1.2 copy-done
  126.3 1.5 collective-permute-start.17
  127.8 1.8 %collective-permute-start.18 = (bf16[4,272,128]{2,1,0:T(8,128)(2,1)S(1)}, bf16[4,272,128]{2,1,0:T(8,128)(2,1)S(1)}, u32[]{:S(2)}, u32[]{:S(2)}) collective-permute-start(bf16[4,272,128]{2,1,0:T(8,128)(2,1)S(1)} %get-tuple-element.121), channel_id=1, source_target_pairs={{0,24},{8,16},{16,8},{24,0},{1,25},{9,17},{17,9},{25,1},{2,26},{10... | collective-permute-start | bytes 835592 | tf_op jit(solution)/shard_map/ppermute | solution.py:673
  129.6 6.0 %collective-permute-done.16.refs_1_ = bf16[4,272,128]{2,1,0:T(8,128)(2,1)S(1)} collective-permute-done((bf16[4,272,128]{2,1,0:T(8,128)(2,1)S(1)}, bf16[4,272,128]{2,1,0:T(8,128)(2,1)S(1)}, u32[]{:S(2)}, u32[]{:S(2)}) %collective-permute-start.16) | collective-permute-done | bytes 278560 | tf_op jit(solution)/shard_map/ppermute | solution.py:673
  135.6 5.2 %collective-permute-done.18.refs_3_ = bf16[4,272,128]{2,1,0:T(8,128)(2,1)S(1)} collective-permute-done((bf16[4,272,128]{2,1,0:T(8,128)(2,1)S(1)}, bf16[4,272,128]{2,1,0:T(8,128)(2,1)S(1)}, u32[]{:S(2)}, u32[]{:S(2)}) %collective-permute-start.18) | collective-permute-done | bytes 278560 | tf_op jit(solution)/shard_map/ppermute | solution.py:673
  141.0 1.0 collective-permute-start.19
  142.0 1.7 collective-permute-start.20
  143.7 1.7 collective-permute-start.21
  145.7 3.2 %collective-permute-done.20.refs_2_ = bf16[272,128]{1,0:T(8,128)(2,1)S(1)} collective-permute-done((bf16[272,128]{1,0:T(8,128)(2,1)S(1)}, bf16[272,128]{1,0:T(8,128)(2,1)S(1)}, u32[]{:S(2)}, u32[]{:S(2)}) %collective-permute-start.20) | collective-permute-done | bytes 69664 | tf_op jit(solution)/shard_map/ppermute | solution.py:673
  148.9 1.0 collective-permute-done.21.refs_3_
  150.0 1.8 %collective-permute-start.24 = (bf16[272,128]{1,0:T(8,128)(2,1)S(1)}, bf16[272,128]{1,0:T(8,128)(2,1)S(1)}, u32[]{:S(2)}, u32[]{:S(2)}) collective-permute-start(bf16[272,128]{1,0:T(8,128)(2,1)S(1)} %shard_map.246), channel_id=1, source_target_pairs={{0,6},{1,7},{2,4},{3,5},{4,2},{5,3},{6,0},{7,1},{8,14},{9,15},{10,... | collective-permute-start | bytes 208904 | tf_op jit(solution)/shard_map/ppermute | solution.py:673
  151.8 1.2 collective-permute-start.23
  152.9 1.5 collective-permute-start.22
  154.4 1.8 %collective-permute-done.24 = bf16[272,128]{1,0:T(8,128)(2,1)S(1)} collective-permute-done((bf16[272,128]{1,0:T(8,128)(2,1)S(1)}, bf16[272,128]{1,0:T(8,128)(2,1)S(1)}, u32[]{:S(2)}, u32[]{:S(2)}) %collective-permute-start.24) | collective-permute-done | bytes 69664 | tf_op jit(solution)/shard_map/ppermute | solution.py:673
  156.3 1.5 collective-permute-done.23
  157.8 1.7 collective-permute-start.27
  159.5 1.1 collective-permute-start.26
  160.6 0.7 collective-permute-start.25
  161.4 0.7 reshape.49
  162.1 5.5 %collective-permute-done.27.refs_4_ = bf16[4,272,128]{2,1,0:T(8,128)(2,1)S(1)} collective-permute-done((bf16[4,272,128]{2,1,0:T(8,128)(2,1)S(1)}, bf16[4,272,128]{2,1,0:T(8,128)(2,1)S(1)}, u32[]{:S(2)}, u32[]{:S(2)}) %collective-permute-start.27) | collective-permute-done | bytes 278560 | tf_op jit(solution)/shard_map/ppermute | solution.py:673
  167.6 2.1 %collective-permute-done.26.refs_3_ = bf16[4,272,128]{2,1,0:T(8,128)(2,1)S(1)} collective-permute-done((bf16[4,272,128]{2,1,0:T(8,128)(2,1)S(1)}, bf16[4,272,128]{2,1,0:T(8,128)(2,1)S(1)}, u32[]{:S(2)}, u32[]{:S(2)}) %collective-permute-start.26) | collective-permute-done | bytes 278560 | tf_op jit(solution)/shard_map/ppermute | solution.py:673
  169.7 0.5 collective-permute-start.29
  170.2 0.7 fusion
  171.2 0.4 collective-permute-done.29.refs_6_
  171.6 2.8 %shard_map.247 = (f32[288,128]{1,0:T(8,128)}, f32[128,4096]{1,0:T(8,128)}, f32[4096,128]{1,0:T(8,128)}, f32[32,128]{1,0:T(8,128)}) custom-call(s32[6]{0:T(128)S(1)} %copy-done.7, bf16[4,272,128]{2,1,0:T(8,128)(2,1)S(1)} %pad_maximum_fusion.refs_1_, bf16[4,272,128]{2,1,0:T(8,128)(2,1)S(1)} %collective-permute-done.25.refs_2_, ...), custom_call_target="tpu_custom_call" | custom-call | bytes 6586368 | tf_op jit(solution)/shard_map/pallas_call | solution.py:55
  (93 shorter events, 4.2 us)
Async XLA Ops:
  0.6 1.9 %collective-permute-start = (bf16[8,4096]{1,0:T(8,128)(2,1)}, bf16[8,4096]{1,0:T(8,128)(2,1)S(1)}, u32[]{:S(2)}, u32[]{:S(2)}) collective-permute-start(bf16[8,4096]{1,0:T(8,128)(2,1)} %bitcast.32), channel_id=1, source_target_pairs={{0,1},{1,0},{2,3},{3,2},{4,5},{5,4},{6,7},{7,6},{8,9},{9,8},{10,11... | collective-permute-start | bytes 196616 | tf_op jit(solution)/shard_map/ppermute | solution.py:673
  3.4 13.6 %copy-start.11 = (bf16[3,8,4096]{2,1,0:T(8,128)(2,1)}, bf16[3,8,4096]{2,1,0:T(8,128)(2,1)S(1)}, u32[]{:S(2)}) copy-start(bf16[3,8,4096]{2,1,0:T(8,128)(2,1)S(1)} %pad_maximum_fusion.1.refs_9_.refs_3_) | copy-start | bytes 589828
  3.4 11.9 %collective-permute-start.3 = (bf16[3,8,4096]{2,1,0:T(8,128)(2,1)S(1)}, bf16[3,8,4096]{2,1,0:T(8,128)(2,1)S(1)}, u32[]{:S(2)}, u32[]{:S(2)}) collective-permute-start(bf16[3,8,4096]{2,1,0:T(8,128)(2,1)S(1)} %pad_maximum_fusion.1.refs_9_.refs_3_), channel_id=1, source_target_pairs={{0,24},{8,16},{16,8},{24,0},{1,25},{9,17},{17,9},{25,1},{2,26},{10... | collective-permute-start | bytes 589832 | tf_op jit(solution)/shard_map/ppermute | solution.py:673
  7.0 9.7 %collective-permute-start.2 = (bf16[3,8,4096]{2,1,0:T(8,128)(2,1)S(1)}, bf16[3,8,4096]{2,1,0:T(8,128)(2,1)S(1)}, u32[]{:S(2)}, u32[]{:S(2)}) collective-permute-start(bf16[3,8,4096]{2,1,0:T(8,128)(2,1)S(1)} %pad_maximum_fusion.1.refs_9_.refs_3_), channel_id=1, source_target_pairs={{0,16},{8,24},{16,0},{24,8},{1,17},{9,25},{17,1},{25,9},{2,18},{10... | collective-permute-start | bytes 589832 | tf_op jit(solution)/shard_map/ppermute | solution.py:673
  7.5 9.5 %collective-permute-start.1 = (bf16[3,8,4096]{2,1,0:T(8,128)(2,1)S(1)}, bf16[3,8,4096]{2,1,0:T(8,128)(2,1)S(1)}, u32[]{:S(2)}, u32[]{:S(2)}) collective-permute-start(bf16[3,8,4096]{2,1,0:T(8,128)(2,1)S(1)} %pad_maximum_fusion.1.refs_9_.refs_3_), channel_id=1, source_target_pairs={{0,8},{8,0},{16,24},{24,16},{1,9},{9,1},{17,25},{25,17},{2,10},{10... | collective-permute-start | bytes 589832 | tf_op jit(solution)/shard_map/ppermute | solution.py:673
  9.0 25.7 %all-to-all-start = ((bf16[32,4,640]{2,1,0:T(4,128)(2,1)}), bf16[32,4,640]{2,1,0:T(4,128)(2,1)S(1)}, u32[]{:S(2)}, u32[]{:S(2)}) async-start(bf16[32,4,640]{2,1,0:T(4,128)(2,1)} %broadcast_in_dim.7), calls=%async_computation | async-start | bytes 327680 | tf_op jit(solution)/shard_map/all_to_all | solution.py:669
  15.3 1.8 %copy-start.12 = (bf16[3,8,4096]{2,1,0:T(8,128)(2,1)}, bf16[3,8,4096]{2,1,0:T(8,128)(2,1)S(1)}, u32[]{:S(2)}) copy-start(bf16[3,8,4096]{2,1,0:T(8,128)(2,1)S(1)} %collective-permute-done.3.refs_12_.refs_6_) | copy-start | bytes 589828
  16.7 0.7 copy-start.13
  17.0 0.7 copy-start.14
  27.3 16.6 %collective-permute-start.5 = (bf16[64,384]{1,0:T(8,128)(2,1)}, bf16[64,384]{1,0:T(8,128)(2,1)S(1)}, u32[]{:S(2)}, u32[]{:S(2)}) collective-permute-start(bf16[64,384]{1,0:T(8,128)(2,1)} %get-tuple-element.79), channel_id=1, source_target_pairs={{0,1},{1,5},{2,0},{3,4},{4,3},{5,7},{6,2},{7,6},{8,9},{9,13},{10,8... | collective-permute-start | bytes 147464 | tf_op jit(solution)/shard_map/ppermute | solution.py:705
  27.4 16.5 %collective-permute-start.6 = (bf16[64,384]{1,0:T(8,128)(2,1)}, bf16[64,384]{1,0:T(8,128)(2,1)S(1)}, u32[]{:S(2)}, u32[]{:S(2)}) collective-permute-start(bf16[64,384]{1,0:T(8,128)(2,1)} %get-tuple-element.80), channel_id=1, source_target_pairs={{0,2},{1,6},{2,3},{3,7},{4,0},{5,4},{6,1},{7,5},{8,10},{9,14},{10,... | collective-permute-start | bytes 147464 | tf_op jit(solution)/shard_map/ppermute | solution.py:705
  29.4 14.5 %collective-permute-start.7 = (bf16[64,384]{1,0:T(8,128)(2,1)}, bf16[64,384]{1,0:T(8,128)(2,1)S(1)}, u32[]{:S(2)}, u32[]{:S(2)}) collective-permute-start(bf16[64,384]{1,0:T(8,128)(2,1)} %get-tuple-element.81), channel_id=1, source_target_pairs={{0,3},{1,7},{2,2},{3,6},{4,1},{5,5},{6,0},{7,4},{8,11},{9,15},{10,... | collective-permute-start | bytes 147464 | tf_op jit(solution)/shard_map/ppermute | solution.py:705
  33.3 10.7 %collective-permute-start.4 = (bf16[64,384]{1,0:T(8,128)(2,1)}, bf16[64,384]{1,0:T(8,128)(2,1)S(1)}, u32[]{:S(2)}, u32[]{:S(2)}) collective-permute-start(bf16[64,384]{1,0:T(8,128)(2,1)} %get-tuple-element.75.refs_10_), channel_id=1, source_target_pairs={{0,0},{1,4},{2,1},{3,5},{4,2},{5,6},{6,3},{7,7},{8,8},{9,12},{10,9... | collective-permute-start | bytes 147464 | tf_op jit(solution)/shard_map/ppermute | solution.py:705
  43.9 0.6 copy-start.26
  43.9 0.6 copy-start.27
  43.9 0.6 copy-start.28
  43.9 0.6 copy-start.29
  53.9 25.8 %all-to-all-start.1 = ((bf16[32,64,128]{2,1,0:T(8,128)(2,1)}), bf16[32,64,128]{2,1,0:T(8,128)(2,1)S(1)}, u32[]{:S(2)}, u32[]{:S(2)}) async-start(bf16[32,64,128]{2,1,0:T(8,128)(2,1)} %bitcast.27), calls=%async_computation.1 | async-start | bytes 1048576 | tf_op jit(solution)/shard_map/all_to_all | solution.py:746
  60.3 13.9 %copy-start.25 = (bf16[1,4,512]{2,1,0:T(4,128)(2,1)S(1)}, bf16[1,4,512]{2,1,0:T(4,128)(2,1)}, u32[]{:S(2)}) copy-start(bf16[1,4,512]{2,1,0:T(4,128)(2,1)} %param.32) | copy-start | bytes 12292
  60.3 14.0 %copy-start.24 = (bf16[128,32]{0,1:T(8,128)(2,1)S(1)}, bf16[128,32]{0,1:T(8,128)(2,1)}, u32[]{:S(2)}) copy-start(bf16[128,32]{0,1:T(8,128)(2,1)} %param.31) | copy-start | bytes 24580
  60.3 19.4 %copy-start.6 = (s32[6]{0:T(128)S(1)}, s32[6]{0:T(128)}, u32[]{:S(2)}) copy-start(s32[6]{0:T(128)} %stack.45.refs_0_) | copy-start | bytes 76
  60.3 19.4 %copy-start.8 = (bf16[128,128]{1,0:T(8,128)(2,1)S(1)}, bf16[128,128]{1,0:T(8,128)(2,1)}, u32[]{:S(2)}) copy-start(bf16[128,128]{1,0:T(8,128)(2,1)} %get-tuple-element.84.refs_3_.refs_10_) | copy-start | bytes 98308
  60.3 19.4 %copy-start.9 = (f32[8,256,128]{2,1,0:T(8,128)S(1)}, f32[8,256,128]{2,1,0:T(8,128)}, u32[]{:S(2)}) copy-start(f32[8,256,128]{2,1,0:T(8,128)} %get-tuple-element.83.refs_23_) | copy-start | bytes 3145732
  66.8 1.5 collective-permute-start.8
  68.3 0.8 copy-start.1
  69.8 4.6 %collective-permute-start.9 = (bf16[64,256]{1,0:T(8,128)(2,1)S(1)}, bf16[64,256]{1,0:T(8,128)(2,1)S(1)}, u32[]{:S(2)}, u32[]{:S(2)}) collective-permute-start(bf16[64,256]{1,0:T(8,128)(2,1)S(1)} %get-tuple-element.88), channel_id=1, source_target_pairs={{0,2},{1,3},{2,0},{3,1},{4,6},{5,7},{6,4},{7,5},{8,10},{9,11},{10,... | collective-permute-start | bytes 98312 | tf_op jit(solution)/shard_map/ppermute | solution.py:673
  71.6 5.4 %collective-permute-start.10 = (bf16[64,256]{1,0:T(8,128)(2,1)S(1)}, bf16[64,256]{1,0:T(8,128)(2,1)S(1)}, u32[]{:S(2)}, u32[]{:S(2)}) collective-permute-start(bf16[64,256]{1,0:T(8,128)(2,1)S(1)} %get-tuple-element.89), channel_id=1, source_target_pairs={{0,4},{1,5},{2,6},{3,7},{4,0},{5,1},{6,2},{7,3},{8,12},{9,13},{10,... | collective-permute-start | bytes 98312 | tf_op jit(solution)/shard_map/ppermute | solution.py:673
  74.0 5.7 %collective-permute-start.11 = (bf16[64,256]{1,0:T(8,128)(2,1)S(1)}, bf16[64,256]{1,0:T(8,128)(2,1)S(1)}, u32[]{:S(2)}, u32[]{:S(2)}) collective-permute-start(bf16[64,256]{1,0:T(8,128)(2,1)S(1)} %get-tuple-element.90), channel_id=1, source_target_pairs={{0,6},{1,7},{2,4},{3,5},{4,2},{5,3},{6,0},{7,1},{8,14},{9,15},{10,... | collective-permute-start | bytes 98312 | tf_op jit(solution)/shard_map/ppermute | solution.py:673
  74.4 6.9 %copy-start.3 = (bf16[64,256]{1,0:T(8,128)(2,1)}, bf16[64,256]{1,0:T(8,128)(2,1)S(1)}, u32[]{:S(2)}) copy-start(bf16[64,256]{1,0:T(8,128)(2,1)S(1)} %collective-permute-done.9.refs_6_.refs_3_.refs_9_) | copy-start | bytes 98308
  77.0 4.4 %copy-start.4 = (bf16[64,256]{1,0:T(8,128)(2,1)}, bf16[64,256]{1,0:T(8,128)(2,1)S(1)}, u32[]{:S(2)}) copy-start(bf16[64,256]{1,0:T(8,128)(2,1)S(1)} %collective-permute-done.10.refs_7_.refs_4_.refs_10_) | copy-start | bytes 98308
  79.7 1.6 copy-start.5
  81.3 8.7 %copy-start.10 = (f32[32,128]{1,0:T(8,128)}, f32[32,128]{1,0:T(8,128)S(1)}, u32[]{:S(2)}) copy-start(f32[32,128]{1,0:T(8,128)S(1)} %get-tuple-element.103.refs_14_) | copy-start | bytes 49156
  81.4 19.0 %all-to-all-start.2 = ((bf16[32,64,128]{2,1,0:T(8,128)(2,1)}), bf16[32,64,128]{2,1,0:T(8,128)(2,1)S(1)}, u32[]{:S(2)}, u32[]{:S(2)}) async-start(bf16[32,64,128]{2,1,0:T(8,128)(2,1)} %get-tuple-element.93.refs_6_.refs_13_), calls=%async_computation.2 | async-start | bytes 1048576 | tf_op jit(solution)/shard_map/all_to_all | solution.py:768
  90.1 7.4 %collective-permute-start.12 = (bf16[8,4096]{1,0:T(8,128)(2,1)}, bf16[8,4096]{1,0:T(8,128)(2,1)S(1)}, u32[]{:S(2)}, u32[]{:S(2)}) collective-permute-start(bf16[8,4096]{1,0:T(8,128)(2,1)} %get-tuple-element.95), channel_id=1, source_target_pairs={{0,8},{8,0},{16,24},{24,16},{1,9},{9,1},{17,25},{25,17},{2,10},{10... | collective-permute-start | bytes 196616 | tf_op jit(solution)/shard_map/ppermute | solution.py:673
  91.7 5.9 %collective-permute-start.13 = (bf16[8,4096]{1,0:T(8,128)(2,1)}, bf16[8,4096]{1,0:T(8,128)(2,1)S(1)}, u32[]{:S(2)}, u32[]{:S(2)}) collective-permute-start(bf16[8,4096]{1,0:T(8,128)(2,1)} %get-tuple-element.96), channel_id=1, source_target_pairs={{0,16},{8,24},{16,0},{24,8},{1,17},{9,25},{17,1},{25,9},{2,18},{10... | collective-permute-start | bytes 196616 | tf_op jit(solution)/shard_map/ppermute | solution.py:673
  93.2 5.7 %collective-permute-start.14 = (bf16[8,4096]{1,0:T(8,128)(2,1)}, bf16[8,4096]{1,0:T(8,128)(2,1)S(1)}, u32[]{:S(2)}, u32[]{:S(2)}) collective-permute-start(bf16[8,4096]{1,0:T(8,128)(2,1)} %get-tuple-element.97), channel_id=1, source_target_pairs={{0,24},{8,16},{16,8},{24,0},{1,25},{9,17},{17,9},{25,1},{2,26},{10... | collective-permute-start | bytes 196616 | tf_op jit(solution)/shard_map/ppermute | solution.py:673
  97.5 2.9 %copy-start.18 = (bf16[8,4096]{1,0:T(8,128)(2,1)}, bf16[8,4096]{1,0:T(8,128)(2,1)S(1)}, u32[]{:S(2)}) copy-start(bf16[8,4096]{1,0:T(8,128)(2,1)S(1)} %collective-permute-done.12.refs_32_) | copy-start | bytes 196612
  97.6 2.8 %copy-start.20 = (bf16[8,4096]{1,0:T(8,128)(2,1)}, bf16[8,4096]{1,0:T(8,128)(2,1)S(1)}, u32[]{:S(2)}) copy-start(bf16[8,4096]{1,0:T(8,128)(2,1)S(1)} %collective-permute-done.13.refs_33_) | copy-start | bytes 196612
  98.8 1.6 copy-start.22
  100.4 0.8 copy-start.15
  121.5 3.0 %collective-permute-start.15 = (bf16[4,4,272,128]{3,2,1,0:T(8,128)(2,1)}, bf16[4,4,272,128]{3,2,1,0:T(8,128)(2,1)S(1)}, u32[]{:S(2)}, u32[]{:S(2)}) collective-permute-start(bf16[4,4,272,128]{3,2,1,0:T(8,128)(2,1)} %get-tuple-element.117), channel_id=1, source_target_pairs={{0,1},{1,0},{2,3},{3,2},{4,5},{5,4},{6,7},{7,6},{8,9},{9,8},{10,11... | collective-permute-start | bytes 3342344 | tf_op jit(solution)/shard_map/ppermute | solution.py:673
  124.5 1.2 copy-start
  125.7 44.4 %copy-start.16 = (bf16[1,8,4096]{2,1,0:T(8,128)(2,1)S(1)}, bf16[1,8,4096]{2,1,0:T(8,128)(2,1)}, u32[]{:S(2)}) copy-start(bf16[1,8,4096]{2,1,0:T(8,128)(2,1)} %param.20) | copy-start | bytes 196612
  125.7 44.4 %copy-start.17 = (bf16[8,4096]{1,0:T(8,128)(2,1)S(1)}, bf16[8,4096]{1,0:T(8,128)(2,1)}, u32[]{:S(2)}) copy-start(bf16[8,4096]{1,0:T(8,128)(2,1)} %get-tuple-element.94.refs_12_) | copy-start | bytes 196612
  125.7 44.4 %copy-start.19 = (bf16[8,4096]{1,0:T(8,128)(2,1)S(1)}, bf16[8,4096]{1,0:T(8,128)(2,1)}, u32[]{:S(2)}) copy-start(bf16[8,4096]{1,0:T(8,128)(2,1)} %copy-done.18) | copy-start | bytes 196612
  125.7 44.4 %copy-start.21 = (bf16[8,4096]{1,0:T(8,128)(2,1)S(1)}, bf16[8,4096]{1,0:T(8,128)(2,1)}, u32[]{:S(2)}) copy-start(bf16[8,4096]{1,0:T(8,128)(2,1)} %copy-done.20) | copy-start | bytes 196612
  125.8 44.4 %copy-start.23 = (bf16[8,4096]{1,0:T(8,128)(2,1)S(1)}, bf16[8,4096]{1,0:T(8,128)(2,1)}, u32[]{:S(2)}) copy-start(bf16[8,4096]{1,0:T(8,128)(2,1)} %copy-done.22) | copy-start | bytes 196612
  125.8 45.9 %copy-start.7 = (s32[6]{0:T(128)S(1)}, s32[6]{0:T(128)}, u32[]{:S(2)}) copy-start(s32[6]{0:T(128)} %stack.45.refs_0_) | copy-start | bytes 76
  126.0 9.6 %collective-permute-start.16 = (bf16[4,272,128]{2,1,0:T(8,128)(2,1)S(1)}, bf16[4,272,128]{2,1,0:T(8,128)(2,1)S(1)}, u32[]{:S(2)}, u32[]{:S(2)}) collective-permute-start(bf16[4,272,128]{2,1,0:T(8,128)(2,1)S(1)} %get-tuple-element.119), channel_id=1, source_target_pairs={{0,8},{8,0},{16,24},{24,16},{1,9},{9,1},{17,25},{25,17},{2,10},{10... | collective-permute-start | bytes 835592 | tf_op jit(solution)/shard_map/ppermute | solution.py:673
  126.3 9.3 %collective-permute-start.17 = (bf16[4,272,128]{2,1,0:T(8,128)(2,1)S(1)}, bf16[4,272,128]{2,1,0:T(8,128)(2,1)S(1)}, u32[]{:S(2)}, u32[]{:S(2)}) collective-permute-start(bf16[4,272,128]{2,1,0:T(8,128)(2,1)S(1)} %get-tuple-element.120), channel_id=1, source_target_pairs={{0,16},{8,24},{16,0},{24,8},{1,17},{9,25},{17,1},{25,9},{2,18},{10... | collective-permute-start | bytes 835592 | tf_op jit(solution)/shard_map/ppermute | solution.py:673
  127.8 13.0 %collective-permute-start.18 = (bf16[4,272,128]{2,1,0:T(8,128)(2,1)S(1)}, bf16[4,272,128]{2,1,0:T(8,128)(2,1)S(1)}, u32[]{:S(2)}, u32[]{:S(2)}) collective-permute-start(bf16[4,272,128]{2,1,0:T(8,128)(2,1)S(1)} %get-tuple-element.121), channel_id=1, source_target_pairs={{0,24},{8,16},{16,8},{24,0},{1,25},{9,17},{17,9},{25,1},{2,26},{10... | collective-permute-start | bytes 835592 | tf_op jit(solution)/shard_map/ppermute | solution.py:673
  141.0 4.7 %collective-permute-start.19 = (bf16[272,128]{1,0:T(8,128)(2,1)S(1)}, bf16[272,128]{1,0:T(8,128)(2,1)S(1)}, u32[]{:S(2)}, u32[]{:S(2)}) collective-permute-start(bf16[272,128]{1,0:T(8,128)(2,1)S(1)} %get-tuple-element.123), channel_id=1, source_target_pairs={{0,2},{1,3},{2,0},{3,1},{4,6},{5,7},{6,4},{7,5},{8,10},{9,11},{10,... | collective-permute-start | bytes 208904 | tf_op jit(solution)/shard_map/ppermute | solution.py:673
  142.0 6.9 %collective-permute-start.20 = (bf16[272,128]{1,0:T(8,128)(2,1)S(1)}, bf16[272,128]{1,0:T(8,128)(2,1)S(1)}, u32[]{:S(2)}, u32[]{:S(2)}) collective-permute-start(bf16[272,128]{1,0:T(8,128)(2,1)S(1)} %get-tuple-element.124), channel_id=1, source_target_pairs={{0,4},{1,5},{2,6},{3,7},{4,0},{5,1},{6,2},{7,3},{8,12},{9,13},{10,... | collective-permute-start | bytes 208904 | tf_op jit(solution)/shard_map/ppermute | solution.py:673
  143.7 6.2 %collective-permute-start.21 = (bf16[272,128]{1,0:T(8,128)(2,1)S(1)}, bf16[272,128]{1,0:T(8,128)(2,1)S(1)}, u32[]{:S(2)}, u32[]{:S(2)}) collective-permute-start(bf16[272,128]{1,0:T(8,128)(2,1)S(1)} %get-tuple-element.125), channel_id=1, source_target_pairs={{0,6},{1,7},{2,4},{3,5},{4,2},{5,3},{6,0},{7,1},{8,14},{9,15},{10,... | collective-permute-start | bytes 208904 | tf_op jit(solution)/shard_map/ppermute | solution.py:673
  150.0 6.3 %collective-permute-start.24 = (bf16[272,128]{1,0:T(8,128)(2,1)S(1)}, bf16[272,128]{1,0:T(8,128)(2,1)S(1)}, u32[]{:S(2)}, u32[]{:S(2)}) collective-permute-start(bf16[272,128]{1,0:T(8,128)(2,1)S(1)} %shard_map.246), channel_id=1, source_target_pairs={{0,6},{1,7},{2,4},{3,5},{4,2},{5,3},{6,0},{7,1},{8,14},{9,15},{10,... | collective-permute-start | bytes 208904 | tf_op jit(solution)/shard_map/ppermute | solution.py:673
  151.8 6.0 %collective-permute-start.23 = (bf16[272,128]{1,0:T(8,128)(2,1)S(1)}, bf16[272,128]{1,0:T(8,128)(2,1)S(1)}, u32[]{:S(2)}, u32[]{:S(2)}) collective-permute-start(bf16[272,128]{1,0:T(8,128)(2,1)S(1)} %shard_map.246), channel_id=1, source_target_pairs={{0,4},{1,5},{2,6},{3,7},{4,0},{5,1},{6,2},{7,3},{8,12},{9,13},{10,... | collective-permute-start | bytes 208904 | tf_op jit(solution)/shard_map/ppermute | solution.py:673
  152.9 4.8 %collective-permute-start.22 = (bf16[272,128]{1,0:T(8,128)(2,1)S(1)}, bf16[272,128]{1,0:T(8,128)(2,1)S(1)}, u32[]{:S(2)}, u32[]{:S(2)}) collective-permute-start(bf16[272,128]{1,0:T(8,128)(2,1)S(1)} %shard_map.246), channel_id=1, source_target_pairs={{0,2},{1,3},{2,0},{3,1},{4,6},{5,7},{6,4},{7,5},{8,10},{9,11},{10,... | collective-permute-start | bytes 208904 | tf_op jit(solution)/shard_map/ppermute | solution.py:673
  157.8 9.8 %collective-permute-start.27 = (bf16[4,272,128]{2,1,0:T(8,128)(2,1)S(1)}, bf16[4,272,128]{2,1,0:T(8,128)(2,1)S(1)}, u32[]{:S(2)}, u32[]{:S(2)}) collective-permute-start(bf16[4,272,128]{2,1,0:T(8,128)(2,1)S(1)} %pad_maximum_fusion.refs_1_), channel_id=1, source_target_pairs={{0,24},{8,16},{16,8},{24,0},{1,25},{9,17},{17,9},{25,1},{2,26},{10... | collective-permute-start | bytes 835592 | tf_op jit(solution)/shard_map/ppermute | solution.py:673
  159.5 10.2 %collective-permute-start.26 = (bf16[4,272,128]{2,1,0:T(8,128)(2,1)S(1)}, bf16[4,272,128]{2,1,0:T(8,128)(2,1)S(1)}, u32[]{:S(2)}, u32[]{:S(2)}) collective-permute-start(bf16[4,272,128]{2,1,0:T(8,128)(2,1)S(1)} %pad_maximum_fusion.refs_1_), channel_id=1, source_target_pairs={{0,16},{8,24},{16,0},{24,8},{1,17},{9,25},{17,1},{25,9},{2,18},{10... | collective-permute-start | bytes 835592 | tf_op jit(solution)/shard_map/ppermute | solution.py:673
  160.6 9.0 %collective-permute-start.25 = (bf16[4,272,128]{2,1,0:T(8,128)(2,1)S(1)}, bf16[4,272,128]{2,1,0:T(8,128)(2,1)S(1)}, u32[]{:S(2)}, u32[]{:S(2)}) collective-permute-start(bf16[4,272,128]{2,1,0:T(8,128)(2,1)S(1)} %pad_maximum_fusion.refs_1_), channel_id=1, source_target_pairs={{0,8},{8,0},{16,24},{24,16},{1,9},{9,1},{17,25},{25,17},{2,10},{10... | collective-permute-start | bytes 835592 | tf_op jit(solution)/shard_map/ppermute | solution.py:673
  162.1 8.8 %collective-permute-start.28 = (bf16[4,272,128]{2,1,0:T(8,128)(2,1)S(1)}, bf16[4,272,128]{2,1,0:T(8,128)(2,1)S(1)}, u32[]{:S(2)}, u32[]{:S(2)}) collective-permute-start(bf16[4,272,128]{2,1,0:T(8,128)(2,1)S(1)} %pad_maximum_fusion.refs_1_), channel_id=1, source_target_pairs={{0,1},{1,0},{2,3},{3,2},{4,5},{5,4},{6,7},{7,6},{8,9},{9,8},{10,11... | collective-permute-start | bytes 835592 | tf_op jit(solution)/shard_map/ppermute | solution.py:673
  167.6 3.3 %collective-permute-start.31 = (bf16[4,272,128]{2,1,0:T(8,128)(2,1)S(1)}, bf16[4,272,128]{2,1,0:T(8,128)(2,1)S(1)}, u32[]{:S(2)}, u32[]{:S(2)}) collective-permute-start(bf16[4,272,128]{2,1,0:T(8,128)(2,1)S(1)} %collective-permute-done.27.refs_4_), channel_id=1, source_target_pairs={{0,1},{1,0},{2,3},{3,2},{4,5},{5,4},{6,7},{7,6},{8,9},{9,8},{10,11... | collective-permute-start | bytes 835592 | tf_op jit(solution)/shard_map/ppermute | solution.py:673
  169.7 1.6 collective-permute-start.30
  169.7 2.0 %collective-permute-start.29 = (bf16[4,272,128]{2,1,0:T(8,128)(2,1)S(1)}, bf16[4,272,128]{2,1,0:T(8,128)(2,1)S(1)}, u32[]{:S(2)}, u32[]{:S(2)}) collective-permute-start(bf16[4,272,128]{2,1,0:T(8,128)(2,1)S(1)} %collective-permute-done.25.refs_2_), channel_id=1, source_target_pairs={{0,1},{1,0},{2,3},{3,2},{4,5},{5,4},{6,7},{7,6},{8,9},{9,8},{10,11... | collective-permute-start | bytes 835592 | tf_op jit(solution)/shard_map/ppermute | solution.py:673
  (1 other events, 0.6 us)
